TPU v7x, 256 devices: a whole 4x4x8 slice. The times are simulated.
256 devices in a mesh: rep: 32 (over z, x), fsdp: 8 (over y, core).
Axes of the slice: x: 4, y: 4, z: 8, core: 2. Of those that a mesh axis runs over, the one named last changes fastest.
Arguments:
- acts: bfloat16 [32768, 8192], P(('rep', 'fsdp')), may hold values from -6 to 6
- grads_out: bfloat16 [32768, 2048], P(('rep', 'fsdp')), may hold values from -0.1875 to 0.1875
- error: bfloat16 [32, 2, 8192, 1024], P('rep', None, 'fsdp'), may hold values from -6 to 6
- warm_q: float32 [2, 32, 1024], replicated, may hold values from -6 to 6
Outputs:
- new_error: bfloat16 [32, 2, 8192, 1024], P('rep', None, 'fsdp')
- p_factor: float32 [2, 32, 8192], P(None, None, 'fsdp')
- q_factor: float32 [2, 32, 1024], replicated
All inputs are finite; a program needn't handle non-finite values.
Results may differ from a plain program's by a relative error of at most 0.01.
Values may be sent and summed in bfloat16 or wider, within the bound.
No kernel may reach another device: no remote copies, remote signals or barrier semaphores. Data moves between devices by JAX's collectives and lax.ppermute only.
A program may use at most 128 MiB of HBM per device.

v0:
```python
import math

import jax
import jax.numpy as jnp
from jax import lax
from jax.sharding import PartitionSpec as P

D = 8192
POWER = 2


def contract(left, right):
    return lax.dot_general(
        left, right, (((0,), (0,)), ((), ())), preferred_element_type=jnp.float32
    )


def on_device(acts, grads_out, error, warm_q):
    local_err = error[0]
    shard_rows = local_err.shape[1]
    kv_width = local_err.shape[2]
    fsdp_index = lax.axis_index("fsdp")
    x_piece = lax.all_gather(acts, "fsdp", axis=0, tiled=True)
    d_piece = lax.all_gather(grads_out, "fsdp", axis=0, tiled=True)
    columns = lax.dynamic_slice_in_dim(x_piece, fsdp_index * shard_rows, shard_rows, 1)
    grad = contract(columns, d_piece)
    merged = grad.reshape(shard_rows, 2, kv_width).transpose(1, 0, 2) + local_err.astype(
        jnp.float32
    )
    replicas = lax.axis_size("rep")
    q_now = warm_q
    p_hat = None
    for turn_index in range(POWER):
        p_part = jnp.einsum("krc,kac->kra", q_now, merged, precision=lax.Precision.HIGHEST)
        p_raw = lax.psum(p_part, "rep") / replicas
        gram_part = jnp.einsum("kra,ksa->krs", p_raw, p_raw, precision=lax.Precision.HIGHEST)
        gram = lax.psum(gram_part, "fsdp")
        lower = jnp.linalg.cholesky(gram)
        p_hat = lax.linalg.triangular_solve(lower, p_raw, left_side=True, lower=True)
        q_part = jnp.einsum("kra,kac->krc", p_hat, merged, precision=lax.Precision.HIGHEST)
        q_total = lax.psum(q_part, ("rep", "fsdp"))
        q_now = q_total / replicas
    approx = jnp.einsum("kra,krc->kac", p_hat, q_now, precision=lax.Precision.HIGHEST)
    new_error = (merged - approx).astype(jnp.bfloat16)[None]
    return (new_error, p_hat * math.sqrt(D), q_now)


def solution(mesh):
    in_specs = (
        P(("rep", "fsdp"), None),
        P(("rep", "fsdp"), None),
        P("rep", None, "fsdp", None),
        P(),
    )
    out_specs = (P("rep", None, "fsdp", None), P(None, None, "fsdp"), P())
    return jax.shard_map(
        on_device, mesh=mesh, in_specs=in_specs, out_specs=out_specs, check_vma=False
    )
```

profile of v0, /device:TPU:1, one launch (start us, length us, event | category | flops | bytes accessed | tf_op | source)
XLA Modules:
  0.0 1059.3 jit_solution(7998951363102511038)
XLA Ops:
  8.7 40.1 %all-gather.5.cloned.1.call-done = bf16[1024,2048]{1,0:T(8,128)(2,1)} async-done(((bf16[128,2048]{1,0:T(8,128)(2,1)}), bf16[1024,2048]{1,0:T(8,128)(2,1)}) %all-gather.5.cloned.1.call-update) | async-done | bytes 4194320 | tf_op jit(solution)/shard_map/all_gather | solution.py:24
  48.8 89.4 %all-gather.3.cloned.1.call-done = bf16[1024,8192]{1,0:T(8,128)(2,1)} async-done(((bf16[128,8192]{1,0:T(8,128)(2,1)}), bf16[1024,8192]{1,0:T(8,128)(2,1)}) %all-gather.3.cloned.1.call-update) | async-done | bytes 16777232 | tf_op jit(solution)/shard_map/all_gather | solution.py:23
  138.2 7.3 fusion.2
  145.5 3.2 copy-done.1
  148.7 8.6 convolution_bitcast_fusion
  157.4 139.8 %all-reduce.5.cloned.1.call-done = f32[2,32,1024]{2,1,0:T(8,128)} async-done(((f32[2,32,1024]{2,1,0:T(8,128)}), f32[2,32,1024]{2,1,0:T(8,128)}) %all-reduce.5.cloned.1.call-update) | async-done | bytes 262160 | tf_op jit(solution)/shard_map/psum | solution.py:35
  297.3 1.4 fusion.12
  298.7 25.3 %psum.43 = f32[2,32,32]{1,2,0:T(8,128)S(1)} all-reduce(f32[2,32,32]{1,2,0:T(8,128)S(1)} %fusion.12), channel_id=1, replica_groups=mesh['rep'=32,'fsdp'=8] {'fsdp'}, use_global_device_ids=true, to_apply=%region_1.0 | all-reduce | flops 2048 | bytes 16384 | tf_op jit(solution)/shard_map/psum | solution.py:37
  324.1 5.9 custom-call.8
  330.2 4.9 custom-call.9
  335.1 1.4 fusion.10
  336.5 9.0 fusion.32
  345.6 246.4 %all-reduce.7.cloned.1.call-done = f32[2,32,1024]{2,1,0:T(8,128)} async-done(((f32[2,32,1024]{2,1,0:T(8,128)}), f32[2,32,1024]{2,1,0:T(8,128)}) %all-reduce.7.cloned.1.call-update) | async-done | bytes 262160 | tf_op jit(solution)/shard_map/psum | solution.py:41
  592.0 12.8 %fusion.4 = f32[2,32,1024]{2,1,0:T(8,128)} fusion(f32[2,32,1024]{2,1,0:T(8,128)} %all-reduce.7.cloned.1.call-done, f32[128,2,8,1024]{3,2,1,0:T(8,128)} %bitcast.62, bf16[1,2,1024,1024]{3,2,1,0:T(8,128)(2,1)} %param.9), kind=kOutput, calls=%fused_computation.7 | convolution fusion | flops 809566208 | bytes 13107200 | tf_op jit(solution)/shard_map/krc,kac->kra/dot_general | solution.py:34
  604.9 139.8 %all-reduce.9.cloned.1.call-done = f32[2,32,1024]{2,1,0:T(8,128)} async-done(((f32[2,32,1024]{2,1,0:T(8,128)}), f32[2,32,1024]{2,1,0:T(8,128)}) %all-reduce.9.cloned.1.call-update) | async-done | bytes 262160 | tf_op jit(solution)/shard_map/psum | solution.py:35
  744.7 1.4 fusion.8
  746.1 25.4 %psum.46 = f32[2,32,32]{1,2,0:T(8,128)S(1)} all-reduce(f32[2,32,32]{1,2,0:T(8,128)S(1)} %fusion.8), channel_id=1, replica_groups=mesh['rep'=32,'fsdp'=8] {'fsdp'}, use_global_device_ids=true, to_apply=%region_6.9 | all-reduce | flops 2048 | bytes 16384 | tf_op jit(solution)/shard_map/psum | solution.py:37
  771.5 5.9 custom-call.10
  777.6 4.9 custom-call.11
  782.6 2.1 broadcast_multiply_fusion
  784.7 9.0 fusion.29
  793.7 246.3 %all-reduce.11.cloned.1.call-done = f32[2,32,1024]{2,1,0:T(8,128)} async-done(((f32[2,32,1024]{2,1,0:T(8,128)}), f32[2,32,1024]{2,1,0:T(8,128)}) %all-reduce.11.cloned.1.call-update) | async-done | bytes 262160 | tf_op jit(solution)/shard_map/psum | solution.py:41
  1040.0 1.0 broadcast_multiply_fusion.1
  1041.0 11.5 %fusion.1 = bf16[1,2,1024,1024]{3,2,1,0:T(8,128)(2,1)} fusion(f32[2,32,1024]{2,1,0:T(8,128)S(1)} %get-tuple-element.6, f32[2,32,1024]{2,1,0:T(8,128)S(1)} %broadcast_multiply_fusion.1, bf16[1,2,1024,1024]{3,2,1,0:T(8,128)(2,1)} %param.9, f32[128,2,8,1024]{3,2,1,0:T(8,128)} %bitcast.64), kind=kOutput, calls=%fused_computation.3 | convolution fusion | flops 813694976 | bytes 17301504 | tf_op jit(solution)/shard_map/kra,krc->kac/dot_general | solution.py:43
  (31 shorter events, 2.3 us)
Async XLA Ops:
  7.2 141.5 %copy-start = (f32[2,32,1024]{2,1,0:T(8,128)S(1)}, f32[2,32,1024]{2,1,0:T(8,128)}, u32[]{:S(2)}) copy-start(f32[2,32,1024]{2,1,0:T(8,128)} %param.10) | copy-start | bytes 786436
  7.2 41.6 %all-gather.5.cloned.1.call-start = ((), (), s32[]{:S(2)}) async-start(), calls=%async_computation.1 | async-start | bytes 4718592 | tf_op jit(solution)/shard_map/all_gather | solution.py:24
  7.9 130.3 %all-gather.3.cloned.1.call-start = ((), (), s32[]{:S(2)}) async-start(), calls=%async_computation | async-start | bytes 18874368 | tf_op jit(solution)/shard_map/all_gather | solution.py:23
  8.7 288.6 %all-reduce.5.cloned.1.call-start = ((), (), s32[]{:S(2)}) async-start(), calls=%async_computation.2 | async-start | bytes 524288 | tf_op jit(solution)/shard_map/psum | solution.py:35
  138.2 10.5 copy-start.2
  145.5 3.2 copy-start.1
  157.4 434.7 %all-reduce.7.cloned.1.call-start = ((), (), s32[]{:S(2)}) async-start(), calls=%async_computation.3 | async-start | bytes 524288 | tf_op jit(solution)/shard_map/psum | solution.py:41
  345.5 399.1 %all-reduce.9.cloned.1.call-start = ((), (), s32[]{:S(2)}) async-start(), calls=%async_computation.4 | async-start | bytes 524288 | tf_op jit(solution)/shard_map/psum | solution.py:35
  604.9 435.1 %all-reduce.11.cloned.1.call-start = ((), (), s32[]{:S(2)}) async-start(), calls=%async_computation.5 | async-start | bytes 524288 | tf_op jit(solution)/shard_map/psum | solution.py:41
  1041.0 11.5 %copy-start.3 = (f32[2,32,1024]{2,1,0:T(8,128)}, f32[2,32,1024]{2,1,0:T(8,128)S(1)}, u32[]{:S(2)}) copy-start(f32[2,32,1024]{2,1,0:T(8,128)S(1)} %broadcast_multiply_fusion.1) | copy-start | bytes 786436
Sparse Core Ops, SparseCore 0:
  9.9 38.8 all-gather.4
  50.7 87.4 all-gather.2
  157.5 139.7 all-reduce.4
  345.7 246.3 all-reduce.6
  605.0 139.6 all-reduce.8
  793.8 246.1 all-reduce.10
where the time goes:
time: 1060 us
  waiting for transfers between devices  903 us (85%)
  matrix products  64.5 us (6%)
  blocking collectives  50.7 us (5%)
  other arithmetic  23 us (2%)
  between operations  14.2 us (1%)
    psum x2, waiting for transfers between devices, on_device(): q_total = lax.psum(q_part, ('rep', 'fsdp'))  493 us
    psum x2, waiting for transfers between devices, on_device(): p_raw = lax.psum(p_part, 'rep') / replicas  280 us
    all_gather x1, waiting for transfers between devices, on_device(): x_piece = lax.all_gather(acts, 'fsdp', axis=0, tiled=True)  89.4 us
    psum x2, blocking collectives, on_device(): gram = lax.psum(gram_part, 'fsdp')  50.7 us
    all_gather x1, waiting for transfers between devices, on_device(): d_piece = lax.all_gather(grads_out, 'fsdp', axis=0, tiled=True)  40.1 us
    dot_general x2, matrix products, on_device(): jnp.einsum('krc,kac->kra', q_now, merged, precision=lax.Precision.HIGHEST)  21.5 us
  transfers between devices with their start and end apart: 6, of which 6 were waited for; matrix products, arithmetic and copies ran while one was open for 0% of the time, Pallas kernels for 0%

commit v1 on v0

v1 whole, which is shorter than its diff:
```python
import math

import jax
import jax.numpy as jnp
from jax import lax
from jax.sharding import PartitionSpec as P

D = 8192
POWER = 2
BF16 = jnp.bfloat16
F32 = jnp.float32


def halves(x):
    high = lax.reduce_precision(x, 8, 7)
    return high.astype(BF16), (x - high).astype(BF16)


def stacked(x):
    return jnp.concatenate(halves(x), axis=-2)


def folded(x):
    rank = x.shape[-2] // 2
    return x[..., :rank, :] + x[..., rank:, :]


def product(spec, left, right):
    return jnp.einsum(spec, left, right, preferred_element_type=F32)


def fold_columns(x, parts):
    width = x.shape[1] // parts
    return jnp.concatenate([x[:, i * width : (i + 1) * width] for i in range(parts)], 0)


def unfold_columns(x, parts):
    height = x.shape[0] // parts
    return jnp.concatenate([x[i * height : (i + 1) * height] for i in range(parts)], 1)


def swap(x, axis):
    return lax.all_to_all(x, axis, 0, 0, tiled=True)


def total(x, axis):
    n = lax.axis_size(axis)
    mine = swap(x, axis).reshape(n, x.shape[0] // n, x.shape[1]).sum(0)
    everywhere = jnp.broadcast_to(mine[None], (n,) + mine.shape)
    return swap(everywhere.reshape(x.shape), axis)


def on_device(acts, grads_out, error, warm_q):
    err = error[0]
    rank = warm_q.shape[1]
    rows, width = err.shape[1], err.shape[2]
    tokens = acts.shape[0]
    fsdp = lax.axis_size("fsdp")
    replicas = lax.axis_size("rep")
    everyone = replicas * fsdp

    q_halves = stacked(warm_q)
    w = folded(product("krc,tkc->krt", q_halves, grads_out.reshape(tokens, 2, width)))
    w_high, w_low = halves(w.reshape(2 * rank, tokens))
    w_rows = jnp.concatenate(
        [unfold_columns(w_high, 4), unfold_columns(w_low, 4)], axis=1
    )
    extra = w_rows.shape[0]
    blocks = jnp.concatenate(
        [
            acts.reshape(tokens, fsdp, rows).transpose(1, 0, 2),
            jnp.broadcast_to(w_rows[None], (fsdp,) + w_rows.shape),
        ],
        axis=1,
    )
    got = lax.all_to_all(blocks, "fsdp", 0, 0, tiled=True)
    x = got[:, :tokens].reshape(fsdp * tokens, rows)
    w_got = got[:, tokens:].reshape(fsdp, extra, 2, 2, 2, extra * 8)
    w_all = w_got.transpose(3, 2, 4, 1, 0, 5).reshape(2, 2 * rank, fsdp * tokens)

    grads_out, _ = lax.optimization_barrier((grads_out, got))
    d = lax.all_gather(grads_out, "fsdp", axis=0, tiled=True)

    p_part = folded(product("krt,ta->kra", w_all, x)) + folded(
        product("krc,kac->kra", q_halves, err)
    )

    grad = lax.dot_general(x, d, (((0,), (0,)), ((), ())), preferred_element_type=F32)
    merged = grad.reshape(rows, 2, width).transpose(1, 0, 2) + err.astype(F32)
    m_high, m_low = halves(merged)

    def times_merged(spec, left):
        high, low = halves(left)
        both = jnp.concatenate([high, low], axis=-2)
        return folded(product(spec, both, m_high)) + product(spec, high, m_low)

    q_now = None
    for turn in range(POWER):
        if turn:
            p_part = times_merged("krc,kac->kra", q_now)
        p_fold = fold_columns(p_part.reshape(2 * rank, rows), 4)
        p_raw = unfold_columns(total(p_fold, "rep"), 4) / replicas
        p_raw = p_raw.reshape(2, rank, rows)
        gram_part = jnp.einsum(
            "kra,ksa->krs", p_raw, p_raw, precision=lax.Precision.HIGHEST
        )
        q_part = times_merged("kra,kac->krc", p_raw)
        sent = jnp.concatenate(
            [
                fold_columns(q_part.reshape(2 * rank, width), 4),
                fold_columns(gram_part.reshape(2 * rank, rank), 4),
            ],
            axis=1,
        )
        summed = total(sent, ("rep", "fsdp")) / replicas
        q_raw = unfold_columns(summed[:, : width // 4], 4).reshape(2, rank, width)
        gram = unfold_columns(summed[:, width // 4 :], 4).reshape(2, rank, rank)
        lower = jnp.linalg.cholesky(gram)
        q_now = lax.linalg.triangular_solve(lower, q_raw, left_side=True, lower=True)
    p_hat = lax.linalg.triangular_solve(lower, p_raw, left_side=True, lower=True)
    p_halves, q_last = stacked(p_hat), halves(q_now)
    both = jnp.concatenate([q_last[0], q_last[0]], axis=1)
    approx = product("kra,krc->kac", p_halves, both) + product(
        "kra,krc->kac", p_halves[:, :rank], q_last[1]
    )
    new_error = (merged - approx).astype(BF16)[None]
    return (new_error, p_hat * math.sqrt(D), q_now)


def solution(mesh):
    in_specs = (
        P(("rep", "fsdp"), None),
        P(("rep", "fsdp"), None),
        P("rep", None, "fsdp", None),
        P(),
    )
    out_specs = (P("rep", None, "fsdp", None), P(None, None, "fsdp"), P())
    return jax.shard_map(
        on_device, mesh=mesh, in_specs=in_specs, out_specs=out_specs, check_vma=False
    )
```

time: 1060 us -> 312 us (0.29)
  waiting for transfers between devices: 903 us -> 17.1 us
  blocking collectives: 50.7 us -> 177 us
  local copies, waits for them, and re-layouts: 3.39 us -> 24.8 us
  matrix products: 64.5 us -> 43.8 us
    psum x4 -> x0, waiting for transfers between devices: 772 us -> none  [the longest x2 493 us: on_device(): q_total = lax.psum(q_part, ('rep', 'fsdp'))]
    all_to_all x0 -> x8, blocking collectives: none -> 177 us  [the longest x7 141 us: swap(): return lax.all_to_all(x, axis, 0, 0, tiled=True)]
    all_gather x2 -> x1, waiting for transfers between devices: 130 us -> 0.02 us  [on_device(): d = lax.all_gather(grads_out, 'fsdp', axis=0, tiled=True)]
    psum x2 -> x0, blocking collectives: 50.7 us -> none  [on_device(): gram = lax.psum(gram_part, 'fsdp')]
    dot_general x6 -> x12, matrix products: 58.2 us -> 41.1 us  [the longest x11 33.4 us: product(): return jnp.einsum(spec, left, right, preferred_element_type=F32)]
    all_to_all x0 -> x1, waiting for transfers between devices: none -> 17.1 us  [swap(): return lax.all_to_all(x, axis, 0, 0, tiled=True)]
  transfers between devices with their start and end apart: 6 -> 2, of which waited for: 6 -> 1; matrix products, arithmetic and copies ran while one was open for 0% -> 2% of each run, Pallas kernels for 0% -> 0%
where the time goes in v1:
time: 312 us; the launch traced here: 311 us
  blocking collectives  177 us (57%)
  matrix products  43.8 us (14%)
  other arithmetic  27.4 us (9%)
  local copies, waits for them, and re-layouts  24.8 us (8%)
  waiting for transfers between devices  17.1 us (5%)
  between operations  14.6 us (5%)
  starting transfers between devices  6.24 us (2%)
    all_to_all x7, blocking collectives, swap(): return lax.all_to_all(x, axis, 0, 0, tiled=True)  141 us
    all_to_all x1, blocking collectives, on_device(): got = lax.all_to_all(blocks, 'fsdp', 0, 0, tiled=True)  35.7 us
    dot_general x11, matrix products, product(): return jnp.einsum(spec, left, right, preferred_element_type=F32)  33.4 us
    all_to_all x1, waiting for transfers between devices, swap(): return lax.all_to_all(x, axis, 0, 0, tiled=True)  17.1 us
    another operation x7, other arithmetic, on_device(): lower = jnp.linalg.cholesky(gram)  12 us
    unnamed x34, local copies, waits for them, and re-layouts  8.18 us
    dot_general x1, matrix products, on_device(): lax.dot_general(x, d, (((0,), (0,)), ((), ())), preferred_element_type=F32)  7.68 us
    dot_general x1, local copies, waits for them, and re-layouts, on_device(): lax.dot_general(x, d, (((0,), (0,)), ((), ())), preferred_element_type=F32)  6.55 us
  transfers between devices with their start and end apart: 2, of which 1 were waited for; matrix products, arithmetic and copies ran while one was open for 2% of the time, Pallas kernels for 0%

profile of v1, /device:TPU:1, one launch (start us, length us, event | category | flops | bytes accessed | tf_op | source)
XLA Modules:
  0.0 311.2 jit_solution(7625548422261965320)
XLA Ops:
  9.8 3.2 %copy.98 = bf16[128,8192]{0,1:T(8,128)(2,1)S(1)} copy(bf16[128,8192]{1,0:T(8,128)(2,1)} %param.7) | data formatting | bytes 4194304 | tf_op args[0]
  16.2 5.0 %copy.101 = bf16[8,144,1024]{2,1,0:T(8,128)(2,1)S(1)} copy(bf16[8,144,1024]{1,2,0:T(8,128)(2,1)} %pad_maximum_fusion) | data formatting | bytes 4718592 | tf_op jit(solution)/shard_map/concatenate | solution.py:69
  21.2 35.7 %all_to_all.65 = bf16[8,144,1024]{2,1,0:T(8,128)(2,1)} all-to-all(bf16[8,144,1024]{2,1,0:T(8,128)(2,1)S(1)} %copy.101), channel_id=1, replica_groups=mesh['rep'=32,'fsdp'=8] {'fsdp'}, dimensions={0} | all-to-all | bytes 4718592 | tf_op jit(solution)/shard_map/all_to_all | solution.py:76
  57.0 3.7 %fusion.2 = f32[2,64,1024]{2,1,0:T(8,128)S(1)} fusion(bf16[1,2,1024,1024]{3,2,1,0:T(8,128)(2,1)} %param.9, bf16[2,32,1024]{2,1,0:T(8,128)(2,1)S(1)} %get-tuple-element.57, bf16[2,32,1024]{2,1,0:T(8,128)(2,1)S(1)} %get-tuple-element.56), kind=kOutput, calls=%fused_computation.7 | convolution fusion | flops 268959744 | bytes 4980736 | tf_op jit(solution)/shard_map/krc,kac->kra/dot_general | solution.py:29
  63.3 20.8 %all_to_all.66 = f32[32,8,256]{2,1,0:T(8,128)S(1)} all-to-all(f32[32,8,256]{2,1,0:T(8,128)S(1)} %maximum_bitcast_fusion.2), channel_id=1, replica_groups=mesh['rep'=32,'fsdp'=8] {'rep'}, dimensions={0} | all-to-all | bytes 524288 | tf_op jit(solution)/shard_map/all_to_all | solution.py:43
  84.1 15.6 %all_to_all.67 = f32[32,8,256]{2,1,0:T(8,128)S(1)} all-to-all(f32[32,8,256]{2,1,0:T(8,128)S(1)} %broadcast_in_dim.11), channel_id=1, replica_groups=mesh['rep'=32,'fsdp'=8] {'rep'}, dimensions={0} | all-to-all | bytes 524288 | tf_op jit(solution)/shard_map/all_to_all | solution.py:43
  100.5 6.5 %copy.103 = bf16[2048,1024]{1,0:T(8,128)(2,1)} copy(bf16[2048,1024]{0,1:T(8,128)(2,1)} %bitcast.106) | data formatting | bytes 8388608 | tf_op jit(solution)/shard_map/dot_general | solution.py:88
  107.1 7.7 %bitcast_add_fusion = f32[2,1024,1024]{2,1,0:T(8,128)S(1)} fusion(bf16[1,2,1024,1024]{3,2,1,0:T(8,128)(2,1)} %param.9, bf16[1024,1024,1]{1,0,2:T(8,128)(2,1)S(1)} %bitcast.104, bf16[2,1024,1024]{2,1,0:T(8,128)(2,1)} %bitcast.107), kind=kOutput, calls=%fused_computation.3 | convolution fusion | flops 4299161600 | bytes 18874368 | tf_op jit(solution)/shard_map/dot_general | solution.py:88
  120.0 25.8 %all_to_all.68 = f32[256,1,264]{2,1,0:T(1,128)S(1)} all-to-all(f32[256,1,264]{2,1,0:T(1,128)S(1)} %copy.114), channel_id=1, replica_groups=mesh['rep'=32,'fsdp'=8] {'rep','fsdp'}, dimensions={0} | all-to-all | bytes 540672 | tf_op jit(solution)/shard_map/all_to_all | solution.py:43
  147.0 6.2 %all-to-all-start.4 = ((f32[256,1,264]{2,1,0:T(1,128)}), f32[256,1,264]{2,1,0:T(1,128)S(1)}, u32[]{:S(2)}, u32[]{:S(2)}) async-start(f32[256,1,264]{2,1,0:T(1,128)} %reshape.158), calls=%async_computation.4 | async-start | bytes 786432 | tf_op jit(solution)/shard_map/all_to_all | solution.py:43
  153.2 17.1 %all-to-all-done.4 = f32[256,1,264]{2,1,0:T(1,128)S(1)} async-done(((f32[256,1,264]{2,1,0:T(1,128)}), f32[256,1,264]{2,1,0:T(1,128)S(1)}, u32[]{:S(2)}, u32[]{:S(2)}) %all-to-all-start.4) | async-done | bytes 270368 | tf_op jit(solution)/shard_map/all_to_all | solution.py:43
  171.1 5.9 %custom-call.9 = f32[2,32,32]{2,1,0:T(8,128)S(1)} custom-call(f32[2,32,32]{2,1,0:T(8,128)S(1)} %fusion.42), custom_call_target="Cholesky" | custom-call | tf_op jit(solution)/shard_map/jit(cholesky)/cholesky | solution.py:118
  177.2 4.9 %custom-call.10 = f32[2,1,32,32]{2,3,1,0:T(8,128)S(1)} custom-call(f32[2,1,32,32]{3,2,1,0:T(8,128)S(1)} %select_bitcast_fusion.1), custom_call_target="InvertDiagBlocksLowerTriangular" | custom-call | tf_op jit(solution)/shard_map/triangular_solve/custom-call.0 | solution.py:119
  182.8 4.8 %fusion.18 = f32[2,64,1024]{2,1,0:T(8,128)S(1)} fusion(bf16[2,32,1024]{2,1,0:T(8,128)(2,1)S(1)} %get-tuple-element.40, bf16[2,32,1024]{2,1,0:T(8,128)(2,1)S(1)} %get-tuple-element.41, f32[2,1024,1024]{2,1,0:T(8,128)} %copy-done), kind=kOutput, calls=%fused_computation.52 | convolution fusion | flops 273154048 | bytes 9175040 | tf_op jit(solution)/shard_map/krc,kac->kra/dot_general | solution.py:29
  187.6 4.7 %convolution_add_fusion.1 = f32[2,32,1024]{2,1,0:T(8,128)S(1)} fusion(bf16[2,32,1024]{2,1,0:T(8,128)(2,1)S(1)} %get-tuple-element.41, f32[2,64,1024]{2,1,0:T(8,128)S(1)} %fusion.18, f32[2,1024,1024]{2,1,0:T(8,128)} %copy-done), kind=kOutput, calls=%fused_computation.10 | convolution fusion | flops 140640256 | bytes 9306112 | tf_op jit(solution)/shard_map/krc,kac->kra/dot_general | solution.py:29
  192.4 15.5 %all_to_all.69 = f32[32,8,256]{2,1,0:T(8,128)S(1)} all-to-all(f32[32,8,256]{2,1,0:T(8,128)S(1)} %maximum_bitcast_fusion.3), channel_id=1, replica_groups=mesh['rep'=32,'fsdp'=8] {'rep'}, dimensions={0} | all-to-all | bytes 524288 | tf_op jit(solution)/shard_map/all_to_all | solution.py:43
  207.9 15.0 %all_to_all.70 = f32[32,8,256]{2,1,0:T(8,128)S(1)} all-to-all(f32[32,8,256]{2,1,0:T(8,128)S(1)} %broadcast_in_dim.12), channel_id=1, replica_groups=mesh['rep'=32,'fsdp'=8] {'rep'}, dimensions={0} | all-to-all | bytes 524288 | tf_op jit(solution)/shard_map/all_to_all | solution.py:43
  223.6 4.3 %fusion.22 = f32[2,64,1024]{2,1,0:T(8,128)S(1)} fusion(bf16[2,32,1024]{2,1,0:T(8,128)(2,1)S(1)} %get-tuple-element.30, bf16[2,32,1024]{2,1,0:T(8,128)(2,1)S(1)} %get-tuple-element.31, f32[2,1024,1024]{2,1,0:T(8,128)} %copy-done), kind=kOutput, calls=%fused_computation.58 | convolution fusion | flops 273154048 | bytes 9175040 | tf_op jit(solution)/shard_map/kra,kac->krc/dot_general | solution.py:29
  227.9 4.3 %convolution_add_fusion = f32[2,32,1024]{2,1,0:T(8,128)S(1)} fusion(bf16[2,32,1024]{2,1,0:T(8,128)(2,1)S(1)} %get-tuple-element.31, f32[2,64,1024]{2,1,0:T(8,128)S(1)} %fusion.22, f32[2,1024,1024]{2,1,0:T(8,128)} %copy-done), kind=kOutput, calls=%fused_computation.9 | convolution fusion | flops 140640256 | bytes 9306112 | tf_op jit(solution)/shard_map/kra,kac->krc/dot_general | solution.py:29
  233.2 25.8 %all_to_all.71 = f32[256,1,264]{2,1,0:T(1,128)S(1)} all-to-all(f32[256,1,264]{2,1,0:T(1,128)S(1)} %copy.128), channel_id=1, replica_groups=mesh['rep'=32,'fsdp'=8] {'rep','fsdp'}, dimensions={0} | all-to-all | bytes 540672 | tf_op jit(solution)/shard_map/all_to_all | solution.py:43
  259.5 23.2 %all_to_all.72 = f32[256,1,264]{2,1,0:T(1,128)S(1)} all-to-all(f32[256,1,264]{2,1,0:T(1,128)S(1)} %reshape.164), channel_id=1, replica_groups=mesh['rep'=32,'fsdp'=8] {'rep','fsdp'}, dimensions={0} | all-to-all | bytes 540672 | tf_op jit(solution)/shard_map/all_to_all | solution.py:43
  283.5 5.9 %custom-call.11 = f32[2,32,32]{2,1,0:T(8,128)S(1)} custom-call(f32[2,32,32]{2,1,0:T(8,128)S(1)} %fusion.39), custom_call_target="Cholesky" | custom-call | tf_op jit(solution)/shard_map/jit(cholesky)/cholesky | solution.py:118
  289.6 4.9 %custom-call.12 = f32[2,1,32,32]{2,3,1,0:T(8,128)S(1)} custom-call(f32[2,1,32,32]{3,2,1,0:T(8,128)S(1)} %select_bitcast_fusion), custom_call_target="InvertDiagBlocksLowerTriangular" | custom-call | tf_op jit(solution)/shard_map/triangular_solve/custom-call.0 | solution.py:120
  297.6 6.7 %fusion.1 = bf16[1,2,1024,1024]{3,2,1,0:T(8,128)(2,1)} fusion(f32[2,1024,1024]{2,1,0:T(8,128)} %copy-done, f32[2,1024,1024]{2,1,0:T(8,128)S(1)} %fusion.26, bf16[2,32,1024]{2,1,0:T(8,128)(2,1)S(1)} %get-tuple-element.25, f32[2,32,1024]{2,1,0:T(8,128)S(1)} %get-tuple-element.69), kind=kOutput, calls=%fused_computation.5 | convolution fusion | flops 140705792 | bytes 21364736 | tf_op jit(solution)/shard_map/kra,krc->kac/dot_general | solution.py:29
  (112 shorter events, 23.5 us)
Async XLA Ops:
  7.2 93.3 %all-gather.2.cloned.1.call-start = ((), (), s32[]{:S(2)}) async-start(), calls=%async_computation.9 | async-start | bytes 4718592 | tf_op jit(solution)/shard_map/all_gather | solution.py:82
  57.0 3.8 %slice-start = ((bf16[8,144,1024]{2,1,0:T(8,128)(2,1)}), bf16[8,16,1024]{2,1,0:T(8,128)(2,1)S(1)}, s32[]{:S(2)}) async-start(bf16[8,144,1024]{2,1,0:T(8,128)(2,1)} %all_to_all.65), calls=%async_computation.10 | async-start | bytes 524288 | tf_op jit(solution)/shard_map/slice | solution.py:78
  57.0 4.2 %copy-start.1 = (bf16[8,144,1024]{2,1,0:T(8,128)(2,1)S(1)}, bf16[8,144,1024]{2,1,0:T(8,128)(2,1)}, u32[]{:S(2)}) copy-start(bf16[8,144,1024]{2,1,0:T(8,128)(2,1)} %all_to_all.65) | copy-start | bytes 7077892
  61.4 1.3 copy-start.2
  100.5 6.6 %copy-start.3 = (bf16[8,128,1024]{2,1,0:T(8,128)(2,1)S(1)}, bf16[8,128,1024]{2,1,0:T(8,128)(2,1)}, u32[]{:S(2)}) copy-start(bf16[8,128,1024]{2,1,0:T(8,128)(2,1)} %copy-done.2) | copy-start | bytes 6291460
  114.8 3.2 %copy-start = (f32[2,1024,1024]{2,1,0:T(8,128)}, f32[2,1024,1024]{2,1,0:T(8,128)S(1)}, u32[]{:S(2)}) copy-start(f32[2,1024,1024]{2,1,0:T(8,128)S(1)} %bitcast_add_fusion) | copy-start | bytes 25165828
  147.0 23.3 %all-to-all-start.4 = ((f32[256,1,264]{2,1,0:T(1,128)}), f32[256,1,264]{2,1,0:T(1,128)S(1)}, u32[]{:S(2)}, u32[]{:S(2)}) async-start(f32[256,1,264]{2,1,0:T(1,128)} %reshape.158), calls=%async_computation.4 | async-start | bytes 786432 | tf_op jit(solution)/shard_map/all_to_all | solution.py:43
  296.3 1.3 copy-start.4
Sparse Core Ops, SparseCore 0:
  57.1 35.8 all-gather.1

commit v2 on v0

v2 whole, which is shorter than its diff:
```python
import functools
import math

import jax
import jax.numpy as jnp
from jax import lax
from jax.experimental import pallas as pl
from jax.experimental.pallas import tpu as pltpu
from jax.sharding import Mesh, PartitionSpec as P

D = 8192
BF16 = jnp.bfloat16
F32 = jnp.float32
REP = ("z", "x")
FSDP = ("y", "core")
VMEM = pl.BlockSpec(memory_space=pltpu.VMEM)
HBM = pl.BlockSpec(memory_space=pltpu.HBM)
MEGA = 1024 * 1024
CUTS = 4


def halves(x):
    high = x.astype(BF16)
    return high, (x - high.astype(F32)).astype(BF16)


def dot(left, right, dims):
    return lax.dot_general(left, right, (dims, ((), ())), preferred_element_type=F32)


def exact(left, right, dims):
    return lax.dot_general(
        left,
        right,
        (dims, ((), ())),
        precision=lax.Precision.HIGHEST,
        preferred_element_type=F32,
    )


def narrow(x, rank):
    return x[:rank] + x[rank : 2 * rank]


def stack(ref, value, row, lane):
    height, width = value.shape[0], value.shape[1] // CUTS
    step = ref.shape[0] // CUTS
    for i in range(CUTS):
        ref[i * step + row : i * step + row + height, lane : lane + width] = value[
            :, i * width : (i + 1) * width
        ]


def unstack(value):
    height = value.shape[0] // CUTS
    return jnp.concatenate(
        [value[i * height : (i + 1) * height] for i in range(CUTS)], axis=1
    )


def prepare(acts, grads_out, warm_q, out, sems):
    parts, height, rows = out.shape
    tokens = acts.shape[0]
    piece = height - tokens
    moves = [
        pltpu.make_async_copy(
            acts.at[:, pl.ds(i * rows, rows)], out.at[i, pl.ds(0, tokens)], sems.at[i]
        )
        for i in range(parts)
    ]
    for move in moves:
        move.start()
    rank, width = warm_q.shape[1:]
    per = rank // piece
    for k in range(2):
        left = jnp.concatenate(halves(warm_q[k]), axis=0)
        grads = grads_out[:, k * width : (k + 1) * width]
        w = narrow(dot(left, grads, ((1,), (1,))), rank)
        for half, value in enumerate(halves(w)):
            for b in range(per):
                at = (half * 2 * per + k * per + b) * tokens
                for i in range(parts):
                    out[i, tokens:height, at : at + tokens] = value[
                        b * piece : (b + 1) * piece
                    ]
    for move in moves:
        move.wait()


def error_part(error, warm_q, out):
    rank = warm_q.shape[1]
    for k in range(2):
        left = jnp.concatenate(halves(warm_q[k]), axis=0)
        out[k * rank : (k + 1) * rank] = narrow(
            dot(left, error[0, k], ((1,), (1,))), rank
        )


def first_left(got, p_error, out, w):
    parts, height, _ = got.shape
    tokens = w.shape[1] // parts
    piece = height - tokens
    total = w.shape[0] // piece
    for s in range(parts):
        for b in range(total):
            w[b * piece : (b + 1) * piece, s * tokens : (s + 1) * tokens] = got[
                s, tokens:height, b * tokens : (b + 1) * tokens
            ]
    p = p_error[...]
    both = jnp.zeros((w.shape[0], got.shape[2]), F32)
    for s in range(0, parts, 2):
        x = jnp.concatenate([got[s, :tokens], got[s + 1, :tokens]], axis=0)
        both += dot(w[:, s * tokens : (s + 2) * tokens], x, ((1,), (0,)))
    stack(out, p + narrow(both, p.shape[0]), 0, 0)


def merge(got, d, error, high, low):
    parts = got.shape[0]
    tokens = d.shape[0] // parts
    x = jnp.concatenate([got[s, :tokens] for s in range(parts)], axis=0)
    for k in range(2):
        width = error.shape[3]
        grad = dot(x, d[:, k * width : (k + 1) * width], ((0,), (0,)))
        high[k], low[k] = halves(grad + error[0, k].astype(F32))


def fetch(high, low, high_here, low_here, sems):
    moves = []
    for k in range(2):
        pair = [
            pltpu.make_async_copy(high.at[k], high_here.at[k], sems.at[2 * k]),
            pltpu.make_async_copy(low.at[k], low_here.at[k], sems.at[2 * k + 1]),
        ]
        for move in pair:
            move.start()
        moves.append(pair)
    return moves


def multiply(left, high, low, dims):
    left_high, left_low = halves(left)
    both = jnp.concatenate([left_high, left_low], axis=0)
    return narrow(dot(both, high, dims), left.shape[0]) + dot(left_high, low, dims)


def right_factor(replicas, rank, p_sum, high, low, p_out, out, high_here, low_here, sems):
    moves = fetch(high, low, high_here, low_here, sems)
    p = unstack(p_sum[...]) / replicas
    p_out[...] = p
    mine = [p[k * rank : (k + 1) * rank] for k in range(2)]
    grams = [exact(x, x, ((1,), (1,))) for x in mine]
    for k in range(2):
        for move in moves[k]:
            move.wait()
        q = multiply(mine[k], high_here[k], low_here[k], ((1,), (0,)))
        stack(out.at[k], q, 0, 0)
        stack(out.at[k], grams[k], 0, q.shape[1] // CUTS)


def inverse_factors(grams):
    n = grams[0].shape[0]
    row = lax.broadcasted_iota(jnp.int32, (n, n), 0)
    column = lax.broadcasted_iota(jnp.int32, (n, n), 1)
    same = row == column
    one = same.astype(F32)
    below = lax.broadcasted_iota(jnp.int32, (n, 2 * n), 0)
    ts = [jnp.concatenate([gram, one], axis=1) for gram in grams]
    for j in range(n - 1):
        for i, t in enumerate(ts):
            pivot_row = t[j : j + 1] / t[j : j + 1, j : j + 1]
            factor = jnp.where(below > j, jnp.broadcast_to(t[:, j : j + 1], t.shape), 0.0)
            ts[i] = t - factor * pivot_row
    inverses = []
    for t in ts:
        pivots = jnp.sum(jnp.where(same, t[:, :n], 0.0), axis=1, keepdims=True)
        inverses.append(t[:, n:] / jnp.sqrt(pivots))
    return inverses


def solved(summed, replicas, rank, width):
    mine = [unstack(summed[k, :, : width // CUTS]) / replicas for k in range(2)]
    last = (width + rank) // CUTS
    inverses = inverse_factors(
        [unstack(summed[k, :, width // CUTS : last]) / replicas for k in range(2)]
    )
    return inverses, [exact(x, y, ((1,), (0,))) for x, y in zip(inverses, mine)]


def left_factor(replicas, rank, q_sum, high, low, out, high_here, low_here, sems):
    moves = fetch(high, low, high_here, low_here, sems)
    _, q = solved(q_sum[...], replicas, rank, high.shape[2])
    for k in range(2):
        for move in moves[k]:
            move.wait()
        p = multiply(q[k], high_here[k], low_here[k], ((1,), (1,)))
        stack(out, p, k * rank, 0)


def finish(
    replicas, rank, q_sum, p_raw, high, low, new_error, p_factor, q_factor, *scratch
):
    high_here, low_here, sems, out, out_sems = scratch
    rows, width = high.shape[1:]
    moves = fetch(high, low, high_here, low_here, sems)
    inverses, q = solved(q_sum[...], replicas, rank, width)
    cut = rows // CUTS
    sends = []
    for k in range(2):
        q_factor[k] = q[k]
        p_hat = exact(inverses[k], p_raw[k * rank : (k + 1) * rank], ((1,), (0,)))
        p_factor[k] = p_hat * math.sqrt(D)
        p_high, p_low = halves(p_hat)
        q_high, q_low = halves(q[k])
        ps = jnp.concatenate([p_high, p_low, p_high, p_low], axis=0)
        qs = jnp.concatenate([q_high, q_high, q_low, q_low], axis=0)
        for move in moves[k]:
            move.wait()
        for i in range(CUTS):
            at = slice(i * cut, (i + 1) * cut)
            approx = dot(ps[:, at], qs, ((0,), (0,)))
            merged = high_here[k, at].astype(F32) + low_here[k, at].astype(F32)
            out[k, at] = (merged - approx).astype(BF16)
            send = pltpu.make_async_copy(
                out.at[k, at], new_error.at[0, k, at], out_sems.at[CUTS * k + i]
            )
            send.start()
            sends.append(send)
    for send in sends:
        send.wait()


def call(kernel, outs, *args, space=52, cost=None, **kw):
    params = pltpu.CompilerParams(vmem_limit_bytes=space * MEGA)
    if cost is not None:
        kw["cost_estimate"] = pl.CostEstimate(
            flops=cost[0], bytes_accessed=cost[1], transcendentals=0
        )
    kw.setdefault("in_specs", [VMEM] * len(args))
    kw.setdefault("out_specs", [VMEM] * len(outs))
    return pl.pallas_call(kernel, out_shape=outs, compiler_params=params, **kw)(*args)


def array(shape, dtype):
    return jax.ShapeDtypeStruct(shape, dtype)


def swap(x, axis):
    return lax.all_to_all(x, axis, 0, 0, tiled=True)


def shared(x, axis):
    n = lax.axis_size(axis)
    return swap(x, axis).reshape(n, x.shape[0] // n, x.shape[1]).sum(0)


def copied(x, axis):
    everywhere = jnp.broadcast_to(x[None], (lax.axis_size(axis),) + x.shape)
    return swap(everywhere.reshape(-1, x.shape[1]), axis)


def total(x, axis):
    return copied(shared(x, axis), axis)


def total_everywhere(x):
    core = lax.axis_index("core")
    flip = [(0, 1), (1, 0)]
    given = lax.dynamic_index_in_dim(x, 1 - core, 0, keepdims=False)
    kept = lax.dynamic_index_in_dim(x, core, 0, keepdims=False)
    mine = shared(kept + lax.ppermute(given, "core", flip), ("x", "y"))
    tall = mine.shape[0]
    mine = copied(mine, "z").reshape(-1, tall, mine.shape[1]).sum(0)
    mine = copied(mine, ("x", "y"))
    other = lax.ppermute(mine, "core", flip)
    first = core == 0
    return jnp.stack([jnp.where(first, mine, other), jnp.where(first, other, mine)])


def on_device(acts, grads_out, error, warm_q):
    _, rank, width = warm_q.shape
    rows = error.shape[2]
    tokens = acts.shape[0]
    fsdp = lax.axis_size(FSDP)
    replicas = lax.axis_size(REP)
    piece = 4 * rank * tokens // rows
    pairs = 2 * rank

    (blocks,) = call(
        prepare,
        [array((fsdp, tokens + piece, rows), BF16)],
        acts,
        grads_out,
        warm_q,
        in_specs=[HBM, VMEM, VMEM],
        scratch_shapes=[pltpu.SemaphoreType.DMA((fsdp,))],
    )
    got = swap(blocks, FSDP)
    (p_error,) = call(error_part, [array((pairs, rows), F32)], error, warm_q, cost=(10**10, 10**8))
    grads_out, _, got = lax.optimization_barrier((grads_out, p_error, got))
    d = lax.all_gather(grads_out, FSDP, axis=0, tiled=True)

    folded = array((CUTS * pairs, rows // CUTS), F32)
    (p_part,) = call(
        first_left,
        [folded],
        got,
        p_error,
        space=16,
        scratch_shapes=[pltpu.VMEM((2 * pairs, fsdp * tokens), BF16)],
    )
    p_sum = total(p_part, REP)
    cut = rows // 4
    high, low = call(
        merge,
        [array((2, rows, width), BF16)] * 2,
        got,
        d,
        error,
        grid=(4,),
        in_specs=[
            pl.BlockSpec((fsdp, tokens + piece, cut), lambda i: (0, 0, i)),
            pl.BlockSpec((fsdp * tokens, 2 * width), lambda i: (0, 0)),
            pl.BlockSpec((1, 2, cut, width), lambda i: (0, 0, i, 0)),
        ],
        out_specs=[pl.BlockSpec((2, cut, width), lambda i: (0, i, 0))] * 2,
    )

    local = [
        pltpu.VMEM((2, rows, width), BF16),
        pltpu.VMEM((2, rows, width), BF16),
        pltpu.SemaphoreType.DMA((4,)),
    ]

    def right(p_sum):
        p_raw, sent = call(
            functools.partial(right_factor, replicas, rank),
            [
                array((pairs, rows), F32),
                array((2, CUTS * rank, (width + rank) // CUTS), F32),
            ],
            p_sum,
            high,
            low,
            in_specs=[VMEM, HBM, HBM],
            scratch_shapes=local,
        )
        return p_raw, total_everywhere(sent)

    _, q_sum = right(p_sum)
    (p_part,) = call(
        functools.partial(left_factor, replicas, rank),
        [folded],
        q_sum,
        high,
        low,
        in_specs=[VMEM, HBM, HBM],
        scratch_shapes=local,
    )
    p_raw, q_sum = right(total(p_part, REP))
    return call(
        functools.partial(finish, replicas, rank),
        [
            array((1, 2, rows, width), BF16),
            array((2, rank, rows), F32),
            array((2, rank, width), F32),
        ],
        q_sum,
        p_raw,
        high,
        low,
        in_specs=[VMEM, VMEM, HBM, HBM],
        out_specs=[HBM, VMEM, VMEM],
        scratch_shapes=local
        + [pltpu.VMEM((2, rows, width), BF16), pltpu.SemaphoreType.DMA((2 * CUTS,))],
    )


def solution(mesh):
    devices = mesh.devices.reshape(8, 4, 4, 2)
    torus = Mesh(devices, REP + FSDP)
    in_specs = (
        P(REP + FSDP, None),
        P(REP + FSDP, None),
        P(REP, None, FSDP, None),
        P(),
    )
    out_specs = (P(REP, None, FSDP, None), P(None, None, FSDP), P())
    return jax.shard_map(
        on_device, mesh=torus, in_specs=in_specs, out_specs=out_specs, check_vma=False
    )
```

time: 1060 us -> 241 us (0.23)
  waiting for transfers between devices: 903 us -> 38.4 us
  blocking collectives: 50.7 us -> 118 us
  matrix products: 64.5 us -> 0 us
  Pallas kernels: 0 us -> 42.9 us
  starting transfers between devices: 0.24 us -> 24.2 us
  other arithmetic: 23 us -> 0.34 us
    psum x4 -> x0, waiting for transfers between devices: 772 us -> none  [the longest x2 493 us: on_device(): q_total = lax.psum(q_part, ('rep', 'fsdp'))]
    all_gather x2 -> x1, waiting for transfers between devices: 130 us -> 8.43 us  [on_device(): d = lax.all_gather(grads_out, FSDP, axis=0, tiled=True)]
    all_to_all x0 -> x9, blocking collectives: none -> 118 us  [swap(): return lax.all_to_all(x, axis, 0, 0, tiled=True)]
    dot_general x8 -> x0, matrix products: 61 us -> none  [the longest x2 21.5 us: on_device(): jnp.einsum('krc,kac->kra', q_now, merged, precision=lax.Precision.HIGHEST)]
    psum x2 -> x0, blocking collectives: 50.7 us -> none  [on_device(): gram = lax.psum(gram_part, 'fsdp')]
    pallas_call x0 -> x8, Pallas kernels: none -> 42.9 us  [call(): pl.pallas_call(kernel, out_shape=outs, compiler_params=params, **kw)(*args)]
    all_to_all x0 -> x2, waiting for transfers between devices: none -> 25.6 us  [swap(): return lax.all_to_all(x, axis, 0, 0, tiled=True)]
    another operation x12 -> x4, other arithmetic: 22 us -> 0.15 us  [total_everywhere(): jnp.stack([jnp.where(first, mine, other), jnp.where(first, other, mine)])]
  transfers between devices with their start and end apart: 6 -> 7, of which waited for: 6 -> 6; matrix products, arithmetic and copies ran while one was open for 0% -> 0% of each run, Pallas kernels for 0% -> 6%
where the time goes in v2:
time: 241 us
  blocking collectives  118 us (49%)
  Pallas kernels  42.9 us (18%)
  waiting for transfers between devices  38.4 us (16%)
  starting transfers between devices  24.2 us (10%)
  between operations  14.2 us (6%)
  local copies, waits for them, and re-layouts  2.83 us (1%)
    all_to_all x9, blocking collectives, swap(): return lax.all_to_all(x, axis, 0, 0, tiled=True)  118 us
    pallas_call x8, Pallas kernels, call(): pl.pallas_call(kernel, out_shape=outs, compiler_params=params, **kw)(*args)  42.9 us
    all_to_all x2, waiting for transfers between devices, swap(): return lax.all_to_all(x, axis, 0, 0, tiled=True)  25.6 us
    all_to_all x2, starting transfers between devices, swap(): return lax.all_to_all(x, axis, 0, 0, tiled=True)  11.6 us
    all_gather x1, waiting for transfers between devices, on_device(): d = lax.all_gather(grads_out, FSDP, axis=0, tiled=True)  8.43 us
    ppermute x2, starting transfers between devices, total_everywhere(): other = lax.ppermute(mine, 'core', flip)  8.36 us
  transfers between devices with their start and end apart: 7, of which 6 were waited for; matrix products, arithmetic and copies ran while one was open for 0% of the time, Pallas kernels for 6%

profile of v2, /device:TPU:1, one launch (start us, length us, event | category | flops | bytes accessed | tf_op | source)
XLA Modules:
  0.0 240.5 jit_solution(17906918099698089568)
XLA Ops:
  9.2 3.1 %shard_map.68 = bf16[8,144,1024]{2,1,0:T(8,128)(2,1)} custom-call(bf16[128,8192]{1,0:T(8,128)(2,1)} %acts.1, bf16[128,2048]{1,0:T(8,128)(2,1)S(1)} %copy-done.1, f32[2,32,1024]{2,1,0:T(8,128)S(1)} %copy-done.2), custom_call_target="tpu_custom_call" | custom-call | tf_op jit(solution)/shard_map/pallas_call | solution.py:240
  12.2 6.8 %all-to-all-start = ((bf16[8,144,1024]{2,1,0:T(8,128)(2,1)}), bf16[8,144,1024]{2,1,0:T(8,128)(2,1)S(1)}, u32[]{:S(2)}, u32[]{:S(2)}) async-start(bf16[8,144,1024]{2,1,0:T(8,128)(2,1)} %shard_map.68), calls=%async_computation | async-start | bytes 4718592 | tf_op jit(solution)/shard_map/all_to_all | solution.py:248
  19.0 3.6 %shard_map.67.p_error = f32[64,1024]{1,0:T(8,128)S(1)} custom-call(bf16[1,2,1024,1024]{3,2,1,0:T(8,128)(2,1)} %error.3, f32[2,32,1024]{2,1,0:T(8,128)S(1)} %copy-done.3), custom_call_target="tpu_custom_call" | custom-call | flops 10000000000 | bytes 100000000 | tf_op jit(solution)/shard_map/pallas_call | solution.py:240
  22.6 25.6 %all-to-all-done.got = bf16[8,144,1024]{2,1,0:T(8,128)(2,1)S(1)} async-done(((bf16[8,144,1024]{2,1,0:T(8,128)(2,1)}), bf16[8,144,1024]{2,1,0:T(8,128)(2,1)S(1)}, u32[]{:S(2)}, u32[]{:S(2)}) %all-to-all-start) | async-done | bytes 2359328 | tf_op jit(solution)/shard_map/all_to_all | solution.py:248
  48.7 21.1 %all_to_all.87 = f32[32,8,256]{2,1,0:T(8,128)S(1)} all-to-all(f32[32,8,256]{2,1,0:T(8,128)S(1)} %bitcast.37), channel_id=1, replica_groups=mesh['z'=8,'x'=4,'y'=4,'core'=2] {'z','x'}, dimensions={0} | all-to-all | bytes 524288 | tf_op jit(solution)/shard_map/all_to_all | solution.py:248
  70.5 4.8 %all-to-all-start.2 = ((f32[32,8,256]{2,1,0:T(8,128)}), f32[32,8,256]{2,1,0:T(8,128)S(1)}, u32[]{:S(2)}, u32[]{:S(2)}) async-start(f32[32,8,256]{2,1,0:T(8,128)} %broadcast_in_dim.12), calls=%async_computation.2 | async-start | bytes 524288 | tf_op jit(solution)/shard_map/all_to_all | solution.py:248
  75.4 8.4 %all-gather.2.cloned.1.call-done.d = bf16[1024,2048]{1,0:T(8,128)(2,1)} async-done(((bf16[128,2048]{1,0:T(8,128)(2,1)}), bf16[1024,2048]{1,0:T(8,128)(2,1)}) %all-gather.2.cloned.1.call-update) | async-done | bytes 4194320 | tf_op jit(solution)/shard_map/all_gather | solution.py:300
  83.8 10.6 %shard_map.70 = (bf16[2,1024,1024]{2,1,0:T(8,128)(2,1)}, bf16[2,1024,1024]{2,1,0:T(8,128)(2,1)}) custom-call(bf16[8,144,1024]{2,1,0:T(8,128)(2,1)} %copy-done, bf16[1024,2048]{1,0:T(8,128)(2,1)} %all-gather.2.cloned.1.call-done.d, bf16[1,2,1024,1024]{3,2,1,0:T(8,128)(2,1)} %error.3), custom_call_target="tpu_custom_call" | custom-call | tf_op jit(solution)/shard_map/pallas_call | solution.py:240
  94.4 4.5 %shard_map.71 = (f32[64,1024]{1,0:T(8,128)}, f32[2,128,264]{2,1,0:T(8,128)S(1)}) custom-call(f32[256,256]{1,0:T(8,128)S(1)} %bitcast.34, bf16[2,1024,1024]{2,1,0:T(8,128)(2,1)} %get-tuple-element.12.high, bf16[2,1024,1024]{2,1,0:T(8,128)(2,1)} %get-tuple-element.13.low), custom_call_target="tpu_custom_call" | custom-call | tf_op jit(solution)/shard_map/pallas_call | solution.py:240
  99.2 1.2 collective-permute-done
  100.4 12.0 %all_to_all.88 = f32[16,8,264]{2,1,0:T(8,128)S(1)} all-to-all(f32[16,8,264]{2,1,0:T(8,128)S(1)} %fusion.1), channel_id=1, replica_groups=mesh['z'=8,'x'=4,'y'=4,'core'=2] {'x','y'}, dimensions={0} | all-to-all | bytes 270336 | tf_op jit(solution)/shard_map/all_to_all | solution.py:248
  112.5 14.2 %all_to_all.89 = f32[8,8,264]{2,1,0:T(8,128)S(1)} all-to-all(f32[8,8,264]{2,1,0:T(8,128)S(1)} %broadcast_in_dim.13), channel_id=1, replica_groups=mesh['z'=8,'x'=4,'y'=4,'core'=2] {'z'}, dimensions={0} | all-to-all | bytes 135168 | tf_op jit(solution)/shard_map/all_to_all | solution.py:248
  126.7 10.3 %all_to_all.90 = f32[16,8,264]{2,1,0:T(8,128)S(1)} all-to-all(f32[16,8,264]{2,1,0:T(8,128)S(1)} %broadcast_in_dim.14), channel_id=1, replica_groups=mesh['z'=8,'x'=4,'y'=4,'core'=2] {'x','y'}, dimensions={0} | all-to-all | bytes 270336 | tf_op jit(solution)/shard_map/all_to_all | solution.py:248
  137.0 4.3 %collective-permute-start.1 = (f32[128,264]{1,0:T(8,128)S(1)}, f32[128,264]{1,0:T(8,128)S(1)}, u32[]{:S(2)}, u32[]{:S(2)}) collective-permute-start(f32[128,264]{1,0:T(8,128)S(1)} %bitcast.38), channel_id=1, source_target_pairs={{0,1},{1,0},{2,3},{3,2},{4,5},{5,4},{6,7},{7,6},{8,9},{9,8},{10,11... | collective-permute-start | bytes 405512 | tf_op jit(solution)/shard_map/ppermute | solution.py:274
  142.4 8.0 %shard_map.72 = f32[256,256]{1,0:T(8,128)S(1)} custom-call(f32[2,128,264]{2,1,0:T(8,128)S(1)} %pad_maximum_fusion.q_sum, bf16[2,1024,1024]{2,1,0:T(8,128)(2,1)} %get-tuple-element.12.high, bf16[2,1024,1024]{2,1,0:T(8,128)(2,1)} %get-tuple-element.13.low), custom_call_target="tpu_custom_call" | custom-call | tf_op jit(solution)/shard_map/pallas_call | solution.py:240
  150.5 14.8 %all_to_all.91 = f32[32,8,256]{2,1,0:T(8,128)S(1)} all-to-all(f32[32,8,256]{2,1,0:T(8,128)S(1)} %bitcast.36), channel_id=1, replica_groups=mesh['z'=8,'x'=4,'y'=4,'core'=2] {'z','x'}, dimensions={0} | all-to-all | bytes 524288 | tf_op jit(solution)/shard_map/all_to_all | solution.py:248
  165.4 14.4 %all_to_all.92 = f32[32,8,256]{2,1,0:T(8,128)S(1)} all-to-all(f32[32,8,256]{2,1,0:T(8,128)S(1)} %broadcast_in_dim.15), channel_id=1, replica_groups=mesh['z'=8,'x'=4,'y'=4,'core'=2] {'z','x'}, dimensions={0} | all-to-all | bytes 524288 | tf_op jit(solution)/shard_map/all_to_all | solution.py:248
  179.8 4.5 %shard_map.73 = (f32[64,1024]{1,0:T(8,128)S(1)}, f32[2,128,264]{2,1,0:T(8,128)S(1)}) custom-call(f32[256,256]{1,0:T(8,128)S(1)} %bitcast.35, bf16[2,1024,1024]{2,1,0:T(8,128)(2,1)} %get-tuple-element.12.high, bf16[2,1024,1024]{2,1,0:T(8,128)(2,1)} %get-tuple-element.13.low), custom_call_target="tpu_custom_call" | custom-call | tf_op jit(solution)/shard_map/pallas_call | solution.py:240
  184.3 3.8 %collective-permute-start.2 = (f32[128,264]{1,0:T(8,128)S(1)}, f32[128,264]{1,0:T(8,128)S(1)}, u32[]{:S(2)}, u32[]{:S(2)}) collective-permute-start(f32[128,264]{1,0:T(8,128)S(1)} %dynamic-slice_bitcast_fusion), channel_id=1, source_target_pairs={{0,1},{1,0},{2,3},{3,2},{4,5},{5,4},{6,7},{7,6},{8,9},{9,8},{10,11... | collective-permute-start | bytes 405512 | tf_op jit(solution)/shard_map/ppermute | solution.py:270
  189.3 10.5 %all_to_all.93 = f32[16,8,264]{2,1,0:T(8,128)S(1)} all-to-all(f32[16,8,264]{2,1,0:T(8,128)S(1)} %fusion), channel_id=1, replica_groups=mesh['z'=8,'x'=4,'y'=4,'core'=2] {'x','y'}, dimensions={0} | all-to-all | bytes 270336 | tf_op jit(solution)/shard_map/all_to_all | solution.py:248
  199.8 10.0 %all_to_all.94 = f32[8,8,264]{2,1,0:T(8,128)S(1)} all-to-all(f32[8,8,264]{2,1,0:T(8,128)S(1)} %broadcast_in_dim.16), channel_id=1, replica_groups=mesh['z'=8,'x'=4,'y'=4,'core'=2] {'z'}, dimensions={0} | all-to-all | bytes 135168 | tf_op jit(solution)/shard_map/all_to_all | solution.py:248
  209.8 10.2 %all_to_all.95 = f32[16,8,264]{2,1,0:T(8,128)S(1)} all-to-all(f32[16,8,264]{2,1,0:T(8,128)S(1)} %broadcast_in_dim.17), channel_id=1, replica_groups=mesh['z'=8,'x'=4,'y'=4,'core'=2] {'x','y'}, dimensions={0} | all-to-all | bytes 270336 | tf_op jit(solution)/shard_map/all_to_all | solution.py:248
  220.1 4.1 %collective-permute-start.3 = (f32[128,264]{1,0:T(8,128)S(1)}, f32[128,264]{1,0:T(8,128)S(1)}, u32[]{:S(2)}, u32[]{:S(2)}) collective-permute-start(f32[128,264]{1,0:T(8,128)S(1)} %bitcast.39), channel_id=1, source_target_pairs={{0,1},{1,0},{2,3},{3,2},{4,5},{5,4},{6,7},{7,6},{8,9},{9,8},{10,11... | collective-permute-start | bytes 405512 | tf_op jit(solution)/shard_map/ppermute | solution.py:274
  225.4 8.3 %shard_map.74 = (bf16[1,2,1024,1024]{3,2,1,0:T(8,128)(2,1)}, f32[2,32,1024]{2,1,0:T(8,128)}, f32[2,32,1024]{2,1,0:T(8,128)}) custom-call(f32[2,128,264]{2,1,0:T(8,128)S(1)} %pad_maximum_fusion.1.q_sum, f32[64,1024]{1,0:T(8,128)S(1)} %get-tuple-element.16.p_raw, bf16[2,1024,1024]{2,1,0:T(8,128)(2,1)} %get-tuple-element.12.high, ...), custom_call_target="tpu_custom_call" | custom-call | tf_op jit(solution)/shard_map/pallas_call | solution.py:240
  (36 shorter events, 7.2 us)
Async XLA Ops:
  7.2 1.0 copy-start.1
  8.2 0.9 copy-start.2
  9.2 9.9 %copy-start.3 = (f32[2,32,1024]{2,1,0:T(8,128)S(1)}, f32[2,32,1024]{2,1,0:T(8,128)}, u32[]{:S(2)}) copy-start(f32[2,32,1024]{2,1,0:T(8,128)} %warm_q.3) | copy-start | bytes 786436
  12.2 35.9 %all-to-all-start = ((bf16[8,144,1024]{2,1,0:T(8,128)(2,1)}), bf16[8,144,1024]{2,1,0:T(8,128)(2,1)S(1)}, u32[]{:S(2)}, u32[]{:S(2)}) async-start(bf16[8,144,1024]{2,1,0:T(8,128)(2,1)} %shard_map.68), calls=%async_computation | async-start | bytes 4718592 | tf_op jit(solution)/shard_map/all_to_all | solution.py:248
  19.0 64.8 %all-gather.2.cloned.1.call-start = ((), (), s32[]{:S(2)}) async-start(), calls=%async_computation.11 | async-start | bytes 4718592 | tf_op jit(solution)/shard_map/all_gather | solution.py:300
  48.2 35.6 %copy-start = (bf16[8,144,1024]{2,1,0:T(8,128)(2,1)}, bf16[8,144,1024]{2,1,0:T(8,128)(2,1)S(1)}, u32[]{:S(2)}) copy-start(bf16[8,144,1024]{2,1,0:T(8,128)(2,1)S(1)} %all-to-all-done.got) | copy-start | bytes 7077892
  70.5 23.9 %all-to-all-start.2 = ((f32[32,8,256]{2,1,0:T(8,128)}), f32[32,8,256]{2,1,0:T(8,128)S(1)}, u32[]{:S(2)}, u32[]{:S(2)}) async-start(f32[32,8,256]{2,1,0:T(8,128)} %broadcast_in_dim.12), calls=%async_computation.2 | async-start | bytes 524288 | tf_op jit(solution)/shard_map/all_to_all | solution.py:248
  98.9 1.5 collective-permute-start
  137.0 5.3 %collective-permute-start.1 = (f32[128,264]{1,0:T(8,128)S(1)}, f32[128,264]{1,0:T(8,128)S(1)}, u32[]{:S(2)}, u32[]{:S(2)}) collective-permute-start(f32[128,264]{1,0:T(8,128)S(1)} %bitcast.38), channel_id=1, source_target_pairs={{0,1},{1,0},{2,3},{3,2},{4,5},{5,4},{6,7},{7,6},{8,9},{9,8},{10,11... | collective-permute-start | bytes 405512 | tf_op jit(solution)/shard_map/ppermute | solution.py:274
  184.3 4.9 %collective-permute-start.2 = (f32[128,264]{1,0:T(8,128)S(1)}, f32[128,264]{1,0:T(8,128)S(1)}, u32[]{:S(2)}, u32[]{:S(2)}) collective-permute-start(f32[128,264]{1,0:T(8,128)S(1)} %dynamic-slice_bitcast_fusion), channel_id=1, source_target_pairs={{0,1},{1,0},{2,3},{3,2},{4,5},{5,4},{6,7},{7,6},{8,9},{9,8},{10,11... | collective-permute-start | bytes 405512 | tf_op jit(solution)/shard_map/ppermute | solution.py:270
  220.1 5.2 %collective-permute-start.3 = (f32[128,264]{1,0:T(8,128)S(1)}, f32[128,264]{1,0:T(8,128)S(1)}, u32[]{:S(2)}, u32[]{:S(2)}) collective-permute-start(f32[128,264]{1,0:T(8,128)S(1)} %bitcast.39), channel_id=1, source_target_pairs={{0,1},{1,0},{2,3},{3,2},{4,5},{5,4},{6,7},{7,6},{8,9},{9,8},{10,11... | collective-permute-start | bytes 405512 | tf_op jit(solution)/shard_map/ppermute | solution.py:274
Sparse Core Ops, SparseCore 0:
  48.3 35.4 all-gather.1

commit v3 on v2

--- a/solution.py
+++ b/solution.py
@@ -17,6 +17,7 @@
 HBM = pl.BlockSpec(memory_space=pltpu.HBM)
 MEGA = 1024 * 1024
 CUTS = 4
+PIECES = 2
 
 
 def halves(x):
@@ -58,18 +59,27 @@
     )
 
 
-def prepare(acts, grads_out, warm_q, out, sems):
+def prepare(acts, grads_out, warm_q, out, here, w_rows, in_sems, out_sems):
     parts, height, rows = out.shape
     tokens = acts.shape[0]
     piece = height - tokens
     moves = [
         pltpu.make_async_copy(
-            acts.at[:, pl.ds(i * rows, rows)], out.at[i, pl.ds(0, tokens)], sems.at[i]
+            acts.at[:, pl.ds(i * rows, rows)], here.at[i], in_sems.at[i]
         )
         for i in range(parts)
     ]
     for move in moves:
         move.start()
+    sends = []
+    for i in range(parts):
+        moves[i].wait()
+        sends.append(
+            pltpu.make_async_copy(
+                here.at[i], out.at[i, pl.ds(0, tokens)], out_sems.at[i]
+            )
+        )
+        sends[-1].start()
     rank, width = warm_q.shape[1:]
     per = rank // piece
     for k in range(2):
@@ -79,12 +89,16 @@
         for half, value in enumerate(halves(w)):
             for b in range(per):
                 at = (half * 2 * per + k * per + b) * tokens
-                for i in range(parts):
-                    out[i, tokens:height, at : at + tokens] = value[
-                        b * piece : (b + 1) * piece
-                    ]
-    for move in moves:
-        move.wait()
+                w_rows[:, at : at + tokens] = value[b * piece : (b + 1) * piece]
+    for i in range(parts):
+        sends.append(
+            pltpu.make_async_copy(
+                w_rows, out.at[i, pl.ds(tokens, piece)], out_sems.at[parts + i]
+            )
+        )
+        sends[-1].start()
+    for send in sends:
+        send.wait()
 
 
 def error_part(error, warm_q, out):
@@ -114,26 +128,75 @@
     stack(out, p + narrow(both, p.shape[0]), 0, 0)
 
 
-def merge(got, d, error, high, low):
-    parts = got.shape[0]
-    tokens = d.shape[0] // parts
-    x = jnp.concatenate([got[s, :tokens] for s in range(parts)], axis=0)
-    for k in range(2):
-        width = error.shape[3]
-        grad = dot(x, d[:, k * width : (k + 1) * width], ((0,), (0,)))
-        high[k], low[k] = halves(grad + error[0, k].astype(F32))
+def merge(place, got, error, *refs):
+    blocks, (high, low), scratch = refs[:8], refs[8:10], refs[10:]
+    x, d, e, high_here, low_here, in_sems, error_sems, out_sems = scratch
+    y, core = place[0], place[1]
+    tokens = d.shape[0] // 8
+    rows, width = e.shape[1:]
+    cut = rows // CUTS
+    moves = []
+    for i in range(8):
+        step, other = divmod(i, 2)
+        source = 2 * lax.rem(y + 4 - step, 4) + (1 - core if other else core)
+        at = pl.ds(i * tokens, tokens)
+        moves += [
+            pltpu.make_async_copy(blocks[i], d.at[at], in_sems.at[i]),
+            pltpu.make_async_copy(
+                got.at[source, pl.ds(0, tokens)], x.at[at], in_sems.at[8 + i]
+            ),
+        ]
+    errors = [
+        pltpu.make_async_copy(
+            error.at[0, :, pl.ds(i * cut, cut)],
+            e.at[:, pl.ds(i * cut, cut)],
+            error_sems.at[i],
+        )
+        for i in range(CUTS)
+    ]
+    for move in moves + errors:
+        move.start()
+    for move in moves:
+        move.wait()
+    sends = []
+    for i in range(CUTS):
+        at = slice(i * cut, (i + 1) * cut)
+        errors[i].wait()
+        for k in range(2):
+            grad = dot(x[:, at], d[:, k * width : (k + 1) * width], ((0,), (0,)))
+            merged_high, merged_low = halves(grad + e[k, at].astype(F32))
+            high_here[k, at] = merged_high
+            low_here[k, at] = merged_low
+            for here, there, n in ((high_here, high, 0), (low_here, low, 1)):
+                send = pltpu.make_async_copy(
+                    here.at[k, at], there.at[k, at], out_sems.at[4 * i + 2 * k + n]
+                )
+                send.start()
+                sends.append(send)
+    for send in sends:
+        send.wait()
 
 
 def fetch(high, low, high_here, low_here, sems):
+    cut = high.shape[1] // PIECES
     moves = []
     for k in range(2):
-        pair = [
-            pltpu.make_async_copy(high.at[k], high_here.at[k], sems.at[2 * k]),
-            pltpu.make_async_copy(low.at[k], low_here.at[k], sems.at[2 * k + 1]),
-        ]
+        for i in range(PIECES):
+            at = pl.ds(i * cut, cut)
+            n = 2 * (PIECES * k + i)
+            moves.append(
+                [
+                    pltpu.make_async_copy(
+                        high.at[k, at], high_here.at[k, at], sems.at[n]
+                    ),
+                    pltpu.make_async_copy(
+                        low.at[k, at], low_here.at[k, at], sems.at[n + 1]
+                    ),
+                ]
+            )
+    for pair in moves:
         for move in pair:
             move.start()
-        moves.append(pair)
     return moves
 
 
@@ -150,8 +213,9 @@
     mine = [p[k * rank : (k + 1) * rank] for k in range(2)]
     grams = [exact(x, x, ((1,), (1,))) for x in mine]
     for k in range(2):
-        for move in moves[k]:
-            move.wait()
+        for pair in moves[PIECES * k : PIECES * (k + 1)]:
+            for move in pair:
+                move.wait()
         q = multiply(mine[k], high_here[k], low_here[k], ((1,), (0,)))
         stack(out.at[k], q, 0, 0)
         stack(out.at[k], grams[k], 0, q.shape[1] // CUTS)
@@ -168,8 +232,8 @@
     for j in range(n - 1):
         for i, t in enumerate(ts):
             pivot_row = t[j : j + 1] / t[j : j + 1, j : j + 1]
-            factor = jnp.where(below > j, jnp.broadcast_to(t[:, j : j + 1], t.shape), 0.0)
-            ts[i] = t - factor * pivot_row
+            factor = jnp.broadcast_to(t[:, j : j + 1], t.shape)
+            ts[i] = t - jnp.where(below > j, factor, 0.0) * pivot_row
     inverses = []
     for t in ts:
         pivots = jnp.sum(jnp.where(same, t[:, :n], 0.0), axis=1, keepdims=True)
@@ -177,23 +241,27 @@
     return inverses
 
 
-def solved(summed, replicas, rank, width):
-    mine = [unstack(summed[k, :, : width // CUTS]) / replicas for k in range(2)]
+def summed_factors(summed, replicas, rank, width):
     last = (width + rank) // CUTS
-    inverses = inverse_factors(
-        [unstack(summed[k, :, width // CUTS : last]) / replicas for k in range(2)]
-    )
-    return inverses, [exact(x, y, ((1,), (0,))) for x, y in zip(inverses, mine)]
+    q = [unstack(summed[k, :, : width // CUTS]) / replicas for k in range(2)]
+    grams = [unstack(summed[k, :, width // CUTS : last]) / replicas for k in range(2)]
+    return q, inverse_factors(grams)
 
 
 def left_factor(replicas, rank, q_sum, high, low, out, high_here, low_here, sems):
     moves = fetch(high, low, high_here, low_here, sems)
-    _, q = solved(q_sum[...], replicas, rank, high.shape[2])
-    for k in range(2):
-        for move in moves[k]:
+    q, inverses = summed_factors(q_sum[...], replicas, rank, high.shape[2])
+    cut = high.shape[1] // PIECES
+    p = []
+    for n in range(2 * PIECES):
+        for move in moves[n]:
             move.wait()
-        p = multiply(q[k], high_here[k], low_here[k], ((1,), (1,)))
-        stack(out, p, k * rank, 0)
+        k, i = divmod(n, PIECES)
+        at = slice(i * cut, (i + 1) * cut)
+        p.append(multiply(q[k], high_here[k, at], low_here[k, at], ((1,), (1,))))
+    for k in range(2):
+        mine = jnp.concatenate(p[PIECES * k : PIECES * (k + 1)], axis=1)
+        stack(out, exact(inverses[k], mine, ((1,), (0,))), k * rank, 0)
 
 
 def finish(
@@ -202,20 +270,22 @@
     high_here, low_here, sems, out, out_sems = scratch
     rows, width = high.shape[1:]
     moves = fetch(high, low, high_here, low_here, sems)
-    inverses, q = solved(q_sum[...], replicas, rank, width)
+    q_raw, inverses = summed_factors(q_sum[...], replicas, rank, width)
     cut = rows // CUTS
     sends = []
     for k in range(2):
-        q_factor[k] = q[k]
+        q = exact(inverses[k], q_raw[k], ((1,), (0,)))
+        q_factor[k] = q
         p_hat = exact(inverses[k], p_raw[k * rank : (k + 1) * rank], ((1,), (0,)))
         p_factor[k] = p_hat * math.sqrt(D)
         p_high, p_low = halves(p_hat)
-        q_high, q_low = halves(q[k])
+        q_high, q_low = halves(q)
         ps = jnp.concatenate([p_high, p_low, p_high, p_low], axis=0)
         qs = jnp.concatenate([q_high, q_high, q_low, q_low], axis=0)
-        for move in moves[k]:
-            move.wait()
         for i in range(CUTS):
+            if i % (CUTS // PIECES) == 0:
+                for move in moves[PIECES * k + i * PIECES // CUTS]:
+                    move.wait()
             at = slice(i * cut, (i + 1) * cut)
             approx = dot(ps[:, at], qs, ((0,), (0,)))
             merged = high_here[k, at].astype(F32) + low_here[k, at].astype(F32)
@@ -291,14 +361,24 @@
         acts,
         grads_out,
         warm_q,
+        space=60,
         in_specs=[HBM, VMEM, VMEM],
-        scratch_shapes=[pltpu.SemaphoreType.DMA((fsdp,))],
+        out_specs=[HBM],
+        scratch_shapes=[
+            pltpu.VMEM((fsdp, tokens, rows), BF16),
+            pltpu.VMEM((piece, rows), BF16),
+            pltpu.SemaphoreType.DMA((fsdp,)),
+            pltpu.SemaphoreType.DMA((2 * fsdp,)),
+        ],
     )
     got = swap(blocks, FSDP)
     (p_error,) = call(error_part, [array((pairs, rows), F32)], error, warm_q, cost=(10**10, 10**8))
     grads_out, _, got = lax.optimization_barrier((grads_out, p_error, got))
-    d = lax.all_gather(grads_out, FSDP, axis=0, tiled=True)
-
+    place = jnp.stack([lax.axis_index("y"), lax.axis_index("core")]).astype(jnp.int32)
+    here = [grads_out] + [
+        lax.ppermute(grads_out, "y", [(i, (i + step) % 4) for i in range(4)])
+        for step in (1, 3, 2)
+    ]
     folded = array((CUTS * pairs, rows // CUTS), F32)
     (p_part,) = call(
         first_left,
@@ -308,36 +388,44 @@
         space=16,
         scratch_shapes=[pltpu.VMEM((2 * pairs, fsdp * tokens), BF16)],
     )
-    p_sum = total(p_part, REP)
-    cut = rows // 4
+    p_mine = shared(p_part, REP)
+    *here, _ = lax.optimization_barrier((*here, p_mine))
+    here = [here[0], here[1], here[3], here[2]]
+    there = [lax.ppermute(block, "core", [(0, 1), (1, 0)]) for block in here]
+    d = [block for pair in zip(here, there) for block in pair]
+    p_sum = copied(p_mine, REP)
+    halved = array((2, rows, width), BF16)
+    folded_q = array((2, CUTS * rank, (width + rank) // CUTS), F32)
     high, low = call(
         merge,
-        [array((2, rows, width), BF16)] * 2,
+        [halved, halved],
+        place,
         got,
-        d,
         error,
-        grid=(4,),
-        in_specs=[
-            pl.BlockSpec((fsdp, tokens + piece, cut), lambda i: (0, 0, i)),
-            pl.BlockSpec((fsdp * tokens, 2 * width), lambda i: (0, 0)),
-            pl.BlockSpec((1, 2, cut, width), lambda i: (0, 0, i, 0)),
+        *d,
+        in_specs=[pl.BlockSpec(memory_space=pltpu.SMEM)] + [HBM] * 10,
+        out_specs=[HBM, HBM],
+        scratch_shapes=[
+            pltpu.VMEM((fsdp * tokens, rows), BF16),
+            pltpu.VMEM((fsdp * tokens, 2 * width), BF16),
+            pltpu.VMEM((2, rows, width), BF16),
+            pltpu.VMEM((2, rows, width), BF16),
+            pltpu.VMEM((2, rows, width), BF16),
+            pltpu.SemaphoreType.DMA((16,)),
+            pltpu.SemaphoreType.DMA((CUTS,)),
+            pltpu.SemaphoreType.DMA((4 * CUTS,)),
         ],
-        out_specs=[pl.BlockSpec((2, cut, width), lambda i: (0, i, 0))] * 2,
-    )
-
+    )
     local = [
         pltpu.VMEM((2, rows, width), BF16),
         pltpu.VMEM((2, rows, width), BF16),
-        pltpu.SemaphoreType.DMA((4,)),
+        pltpu.SemaphoreType.DMA((4 * PIECES,)),
     ]
 
     def right(p_sum):
         p_raw, sent = call(
             functools.partial(right_factor, replicas, rank),
-            [
-                array((pairs, rows), F32),
-                array((2, CUTS * rank, (width + rank) // CUTS), F32),
-            ],
+            [array((pairs, rows), F32), folded_q],
             p_sum,
             high,
             low,

time: 241 us -> 228 us (0.946)
  between operations: 14.2 us -> 1.02 us
  starting transfers between devices: 24.2 us -> 37.2 us
  waiting for transfers between devices: 38.4 us -> 31 us
    all_gather x1 -> x0, waiting for transfers between devices: 8.43 us -> none  [on_device(): d = lax.all_gather(grads_out, FSDP, axis=0, tiled=True)]
    ppermute x0 -> x7, starting transfers between devices: none -> 6.2 us  [the longest x4 3.52 us: on_device(): there = [lax.ppermute(block, 'core', [(0, 1), (1, 0)]) for block in here]]
    all_to_all x2, starting transfers between devices: 11.6 us -> 16.6 us  [swap(): return lax.all_to_all(x, axis, 0, 0, tiled=True)]
  transfers between devices with their start and end apart: 7 -> 13, of which waited for: 6 -> 7; matrix products, arithmetic and copies ran while one was open for 0% -> 0% of each run, Pallas kernels for 6% -> 7%
where the time goes in v3:
time: 228 us
  blocking collectives  116 us (51%)
  Pallas kernels  41.1 us (18%)
  starting transfers between devices  37.2 us (16%)
  waiting for transfers between devices  31 us (14%)
    all_to_all x9, blocking collectives, swap(): return lax.all_to_all(x, axis, 0, 0, tiled=True)  116 us
    pallas_call x8, Pallas kernels, call(): pl.pallas_call(kernel, out_shape=outs, compiler_params=params, **kw)(*args)  41.1 us
    all_to_all x2, waiting for transfers between devices, swap(): return lax.all_to_all(x, axis, 0, 0, tiled=True)  25.8 us
    all_to_all x2, starting transfers between devices, swap(): return lax.all_to_all(x, axis, 0, 0, tiled=True)  16.6 us
    ppermute x2, starting transfers between devices, total_everywhere(): other = lax.ppermute(mine, 'core', flip)  8.4 us
    ppermute x2, starting transfers between devices, total_everywhere(): mine = shared(kept + lax.ppermute(given, 'core', flip), ('x', 'y'))  6.02 us
  transfers between devices with their start and end apart: 13, of which 7 were waited for; matrix products, arithmetic and copies ran while one was open for 0% of the time, Pallas kernels for 7%

profile of v3, /device:TPU:1, one launch (start us, length us, event | category | flops | bytes accessed | tf_op | source)
XLA Modules:
  0.0 227.8 jit_solution(8213771220399381730)
XLA Ops:
  0.6 3.9 %shard_map.68 = bf16[8,144,1024]{2,1,0:T(8,128)(2,1)} custom-call(bf16[128,8192]{1,0:T(8,128)(2,1)} %acts.1, bf16[128,2048]{1,0:T(8,128)(2,1)} %refs_0_, f32[2,32,1024]{2,1,0:T(8,128)} %warm_q.3), custom_call_target="tpu_custom_call" | custom-call | tf_op jit(solution)/shard_map/pallas_call | solution.py:310
  4.5 6.8 %all-to-all-start = ((bf16[8,144,1024]{2,1,0:T(8,128)(2,1)}), bf16[8,144,1024]{2,1,0:T(8,128)(2,1)S(1)}, u32[]{:S(2)}, u32[]{:S(2)}) async-start(bf16[8,144,1024]{2,1,0:T(8,128)(2,1)} %shard_map.68), calls=%async_computation | async-start | bytes 4718592 | tf_op jit(solution)/shard_map/all_to_all | solution.py:318
  11.3 3.6 %shard_map.67.p_error = f32[64,1024]{1,0:T(8,128)S(1)} custom-call(bf16[1,2,1024,1024]{3,2,1,0:T(8,128)(2,1)} %error.3, f32[2,32,1024]{2,1,0:T(8,128)S(1)} %copy-done.2), custom_call_target="tpu_custom_call" | custom-call | flops 10000000000 | bytes 100000000 | tf_op jit(solution)/shard_map/pallas_call | solution.py:310
  14.9 25.5 %all-to-all-done.got = bf16[8,144,1024]{2,1,0:T(8,128)(2,1)S(1)} async-done(((bf16[8,144,1024]{2,1,0:T(8,128)(2,1)}), bf16[8,144,1024]{2,1,0:T(8,128)(2,1)S(1)}, u32[]{:S(2)}, u32[]{:S(2)}) %all-to-all-start) | async-done | bytes 2359328 | tf_op jit(solution)/shard_map/all_to_all | solution.py:318
  40.7 2.4 %collective-permute-start.1 = (bf16[128,2048]{1,0:T(8,128)(2,1)S(1)}, bf16[128,2048]{1,0:T(8,128)(2,1)}, u32[]{:S(2)}, u32[]{:S(2)}) collective-permute-start(bf16[128,2048]{1,0:T(8,128)(2,1)S(1)} %copy-done.1), channel_id=1, source_target_pairs={{0,6},{2,0},{4,2},{6,4},{1,7},{3,1},{5,3},{7,5},{8,14},{10,8},{12,... | collective-permute-start | bytes 1572872 | tf_op jit(solution)/shard_map/ppermute | solution.py:379
  43.6 20.4 %all_to_all.87 = f32[32,8,256]{2,1,0:T(8,128)S(1)} all-to-all(f32[32,8,256]{2,1,0:T(8,128)S(1)} %bitcast.39), channel_id=1, replica_groups=mesh['z'=8,'x'=4,'y'=4,'core'=2] {'z','x'}, dimensions={0} | all-to-all | bytes 524288 | tf_op jit(solution)/shard_map/all_to_all | solution.py:318
  65.0 2.9 %collective-permute-start.3 = (bf16[128,2048]{1,0:T(8,128)(2,1)S(1)}, bf16[128,2048]{1,0:T(8,128)(2,1)}, u32[]{:S(2)}, u32[]{:S(2)}) collective-permute-start(bf16[128,2048]{1,0:T(8,128)(2,1)S(1)} %copy-done.1), channel_id=1, source_target_pairs={{0,1},{1,0},{2,3},{3,2},{4,5},{5,4},{6,7},{7,6},{8,9},{9,8},{10,11... | collective-permute-start | bytes 1572872 | tf_op jit(solution)/shard_map/ppermute | solution.py:394
  69.2 9.8 %all-to-all-start.2 = ((f32[32,8,256]{2,1,0:T(8,128)}), f32[32,8,256]{2,1,0:T(8,128)S(1)}, u32[]{:S(2)}, u32[]{:S(2)}) async-start(f32[32,8,256]{2,1,0:T(8,128)} %broadcast_in_dim.12), calls=%async_computation.2 | async-start | bytes 524288 | tf_op jit(solution)/shard_map/all_to_all | solution.py:318
  79.2 11.0 %shard_map.70 = (bf16[2,1024,1024]{2,1,0:T(8,128)(2,1)}, bf16[2,1024,1024]{2,1,0:T(8,128)(2,1)}) custom-call(s32[2]{0:T(128)S(1)} %pad_add_fusion.place, bf16[8,144,1024]{2,1,0:T(8,128)(2,1)} %copy-done, bf16[1,2,1024,1024]{3,2,1,0:T(8,128)(2,1)} %error.3, bf16[128,2048]{1,0:T(8,128)(2,1)S(1)} %copy-done.1, ...), custom_call_target="tpu_custom_call" | custom-call | tf_op jit(solution)/shard_map/pallas_call | solution.py:310
  90.5 4.5 %shard_map.71 = (f32[64,1024]{1,0:T(8,128)}, f32[2,128,264]{2,1,0:T(8,128)S(1)}) custom-call(f32[256,256]{1,0:T(8,128)S(1)} %bitcast.36, bf16[2,1024,1024]{2,1,0:T(8,128)(2,1)} %get-tuple-element.20.high, bf16[2,1024,1024]{2,1,0:T(8,128)(2,1)} %get-tuple-element.21.low), custom_call_target="tpu_custom_call" | custom-call | tf_op jit(solution)/shard_map/pallas_call | solution.py:310
  98.4 11.9 %all_to_all.88 = f32[16,8,264]{2,1,0:T(8,128)S(1)} all-to-all(f32[16,8,264]{2,1,0:T(8,128)S(1)} %fusion.1), channel_id=1, replica_groups=mesh['z'=8,'x'=4,'y'=4,'core'=2] {'x','y'}, dimensions={0} | all-to-all | bytes 270336 | tf_op jit(solution)/shard_map/all_to_all | solution.py:318
  110.3 13.6 %all_to_all.89 = f32[8,8,264]{2,1,0:T(8,128)S(1)} all-to-all(f32[8,8,264]{2,1,0:T(8,128)S(1)} %broadcast_in_dim.13), channel_id=1, replica_groups=mesh['z'=8,'x'=4,'y'=4,'core'=2] {'z'}, dimensions={0} | all-to-all | bytes 135168 | tf_op jit(solution)/shard_map/all_to_all | solution.py:318
  124.0 10.3 %all_to_all.90 = f32[16,8,264]{2,1,0:T(8,128)S(1)} all-to-all(f32[16,8,264]{2,1,0:T(8,128)S(1)} %broadcast_in_dim.14), channel_id=1, replica_groups=mesh['z'=8,'x'=4,'y'=4,'core'=2] {'x','y'}, dimensions={0} | all-to-all | bytes 270336 | tf_op jit(solution)/shard_map/all_to_all | solution.py:318
  134.3 4.3 %collective-permute-start.8 = (f32[128,264]{1,0:T(8,128)S(1)}, f32[128,264]{1,0:T(8,128)S(1)}, u32[]{:S(2)}, u32[]{:S(2)}) collective-permute-start(f32[128,264]{1,0:T(8,128)S(1)} %bitcast.40), channel_id=1, source_target_pairs={{0,1},{1,0},{2,3},{3,2},{4,5},{5,4},{6,7},{7,6},{8,9},{9,8},{10,11... | collective-permute-start | bytes 405512 | tf_op jit(solution)/shard_map/ppermute | solution.py:344
  139.7 6.0 %shard_map.72 = f32[256,256]{1,0:T(8,128)S(1)} custom-call(f32[2,128,264]{2,1,0:T(8,128)S(1)} %pad_maximum_fusion.q_sum, bf16[2,1024,1024]{2,1,0:T(8,128)(2,1)} %get-tuple-element.20.high, bf16[2,1024,1024]{2,1,0:T(8,128)(2,1)} %get-tuple-element.21.low), custom_call_target="tpu_custom_call" | custom-call | tf_op jit(solution)/shard_map/pallas_call | solution.py:310
  145.7 14.8 %all_to_all.91 = f32[32,8,256]{2,1,0:T(8,128)S(1)} all-to-all(f32[32,8,256]{2,1,0:T(8,128)S(1)} %bitcast.38), channel_id=1, replica_groups=mesh['z'=8,'x'=4,'y'=4,'core'=2] {'z','x'}, dimensions={0} | all-to-all | bytes 524288 | tf_op jit(solution)/shard_map/all_to_all | solution.py:318
  160.6 14.5 %all_to_all.92 = f32[32,8,256]{2,1,0:T(8,128)S(1)} all-to-all(f32[32,8,256]{2,1,0:T(8,128)S(1)} %broadcast_in_dim.15), channel_id=1, replica_groups=mesh['z'=8,'x'=4,'y'=4,'core'=2] {'z','x'}, dimensions={0} | all-to-all | bytes 524288 | tf_op jit(solution)/shard_map/all_to_all | solution.py:318
  175.1 4.4 %shard_map.73 = (f32[64,1024]{1,0:T(8,128)S(1)}, f32[2,128,264]{2,1,0:T(8,128)S(1)}) custom-call(f32[256,256]{1,0:T(8,128)S(1)} %bitcast.37, bf16[2,1024,1024]{2,1,0:T(8,128)(2,1)} %get-tuple-element.20.high, bf16[2,1024,1024]{2,1,0:T(8,128)(2,1)} %get-tuple-element.21.low), custom_call_target="tpu_custom_call" | custom-call | tf_op jit(solution)/shard_map/pallas_call | solution.py:310
  179.5 3.7 %collective-permute-start.9 = (f32[128,264]{1,0:T(8,128)S(1)}, f32[128,264]{1,0:T(8,128)S(1)}, u32[]{:S(2)}, u32[]{:S(2)}) collective-permute-start(f32[128,264]{1,0:T(8,128)S(1)} %dynamic-slice_bitcast_fusion), channel_id=1, source_target_pairs={{0,1},{1,0},{2,3},{3,2},{4,5},{5,4},{6,7},{7,6},{8,9},{9,8},{10,11... | collective-permute-start | bytes 405512 | tf_op jit(solution)/shard_map/ppermute | solution.py:340
  184.3 10.5 %all_to_all.93 = f32[16,8,264]{2,1,0:T(8,128)S(1)} all-to-all(f32[16,8,264]{2,1,0:T(8,128)S(1)} %fusion), channel_id=1, replica_groups=mesh['z'=8,'x'=4,'y'=4,'core'=2] {'x','y'}, dimensions={0} | all-to-all | bytes 270336 | tf_op jit(solution)/shard_map/all_to_all | solution.py:318
  194.8 10.0 %all_to_all.94 = f32[8,8,264]{2,1,0:T(8,128)S(1)} all-to-all(f32[8,8,264]{2,1,0:T(8,128)S(1)} %broadcast_in_dim.16), channel_id=1, replica_groups=mesh['z'=8,'x'=4,'y'=4,'core'=2] {'z'}, dimensions={0} | all-to-all | bytes 135168 | tf_op jit(solution)/shard_map/all_to_all | solution.py:318
  204.9 10.2 %all_to_all.95 = f32[16,8,264]{2,1,0:T(8,128)S(1)} all-to-all(f32[16,8,264]{2,1,0:T(8,128)S(1)} %broadcast_in_dim.17), channel_id=1, replica_groups=mesh['z'=8,'x'=4,'y'=4,'core'=2] {'x','y'}, dimensions={0} | all-to-all | bytes 270336 | tf_op jit(solution)/shard_map/all_to_all | solution.py:318
  215.1 4.1 %collective-permute-start.10 = (f32[128,264]{1,0:T(8,128)S(1)}, f32[128,264]{1,0:T(8,128)S(1)}, u32[]{:S(2)}, u32[]{:S(2)}) collective-permute-start(f32[128,264]{1,0:T(8,128)S(1)} %bitcast.41), channel_id=1, source_target_pairs={{0,1},{1,0},{2,3},{3,2},{4,5},{5,4},{6,7},{7,6},{8,9},{9,8},{10,11... | collective-permute-start | bytes 405512 | tf_op jit(solution)/shard_map/ppermute | solution.py:344
  220.4 7.3 %shard_map.74 = (bf16[1,2,1024,1024]{3,2,1,0:T(8,128)(2,1)}, f32[2,32,1024]{2,1,0:T(8,128)}, f32[2,32,1024]{2,1,0:T(8,128)}) custom-call(f32[2,128,264]{2,1,0:T(8,128)S(1)} %pad_maximum_fusion.1.q_sum, f32[64,1024]{1,0:T(8,128)S(1)} %get-tuple-element.24.p_raw, bf16[2,1024,1024]{2,1,0:T(8,128)(2,1)} %get-tuple-element.20.high, ...), custom_call_target="tpu_custom_call" | custom-call | tf_op jit(solution)/shard_map/pallas_call | solution.py:310
  (46 shorter events, 10.5 us)
Async XLA Ops:
  0.6 10.7 %copy-start.2 = (f32[2,32,1024]{2,1,0:T(8,128)S(1)}, f32[2,32,1024]{2,1,0:T(8,128)}, u32[]{:S(2)}) copy-start(f32[2,32,1024]{2,1,0:T(8,128)} %warm_q.3) | copy-start | bytes 786436
  4.5 35.9 %all-to-all-start = ((bf16[8,144,1024]{2,1,0:T(8,128)(2,1)}), bf16[8,144,1024]{2,1,0:T(8,128)(2,1)S(1)}, u32[]{:S(2)}, u32[]{:S(2)}) async-start(bf16[8,144,1024]{2,1,0:T(8,128)(2,1)} %shard_map.68), calls=%async_computation | async-start | bytes 4718592 | tf_op jit(solution)/shard_map/all_to_all | solution.py:318
  11.3 29.2 %copy-start.1 = (bf16[128,2048]{1,0:T(8,128)(2,1)S(1)}, bf16[128,2048]{1,0:T(8,128)(2,1)}, u32[]{:S(2)}) copy-start(bf16[128,2048]{1,0:T(8,128)(2,1)} %refs_0_) | copy-start | bytes 1572868
  40.4 38.8 %copy-start = (bf16[8,144,1024]{2,1,0:T(8,128)(2,1)}, bf16[8,144,1024]{2,1,0:T(8,128)(2,1)S(1)}, u32[]{:S(2)}) copy-start(bf16[8,144,1024]{2,1,0:T(8,128)(2,1)S(1)} %all-to-all-done.got) | copy-start | bytes 7077892
  40.4 23.6 %collective-permute-start = (bf16[128,2048]{1,0:T(8,128)(2,1)S(1)}, bf16[128,2048]{1,0:T(8,128)(2,1)}, u32[]{:S(2)}, u32[]{:S(2)}) collective-permute-start(bf16[128,2048]{1,0:T(8,128)(2,1)S(1)} %copy-done.1), channel_id=1, source_target_pairs={{0,2},{2,4},{4,6},{6,0},{1,3},{3,5},{5,7},{7,1},{8,10},{10,12},{12... | collective-permute-start | bytes 1572872 | tf_op jit(solution)/shard_map/ppermute | solution.py:379
  40.7 23.3 %collective-permute-start.1 = (bf16[128,2048]{1,0:T(8,128)(2,1)S(1)}, bf16[128,2048]{1,0:T(8,128)(2,1)}, u32[]{:S(2)}, u32[]{:S(2)}) collective-permute-start(bf16[128,2048]{1,0:T(8,128)(2,1)S(1)} %copy-done.1), channel_id=1, source_target_pairs={{0,6},{2,0},{4,2},{6,4},{1,7},{3,1},{5,3},{7,5},{8,14},{10,8},{12,... | collective-permute-start | bytes 1572872 | tf_op jit(solution)/shard_map/ppermute | solution.py:379
  43.1 21.9 %collective-permute-start.2 = (bf16[128,2048]{1,0:T(8,128)(2,1)S(1)}, bf16[128,2048]{1,0:T(8,128)(2,1)}, u32[]{:S(2)}, u32[]{:S(2)}) collective-permute-start(bf16[128,2048]{1,0:T(8,128)(2,1)S(1)} %copy-done.1), channel_id=1, source_target_pairs={{0,4},{2,6},{4,0},{6,2},{1,5},{3,7},{5,1},{7,3},{8,12},{10,14},{12... | collective-permute-start | bytes 1572872 | tf_op jit(solution)/shard_map/ppermute | solution.py:379
  65.0 14.2 %collective-permute-start.3 = (bf16[128,2048]{1,0:T(8,128)(2,1)S(1)}, bf16[128,2048]{1,0:T(8,128)(2,1)}, u32[]{:S(2)}, u32[]{:S(2)}) collective-permute-start(bf16[128,2048]{1,0:T(8,128)(2,1)S(1)} %copy-done.1), channel_id=1, source_target_pairs={{0,1},{1,0},{2,3},{3,2},{4,5},{5,4},{6,7},{7,6},{8,9},{9,8},{10,11... | collective-permute-start | bytes 1572872 | tf_op jit(solution)/shard_map/ppermute | solution.py:394
  67.9 11.3 %collective-permute-start.4 = (bf16[128,2048]{1,0:T(8,128)(2,1)}, bf16[128,2048]{1,0:T(8,128)(2,1)}, u32[]{:S(2)}, u32[]{:S(2)}) collective-permute-start(bf16[128,2048]{1,0:T(8,128)(2,1)} %collective-permute-done.refs_2_), channel_id=1, source_target_pairs={{0,1},{1,0},{2,3},{3,2},{4,5},{5,4},{6,7},{7,6},{8,9},{9,8},{10,11... | collective-permute-start | bytes 1572872 | tf_op jit(solution)/shard_map/ppermute | solution.py:394
  68.0 11.2 %collective-permute-start.5 = (bf16[128,2048]{1,0:T(8,128)(2,1)}, bf16[128,2048]{1,0:T(8,128)(2,1)}, u32[]{:S(2)}, u32[]{:S(2)}) collective-permute-start(bf16[128,2048]{1,0:T(8,128)(2,1)} %collective-permute-done.2.refs_4_), channel_id=1, source_target_pairs={{0,1},{1,0},{2,3},{3,2},{4,5},{5,4},{6,7},{7,6},{8,9},{9,8},{10,11... | collective-permute-start | bytes 1572872 | tf_op jit(solution)/shard_map/ppermute | solution.py:394
  68.4 10.8 %collective-permute-start.6 = (bf16[128,2048]{1,0:T(8,128)(2,1)}, bf16[128,2048]{1,0:T(8,128)(2,1)}, u32[]{:S(2)}, u32[]{:S(2)}) collective-permute-start(bf16[128,2048]{1,0:T(8,128)(2,1)} %collective-permute-done.1.refs_6_), channel_id=1, source_target_pairs={{0,1},{1,0},{2,3},{3,2},{4,5},{5,4},{6,7},{7,6},{8,9},{9,8},{10,11... | collective-permute-start | bytes 1572872 | tf_op jit(solution)/shard_map/ppermute | solution.py:394
  69.2 21.2 %all-to-all-start.2 = ((f32[32,8,256]{2,1,0:T(8,128)}), f32[32,8,256]{2,1,0:T(8,128)S(1)}, u32[]{:S(2)}, u32[]{:S(2)}) async-start(f32[32,8,256]{2,1,0:T(8,128)} %broadcast_in_dim.12), calls=%async_computation.2 | async-start | bytes 524288 | tf_op jit(solution)/shard_map/all_to_all | solution.py:318
  95.0 3.4 %collective-permute-start.7 = (f32[128,264]{1,0:T(8,128)S(1)}, f32[128,264]{1,0:T(8,128)S(1)}, u32[]{:S(2)}, u32[]{:S(2)}) collective-permute-start(f32[128,264]{1,0:T(8,128)S(1)} %dynamic-slice_bitcast_fusion.1), channel_id=1, source_target_pairs={{0,1},{1,0},{2,3},{3,2},{4,5},{5,4},{6,7},{7,6},{8,9},{9,8},{10,11... | collective-permute-start | bytes 405512 | tf_op jit(solution)/shard_map/ppermute | solution.py:340
  134.3 5.4 %collective-permute-start.8 = (f32[128,264]{1,0:T(8,128)S(1)}, f32[128,264]{1,0:T(8,128)S(1)}, u32[]{:S(2)}, u32[]{:S(2)}) collective-permute-start(f32[128,264]{1,0:T(8,128)S(1)} %bitcast.40), channel_id=1, source_target_pairs={{0,1},{1,0},{2,3},{3,2},{4,5},{5,4},{6,7},{7,6},{8,9},{9,8},{10,11... | collective-permute-start | bytes 405512 | tf_op jit(solution)/shard_map/ppermute | solution.py:344
  179.5 4.7 %collective-permute-start.9 = (f32[128,264]{1,0:T(8,128)S(1)}, f32[128,264]{1,0:T(8,128)S(1)}, u32[]{:S(2)}, u32[]{:S(2)}) collective-permute-start(f32[128,264]{1,0:T(8,128)S(1)} %dynamic-slice_bitcast_fusion), channel_id=1, source_target_pairs={{0,1},{1,0},{2,3},{3,2},{4,5},{5,4},{6,7},{7,6},{8,9},{9,8},{10,11... | collective-permute-start | bytes 405512 | tf_op jit(solution)/shard_map/ppermute | solution.py:340
  215.1 5.2 %collective-permute-start.10 = (f32[128,264]{1,0:T(8,128)S(1)}, f32[128,264]{1,0:T(8,128)S(1)}, u32[]{:S(2)}, u32[]{:S(2)}) collective-permute-start(f32[128,264]{1,0:T(8,128)S(1)} %bitcast.41), channel_id=1, source_target_pairs={{0,1},{1,0},{2,3},{3,2},{4,5},{5,4},{6,7},{7,6},{8,9},{9,8},{10,11... | collective-permute-start | bytes 405512 | tf_op jit(solution)/shard_map/ppermute | solution.py:344

commit v4 on v3

v4 whole, which is shorter than its diff:
```python
import functools
import math

import jax
import jax.numpy as jnp
from jax import lax
from jax.experimental import pallas as pl
from jax.experimental.pallas import tpu as pltpu
from jax.sharding import Mesh, PartitionSpec as P

D = 8192
BF16 = jnp.bfloat16
F32 = jnp.float32
REP = ("z", "x")
FSDP = ("y", "core")
VMEM = pl.BlockSpec(memory_space=pltpu.VMEM)
HBM = pl.BlockSpec(memory_space=pltpu.HBM)
MEGA = 1024 * 1024
CUTS = 4
PIECES = 2
LANES = 128


def halves(x):
    high = x.astype(BF16)
    return high, (x - high.astype(F32)).astype(BF16)


def dot(left, right, dims):
    return lax.dot_general(left, right, (dims, ((), ())), preferred_element_type=F32)


def exact(left, right, dims):
    return lax.dot_general(
        left,
        right,
        (dims, ((), ())),
        precision=lax.Precision.HIGHEST,
        preferred_element_type=F32,
    )


def narrow(x, rank):
    return x[:rank] + x[rank : 2 * rank]


def stack(ref, value, lane):
    height, width = value.shape[0], value.shape[1] // CUTS
    for i in range(CUTS):
        ref[i * height : (i + 1) * height, lane : lane + width] = value[
            :, i * width : (i + 1) * width
        ]


def unstack(value):
    height = value.shape[0] // CUTS
    return jnp.concatenate(
        [value[i * height : (i + 1) * height] for i in range(CUTS)], axis=1
    )


def pack(ref, pair):
    for h, value in enumerate(pair):
        height = value.shape[0]
        for i in range(value.shape[1] // LANES):
            ref[i * height : (i + 1) * height, h * LANES : (h + 1) * LANES] = value[
                :, i * LANES : (i + 1) * LANES
            ]


def unpack(value, height):
    return [
        jnp.concatenate(
            [
                value[i : i + height, h * LANES : (h + 1) * LANES]
                for i in range(0, value.shape[0], height)
            ],
            axis=1,
        )
        for h in range(2)
    ]


def prepare(acts, grads_out, warm_q, out, here, w_rows, in_sems, out_sems):
    parts, height, rows = out.shape
    tokens = acts.shape[0]
    piece = height - tokens
    moves = [
        pltpu.make_async_copy(
            acts.at[:, pl.ds(i * rows, rows)], here.at[i], in_sems.at[i]
        )
        for i in range(parts)
    ]
    for move in moves:
        move.start()
    sends = []
    for i in range(parts):
        moves[i].wait()
        sends.append(
            pltpu.make_async_copy(
                here.at[i], out.at[i, pl.ds(0, tokens)], out_sems.at[i]
            )
        )
        sends[-1].start()
    rank, width = warm_q.shape[1:]
    per = rank // piece
    for k in range(2):
        left = jnp.concatenate(halves(warm_q[k]), axis=0)
        grads = grads_out[:, k * width : (k + 1) * width]
        w = narrow(dot(left, grads, ((1,), (1,))), rank)
        for half, value in enumerate(halves(w)):
            for b in range(per):
                at = (half * 2 * per + k * per + b) * tokens
                w_rows[:, at : at + tokens] = value[b * piece : (b + 1) * piece]
    for i in range(parts):
        sends.append(
            pltpu.make_async_copy(
                w_rows, out.at[i, pl.ds(tokens, piece)], out_sems.at[parts + i]
            )
        )
        sends[-1].start()
    for send in sends:
        send.wait()


def error_part(place, error, warm_q, out, given):
    given[...] = error[0, 1 - place[1]]
    rank = warm_q.shape[1]
    for k in range(2):
        left = jnp.concatenate(halves(warm_q[k]), axis=0)
        out[k * rank : (k + 1) * rank] = narrow(
            dot(left, error[0, k], ((1,), (1,))), rank
        )


def first_left(got, p_error, out, w):
    parts, height, _ = got.shape
    tokens = w.shape[1] // parts
    piece = height - tokens
    total = w.shape[0] // piece
    for s in range(parts):
        for b in range(total):
            w[b * piece : (b + 1) * piece, s * tokens : (s + 1) * tokens] = got[
                s, tokens:height, b * tokens : (b + 1) * tokens
            ]
    p = p_error[...]
    both = jnp.zeros((w.shape[0], got.shape[2]), F32)
    for s in range(0, parts, 2):
        x = jnp.concatenate([got[s, :tokens], got[s + 1, :tokens]], axis=0)
        both += dot(w[:, s * tokens : (s + 2) * tokens], x, ((1,), (0,)))
    p += narrow(both, p.shape[0])
    rank = p.shape[0] // 2
    pack(out, (p[:rank], p[rank:]))


def merge(place, got, got_other, error, error_other, *refs):
    blocks, outs, scratch = refs[:5], refs[5:9], refs[9:]
    x, d, e, high, low, d_sems, x_sems, e_sems, out_sems = scratch
    y, core = place[0], place[1]
    rows = e.shape[1]
    tokens = blocks[0].shape[0] // 2
    cut = rows // CUTS
    d_moves, at = [], 0
    for i, block in enumerate(blocks):
        tall = block.shape[0]
        d_moves.append(
            pltpu.make_async_copy(block, d.at[pl.ds(at, tall)], d_sems.at[i])
        )
        at += tall
    x_moves, e_moves = [], []
    for h, source in enumerate((got, got_other)):
        for s in range(4):
            first = 2 * lax.rem(y + 4 - s, 4)
            for n, at in ((0, first + core), (1, first + 1 - core)):
                i = 2 * s + n
                x_moves.append(
                    pltpu.make_async_copy(
                        source.at[at, pl.ds(0, tokens)],
                        x.at[h, pl.ds(i * tokens, tokens)],
                        x_sems.at[8 * h + i],
                    )
                )
        for i in range(CUTS):
            at = pl.ds(i * cut, cut)
            part = error_other.at[at] if h else error.at[0, core, at]
            e_moves.append(
                pltpu.make_async_copy(part, e.at[h, at], e_sems.at[CUTS * h + i])
            )
    for move in (
        d_moves + x_moves[:8] + e_moves[:CUTS] + x_moves[8:] + e_moves[CUTS:]
    ):
        move.start()
    for move in d_moves:
        move.wait()
    sends = []
    for h in range(2):
        for move in x_moves[8 * h : 8 * h + 8]:
            move.wait()
        for i in range(CUTS):
            n = CUTS * h + i
            at = slice(i * cut, (i + 1) * cut)
            e_moves[n].wait()
            grad = dot(x[h, :, at], d[...], ((0,), (0,)))
            high[h, at], low[h, at] = halves(grad + e[h, at].astype(F32))
            for m, here in enumerate((high, low)):
                send = pltpu.make_async_copy(
                    here.at[h, at], outs[2 * h + m].at[at], out_sems.at[2 * n + m]
                )
                send.start()
                sends.append(send)
    for send in sends:
        send.wait()


def fetch(sources, high, low, sems):
    cut = high.shape[1] // PIECES
    moves = []
    for h in range(2):
        for i in range(PIECES):
            at = pl.ds(i * cut, cut)
            n = 2 * (PIECES * h + i)
            moves.append(
                [
                    pltpu.make_async_copy(
                        sources[2 * h].at[at], high.at[h, at], sems.at[n]
                    ),
                    pltpu.make_async_copy(
                        sources[2 * h + 1].at[at], low.at[h, at], sems.at[n + 1]
                    ),
                ]
            )
    for both in moves:
        for move in both:
            move.start()
    return moves


def multiply(left, high, low, dims):
    left_high, left_low = halves(left)
    both = jnp.concatenate([left_high, left_low], axis=0)
    return narrow(dot(both, high, dims), left.shape[0]) + dot(left_high, low, dims)


def right_factor(replicas, p_sum, *refs):
    sources, (p_mine, p_given, out, high, low, sems) = refs[:4], refs[4:]
    moves = fetch(sources, high, low, sems)
    p = [x / replicas for x in unpack(p_sum[...], p_mine.shape[0])]
    p_mine[...] = p[0]
    stack(p_given, p[1], 0)
    gram = q = 0.0
    for h in range(2):
        gram += exact(p[h], p[h], ((1,), (1,)))
    for h in range(2):
        for both in moves[PIECES * h : PIECES * (h + 1)]:
            for move in both:
                move.wait()
        q += multiply(p[h], high[h], low[h], ((1,), (0,)))
    stack(out, q, 0)
    stack(out, gram, q.shape[1] // CUTS)


def inverse_factors(grams):
    n = grams[0].shape[0]
    row = lax.broadcasted_iota(jnp.int32, (n, n), 0)
    column = lax.broadcasted_iota(jnp.int32, (n, n), 1)
    same = row == column
    one = same.astype(F32)
    below = lax.broadcasted_iota(jnp.int32, (n, 2 * n), 0)
    ts = [jnp.concatenate([gram, one], axis=1) for gram in grams]
    for j in range(n - 1):
        for i, t in enumerate(ts):
            pivot_row = t[j : j + 1] / t[j : j + 1, j : j + 1]
            factor = jnp.broadcast_to(t[:, j : j + 1], t.shape)
            ts[i] = t - jnp.where(below > j, factor, 0.0) * pivot_row
    inverses = []
    for t in ts:
        pivots = jnp.sum(jnp.where(same, t[:, :n], 0.0), axis=1, keepdims=True)
        inverses.append(t[:, n:] / jnp.sqrt(pivots))
    return inverses


def summed(sums, replicas, rank, width):
    last = (width + rank) // CUTS
    return (
        unstack(sums[:, : width // CUTS]) / replicas,
        unstack(sums[:, width // CUTS : last]) / replicas,
    )


def left_factor(replicas, rank, q_sum, *refs):
    sources, (out, high, low, sems) = refs[:4], refs[4:]
    moves = fetch(sources, high, low, sems)
    q, gram = summed(q_sum[...], replicas, rank, high.shape[2])
    (inverse,) = inverse_factors([gram])
    cut = high.shape[1] // PIECES
    p = []
    for n in range(2 * PIECES):
        for move in moves[n]:
            move.wait()
        h, i = divmod(n, PIECES)
        at = slice(i * cut, (i + 1) * cut)
        p.append(multiply(q, high[h, at], low[h, at], ((1,), (1,))))
    pair = [
        jnp.concatenate(p[PIECES * h : PIECES * (h + 1)], axis=1) for h in range(2)
    ]
    pack(out, [exact(inverse, x, ((1,), (0,))) for x in pair])


def finish(replicas, rank, place, q_mine, other, p_mine, *refs):
    sources, (new_error, p_factor, q_factor), scratch = refs[:4], refs[4:7], refs[7:]
    high, low, sems, out, out_sems, lefts, rights = scratch
    rows, width = high.shape[1:]
    moves = fetch(sources, high, low, sems)
    core = place[1]
    cut = rows // CUTS

    @pl.when(core >= 0)
    def _():
        sums = [
            summed(x, replicas, rank, width) for x in (q_mine[...], other[:, cut:])
        ]
        p_raws = (p_mine[...], unstack(other[:, :cut]))
        inverses = inverse_factors([gram for _, gram in sums])
        for n, p_raw in enumerate(p_raws):
            k = 1 - core if n else core
            q = exact(inverses[n], sums[n][0], ((1,), (0,)))
            q_factor[k] = q
            p_hat = exact(inverses[n], p_raw, ((1,), (0,)))
            p_factor[k] = p_hat * math.sqrt(D)
            p_high, p_low = halves(p_hat)
            q_high, q_low = halves(q)
            lefts[n] = jnp.concatenate([p_high, p_low, p_high, p_low], axis=0)
            rights[n] = jnp.concatenate([q_high, q_high, q_low, q_low], axis=0)
    sends = []
    for n in range(2):
        k = 1 - core if n else core
        for i in range(CUTS):
            if i % (CUTS // PIECES) == 0:
                for move in moves[PIECES * n + i * PIECES // CUTS]:
                    move.wait()
            at = slice(i * cut, (i + 1) * cut)
            approx = dot(lefts[n, :, at], rights[n], ((0,), (0,)))
            merged = high[n, at].astype(F32) + low[n, at].astype(F32)
            out[n, at] = (merged - approx).astype(BF16)
            send = pltpu.make_async_copy(
                out.at[n, at],
                new_error.at[0, k, pl.ds(i * cut, cut)],
                out_sems.at[CUTS * n + i],
            )
            send.start()
            sends.append(send)
    for send in sends:
        send.wait()


def call(kernel, outs, *args, space=52, cost=None, **kw):
    params = pltpu.CompilerParams(vmem_limit_bytes=space * MEGA)
    if cost is not None:
        kw["cost_estimate"] = pl.CostEstimate(
            flops=cost[0], bytes_accessed=cost[1], transcendentals=0
        )
    kw.setdefault("in_specs", [VMEM] * len(args))
    kw.setdefault("out_specs", [VMEM] * len(outs))
    return pl.pallas_call(kernel, out_shape=outs, compiler_params=params, **kw)(*args)


def array(shape, dtype):
    return jax.ShapeDtypeStruct(shape, dtype)


def swap(x, axis):
    return lax.all_to_all(x, axis, 0, 0, tiled=True)


def shared(x, axis):
    n = lax.axis_size(axis)
    return swap(x, axis).reshape(n, x.shape[0] // n, x.shape[1]).sum(0)


def copied(x, axis):
    everywhere = jnp.broadcast_to(x[None], (lax.axis_size(axis),) + x.shape)
    return swap(everywhere.reshape(-1, x.shape[1]), axis)


def total(x, axis):
    return copied(shared(x, axis), axis)


def total_everywhere(x):
    mine = shared(x, ("x", "y"))
    tall = mine.shape[0]
    mine = copied(mine, "z").reshape(-1, tall, mine.shape[1]).sum(0)
    return copied(mine, ("x", "y"))


def flip(x):
    return lax.ppermute(x, "core", [(0, 1), (1, 0)])


def on_device(acts, grads_out, error, warm_q):
    _, rank, width = warm_q.shape
    rows = error.shape[2]
    tokens = acts.shape[0]
    fsdp = lax.axis_size(FSDP)
    replicas = lax.axis_size(REP)
    piece = 4 * rank * tokens // rows
    pairs = 2 * rank

    (blocks,) = call(
        prepare,
        [array((fsdp, tokens + piece, rows), BF16)],
        acts,
        grads_out,
        warm_q,
        space=60,
        in_specs=[HBM, VMEM, VMEM],
        out_specs=[HBM],
        scratch_shapes=[
            pltpu.VMEM((fsdp, tokens, rows), BF16),
            pltpu.VMEM((piece, rows), BF16),
            pltpu.SemaphoreType.DMA((fsdp,)),
            pltpu.SemaphoreType.DMA((2 * fsdp,)),
        ],
    )
    got = swap(blocks, FSDP)

    core = lax.axis_index("core")
    place = jnp.stack([lax.axis_index("y"), core]).astype(jnp.int32)
    late_d, late_error, late_q, _ = lax.optimization_barrier(
        (grads_out, error, warm_q, blocks)
    )
    smem = pl.BlockSpec(memory_space=pltpu.SMEM)
    p_error, error_given = call(
        error_part,
        [array((pairs, rows), F32), array((rows, width), BF16)],
        place,
        late_error,
        late_q,
        in_specs=[smem, VMEM, VMEM],
        cost=(10**10, 10**8),
    )
    d_kept = lax.dynamic_slice_in_dim(late_d, core * width, width, 1)
    d_given = lax.dynamic_slice_in_dim(late_d, (1 - core) * width, width, 1)
    d_here = jnp.concatenate([d_kept, flip(d_given)], axis=0)
    d_here, p_error, got = lax.optimization_barrier((d_here, p_error, got))
    error_other = flip(error_given)

    up = [(i, (i + 1) % 4) for i in range(4)]
    down = [(i, (i + 3) % 4) for i in range(4)]
    d_up, d_down = lax.ppermute(d_here, "y", up), lax.ppermute(d_here, "y", down)
    got_other = flip(got)
    packed = array((rows // LANES * rank, 2 * LANES), F32)
    (p_part,) = call(
        first_left,
        [packed],
        got,
        p_error,
        space=16,
        scratch_shapes=[pltpu.VMEM((2 * pairs, fsdp * tokens), BF16)],
    )
    p_both = shared(p_part, REP)
    first, second = p_both[:, :LANES], p_both[:, LANES:]
    kept = jnp.where(core == 0, first, second)
    given = jnp.where(core == 0, second, first)
    p_piece, _, _ = lax.optimization_barrier(
        (jnp.concatenate([kept, flip(given)], axis=1), d_up, d_down)
    )
    far = [
        lax.ppermute(d_up[:tokens], "y", up),
        lax.ppermute(d_down[tokens:], "y", down),
    ]
    d = [d_here, d_up, *far, d_down]
    p_sum = copied(p_piece, REP)

    part = array((rows, width), BF16)
    local = [
        pltpu.VMEM((2, rows, width), BF16),
        pltpu.VMEM((2, rows, width), BF16),
        pltpu.SemaphoreType.DMA((4 * PIECES,)),
    ]
    merged = call(
        merge,
        [part] * 4,
        place,
        got,
        got_other,
        error,
        error_other,
        *d,
        in_specs=[smem] + [HBM] * 9,
        cost=(4*10**10, 2 * 10**7),
        out_specs=[HBM] * 4,
        scratch_shapes=[
            pltpu.VMEM((2, fsdp * tokens, rows), BF16),
            pltpu.VMEM((fsdp * tokens, width), BF16),
            pltpu.VMEM((2, rows, width), BF16),
            pltpu.VMEM((2, rows, width), BF16),
            pltpu.VMEM((2, rows, width), BF16),
            pltpu.SemaphoreType.DMA((5,)),
            pltpu.SemaphoreType.DMA((16,)),
            pltpu.SemaphoreType.DMA((2 * CUTS,)),
            pltpu.SemaphoreType.DMA((4 * CUTS,)),
        ],
    )
    high, low, high_given, low_given = merged

    def right(p_sum):
        *p_raw, sent = call(
            functools.partial(right_factor, replicas),
            [
                array((rank, rows), F32),
                array((CUTS * rank, rows // CUTS), F32),
                array((CUTS * rank, (width + rank) // CUTS), F32),
            ],
            p_sum,
            *merged,
            in_specs=[VMEM] + [HBM] * 4,
            scratch_shapes=local,
        )
        return p_raw, total_everywhere(sent)

    _, q_sum = right(p_sum)
    (p_part,) = call(
        functools.partial(left_factor, replicas, rank),
        [packed],
        q_sum,
        *merged,
        in_specs=[VMEM] + [HBM] * 4,
        scratch_shapes=local,
    )
    (p_mine, p_given), q_sum = right(total(p_part, REP))
    return call(
        functools.partial(finish, replicas, rank),
        [
            array((1, 2, rows, width), BF16),
            array((2, rank, rows), F32),
            array((2, rank, width), F32),
        ],
        place,
        q_sum,
        flip(jnp.concatenate([p_given, q_sum], axis=1)),
        p_mine,
        high,
        low,
        flip(high_given),
        flip(low_given),
        in_specs=[smem] + [VMEM] * 3 + [HBM] * 4,
        out_specs=[HBM, VMEM, VMEM],
        scratch_shapes=local
        + [
            pltpu.VMEM((2, rows, width), BF16),
            pltpu.SemaphoreType.DMA((2 * CUTS,)),
            pltpu.VMEM((2, 4 * rank, rows), BF16),
            pltpu.VMEM((2, 4 * rank, width), BF16),
        ],
    )


def solution(mesh):
    devices = mesh.devices.reshape(8, 4, 4, 2)
    torus = Mesh(devices, REP + FSDP)
    in_specs = (
        P(REP + FSDP, None),
        P(REP + FSDP, None),
        P(REP, None, FSDP, None),
        P(),
    )
    out_specs = (P(REP, None, FSDP, None), P(None, None, FSDP), P())
    return jax.shard_map(
        on_device, mesh=torus, in_specs=in_specs, out_specs=out_specs, check_vma=False
    )
```

time: 228 us -> 225 us (0.987)
  blocking collectives: 116 us -> 82 us
  starting transfers between devices: 37.2 us -> 48.2 us
  waiting for transfers between devices: 31 us -> 40 us
  Pallas kernels: 41.1 us -> 46.1 us
  local copies, waits for them, and re-layouts: 0.84 us -> 5.58 us
    all_to_all x9 -> x7, blocking collectives: 116 us -> 82 us  [swap(): return lax.all_to_all(x, axis, 0, 0, tiled=True)]
    all_to_all x2 -> x4, waiting for transfers between devices: 25.8 us -> 37.9 us  [swap(): return lax.all_to_all(x, axis, 0, 0, tiled=True)]
    all_to_all x2 -> x4, starting transfers between devices: 16.6 us -> 27.7 us  [swap(): return lax.all_to_all(x, axis, 0, 0, tiled=True)]
    pallas_call x8, Pallas kernels: 41.1 us -> 46.1 us  [call(): pl.pallas_call(kernel, out_shape=outs, compiler_params=params, **kw)(*args)]
    slice x0 -> x2, local copies, waits for them, and re-layouts: none -> 3.33 us  [the longest x1 1.67 us: on_device(): d_up[:tokens]]
    ppermute x11, waiting for transfers between devices: 5.22 us -> 2.1 us  [the longest x7 2.09 us: flip(): return lax.ppermute(x, 'core', [(0, 1), (1, 0)])]
  transfers between devices with their start and end apart: 13 -> 15, of which waited for: 7 -> 5; matrix products, arithmetic and copies ran while one was open for 0% -> 3% of each run, Pallas kernels for 7% -> 13%
where the time goes in v4:
time: 225 us; the launch traced here: 224 us
  blocking collectives  82 us (36%)
  starting transfers between devices  48.2 us (21%)
  Pallas kernels  46.1 us (20%)
  waiting for transfers between devices  40 us (18%)
  local copies, waits for them, and re-layouts  5.58 us (2%)
    all_to_all x7, blocking collectives, swap(): return lax.all_to_all(x, axis, 0, 0, tiled=True)  82 us
    pallas_call x8, Pallas kernels, call(): pl.pallas_call(kernel, out_shape=outs, compiler_params=params, **kw)(*args)  46.1 us
    all_to_all x4, waiting for transfers between devices, swap(): return lax.all_to_all(x, axis, 0, 0, tiled=True)  37.9 us
    all_to_all x4, starting transfers between devices, swap(): return lax.all_to_all(x, axis, 0, 0, tiled=True)  27.7 us
    ppermute x7, starting transfers between devices, flip(): return lax.ppermute(x, 'core', [(0, 1), (1, 0)])  17 us
  transfers between devices with their start and end apart: 15, of which 5 were waited for; matrix products, arithmetic and copies ran while one was open for 3% of the time, Pallas kernels for 13%

profile of v4, /device:TPU:1, one launch (start us, length us, event | category | flops | bytes accessed | tf_op | source)
XLA Modules:
  0.0 224.2 jit_solution(6437045958733645463)
XLA Ops:
  0.6 3.8 %shard_map.67 = bf16[8,144,1024]{2,1,0:T(8,128)(2,1)} custom-call(bf16[128,8192]{1,0:T(8,128)(2,1)} %acts.1, bf16[128,2048]{1,0:T(8,128)(2,1)} %grads_out.1, f32[2,32,1024]{2,1,0:T(8,128)} %warm_q.2), custom_call_target="tpu_custom_call" | custom-call | tf_op jit(solution)/shard_map/pallas_call | solution.py:364
  4.5 6.9 %all-to-all-start = ((bf16[8,144,1024]{2,1,0:T(8,128)(2,1)}), bf16[8,144,1024]{2,1,0:T(8,128)(2,1)S(1)}, u32[]{:S(2)}, u32[]{:S(2)}) async-start(bf16[8,144,1024]{2,1,0:T(8,128)(2,1)} %shard_map.67), calls=%async_computation | async-start | bytes 4718592 | tf_op jit(solution)/shard_map/all_to_all | solution.py:372
  12.3 4.9 %shard_map.68 = (f32[64,1024]{1,0:T(8,128)S(1)}, bf16[1024,1024]{1,0:T(8,128)(2,1)}) custom-call(s32[2]{0:T(128)S(1)} %pad_add_fusion.place, bf16[1,2,1024,1024]{3,2,1,0:T(8,128)(2,1)} %error.2, f32[2,32,1024]{2,1,0:T(8,128)S(1)} %copy-done.1), custom_call_target="tpu_custom_call" | custom-call | flops 10000000000 | bytes 100000000 | tf_op jit(solution)/shard_map/pallas_call | solution.py:364
  19.0 21.6 %all-to-all-done.got = bf16[8,144,1024]{2,1,0:T(8,128)(2,1)S(1)} async-done(((bf16[8,144,1024]{2,1,0:T(8,128)(2,1)}), bf16[8,144,1024]{2,1,0:T(8,128)(2,1)S(1)}, u32[]{:S(2)}, u32[]{:S(2)}) %all-to-all-start) | async-done | bytes 2359328 | tf_op jit(solution)/shard_map/all_to_all | solution.py:372
  44.0 10.2 %all-to-all-start.1 = ((f32[32,8,256]{2,1,0:T(8,128)}), f32[32,8,256]{2,1,0:T(8,128)S(1)}, u32[]{:S(2)}, u32[]{:S(2)}) async-start(f32[32,8,256]{2,1,0:T(8,128)} %bitcast.2), calls=%async_computation.1 | async-start | bytes 524288 | tf_op jit(solution)/shard_map/all_to_all | solution.py:372
  54.3 10.4 %all-to-all-done.1 = f32[32,8,256]{2,1,0:T(8,128)S(1)} async-done(((f32[32,8,256]{2,1,0:T(8,128)}), f32[32,8,256]{2,1,0:T(8,128)S(1)}, u32[]{:S(2)}, u32[]{:S(2)}) %all-to-all-start.1) | async-done | bytes 262176 | tf_op jit(solution)/shard_map/all_to_all | solution.py:372
  66.5 2.1 collective-permute-start.7
  70.2 3.7 %collective-permute-start.1 = (f32[8,128]{1,0:T(8,128)S(1)}, f32[8,128]{1,0:T(8,128)S(1)}, u32[]{:S(2)}, u32[]{:S(2)}) collective-permute-start(f32[8,128]{1,0:T(8,128)S(1)} %get-tuple-element.40), channel_id=1, source_target_pairs={{0,1},{1,0},{2,3},{3,2},{4,5},{5,4},{6,7},{7,6},{8,9},{9,8},{10,11... | collective-permute-start | bytes 12296 | tf_op jit(solution)/shard_map/ppermute | solution.py:397
  75.5 4.1 %all-to-all-start.2 = ((f32[32,8,256]{2,1,0:T(8,128)}), f32[32,8,256]{2,1,0:T(8,128)S(1)}, u32[]{:S(2)}, u32[]{:S(2)}) async-start(f32[32,8,256]{2,1,0:T(8,128)} %broadcast_in_dim.12), calls=%async_computation.2 | async-start | bytes 524288 | tf_op jit(solution)/shard_map/all_to_all | solution.py:372
  79.6 12.0 %shard_map.70 = (bf16[1024,1024]{1,0:T(8,128)(2,1)}, bf16[1024,1024]{1,0:T(8,128)(2,1)}, bf16[1024,1024]{1,0:T(8,128)(2,1)}, bf16[1024,1024]{1,0:T(8,128)(2,1)}) custom-call(s32[2]{0:T(128)S(1)} %pad_add_fusion.place, bf16[8,144,1024]{2,1,0:T(8,128)(2,1)} %copy-done, bf16[8,144,1024]{2,1,0:T(8,128)(2,1)} %collective-permute-done.4.got_other, ...), custom_call_target="tpu_custom_call" | custom-call | flops 40000000000 | bytes 20000000 | tf_op jit(solution)/shard_map/pallas_call | solution.py:364
  91.6 5.6 %shard_map.71 = (f32[32,1024]{1,0:T(8,128)}, f32[128,256]{1,0:T(8,128)}, f32[128,264]{1,0:T(8,128)}) custom-call(f32[256,256]{1,0:T(8,128)S(1)} %bitcast.12, bf16[1024,1024]{1,0:T(8,128)(2,1)} %get-tuple-element.29.refs_0_, bf16[1024,1024]{1,0:T(8,128)(2,1)} %get-tuple-element.30.refs_1_, bf16[1024,1024]{1,0:T(8,128)(2,1)} %get-tuple-element.31.refs_2_, ...), custom_call_target="tpu_custom_call" | custom-call | tf_op jit(solution)/shard_map/pallas_call | solution.py:364
  97.3 6.5 %all-to-all-start.3 = ((f32[16,8,264]{2,1,0:T(8,128)}), f32[16,8,264]{2,1,0:T(8,128)S(1)}, u32[]{:S(2)}, u32[]{:S(2)}) async-start(f32[16,8,264]{2,1,0:T(8,128)} %bitcast.4), calls=%async_computation.3 | async-start | bytes 393216 | tf_op jit(solution)/shard_map/all_to_all | solution.py:372
  105.0 5.9 %all-to-all-done.3 = f32[16,8,264]{2,1,0:T(8,128)S(1)} async-done(((f32[16,8,264]{2,1,0:T(8,128)}), f32[16,8,264]{2,1,0:T(8,128)S(1)}, u32[]{:S(2)}, u32[]{:S(2)}) %all-to-all-start.3) | async-done | bytes 135200 | tf_op jit(solution)/shard_map/all_to_all | solution.py:372
  110.9 14.1 %all_to_all.85 = f32[8,8,264]{2,1,0:T(8,128)S(1)} all-to-all(f32[8,8,264]{2,1,0:T(8,128)S(1)} %broadcast_in_dim.13), channel_id=1, replica_groups=mesh['z'=8,'x'=4,'y'=4,'core'=2] {'z'}, dimensions={0} | all-to-all | bytes 135168 | tf_op jit(solution)/shard_map/all_to_all | solution.py:372
  125.0 10.2 %all_to_all.86 = f32[16,8,264]{2,1,0:T(8,128)S(1)} all-to-all(f32[16,8,264]{2,1,0:T(8,128)S(1)} %broadcast_in_dim.14), channel_id=1, replica_groups=mesh['z'=8,'x'=4,'y'=4,'core'=2] {'x','y'}, dimensions={0} | all-to-all | bytes 270336 | tf_op jit(solution)/shard_map/all_to_all | solution.py:372
  135.2 6.0 %shard_map.72 = f32[256,256]{1,0:T(8,128)S(1)} custom-call(f32[128,264]{1,0:T(8,128)S(1)} %bitcast.15, bf16[1024,1024]{1,0:T(8,128)(2,1)} %get-tuple-element.29.refs_0_, bf16[1024,1024]{1,0:T(8,128)(2,1)} %get-tuple-element.30.refs_1_, bf16[1024,1024]{1,0:T(8,128)(2,1)} %get-tuple-element.31.refs_2_, bf16[1024,1024]{1,0:T(8,128)(2,1)} %get-tuple-element.32.refs_3_), custom_call_target="tpu_custom_call" | custom-call | tf_op jit(solution)/shard_map/pallas_call | solution.py:364
  141.2 13.6 %all_to_all.87 = f32[32,8,256]{2,1,0:T(8,128)S(1)} all-to-all(f32[32,8,256]{2,1,0:T(8,128)S(1)} %bitcast.14), channel_id=1, replica_groups=mesh['z'=8,'x'=4,'y'=4,'core'=2] {'z','x'}, dimensions={0} | all-to-all | bytes 524288 | tf_op jit(solution)/shard_map/all_to_all | solution.py:372
  154.8 13.7 %all_to_all.88 = f32[32,8,256]{2,1,0:T(8,128)S(1)} all-to-all(f32[32,8,256]{2,1,0:T(8,128)S(1)} %broadcast_in_dim.15), channel_id=1, replica_groups=mesh['z'=8,'x'=4,'y'=4,'core'=2] {'z','x'}, dimensions={0} | all-to-all | bytes 524288 | tf_op jit(solution)/shard_map/all_to_all | solution.py:372
  168.5 4.8 %shard_map.73 = (f32[32,1024]{1,0:T(8,128)S(1)}, f32[128,256]{1,0:T(8,128)S(1)}, f32[128,264]{1,0:T(8,128)S(1)}) custom-call(f32[256,256]{1,0:T(8,128)S(1)} %bitcast.13, bf16[1024,1024]{1,0:T(8,128)(2,1)} %get-tuple-element.29.refs_0_, bf16[1024,1024]{1,0:T(8,128)(2,1)} %get-tuple-element.30.refs_1_, bf16[1024,1024]{1,0:T(8,128)(2,1)} %get-tuple-element.31.refs_2_, ...), custom_call_target="tpu_custom_call" | custom-call | tf_op jit(solution)/shard_map/pallas_call | solution.py:364
  173.3 10.4 %all_to_all.89 = f32[16,8,264]{2,1,0:T(8,128)S(1)} all-to-all(f32[16,8,264]{2,1,0:T(8,128)S(1)} %bitcast.16), channel_id=1, replica_groups=mesh['z'=8,'x'=4,'y'=4,'core'=2] {'x','y'}, dimensions={0} | all-to-all | bytes 270336 | tf_op jit(solution)/shard_map/all_to_all | solution.py:372
  183.8 10.0 %all_to_all.90 = f32[8,8,264]{2,1,0:T(8,128)S(1)} all-to-all(f32[8,8,264]{2,1,0:T(8,128)S(1)} %broadcast_in_dim.16), channel_id=1, replica_groups=mesh['z'=8,'x'=4,'y'=4,'core'=2] {'z'}, dimensions={0} | all-to-all | bytes 135168 | tf_op jit(solution)/shard_map/all_to_all | solution.py:372
  193.8 10.2 %all_to_all.91 = f32[16,8,264]{2,1,0:T(8,128)S(1)} all-to-all(f32[16,8,264]{2,1,0:T(8,128)S(1)} %broadcast_in_dim.17), channel_id=1, replica_groups=mesh['z'=8,'x'=4,'y'=4,'core'=2] {'x','y'}, dimensions={0} | all-to-all | bytes 270336 | tf_op jit(solution)/shard_map/all_to_all | solution.py:372
  204.0 11.1 %collective-permute-start.8 = (f32[128,520]{1,0:T(8,128)S(1)}, f32[128,520]{1,0:T(8,128)S(1)}, u32[]{:S(2)}, u32[]{:S(2)}) collective-permute-start(f32[128,520]{1,0:T(8,128)S(1)} %pad_maximum_fusion.1), channel_id=1, source_target_pairs={{0,1},{1,0},{2,3},{3,2},{4,5},{5,4},{6,7},{7,6},{8,9},{9,8},{10,11... | collective-permute-start | bytes 798728 | tf_op jit(solution)/shard_map/ppermute | solution.py:397
  216.3 7.7 %shard_map.74 = (bf16[1,2,1024,1024]{3,2,1,0:T(8,128)(2,1)}, f32[2,32,1024]{2,1,0:T(8,128)}, f32[2,32,1024]{2,1,0:T(8,128)}) custom-call(s32[2]{0:T(128)S(1)} %pad_add_fusion.place, f32[128,264]{1,0:T(8,128)S(1)} %bitcast.11, f32[128,520]{1,0:T(8,128)S(1)} %collective-permute-done.8.other, f32[32,1024]{1,0:T(8,128)S(1)} %get-tuple-element.36.p_mine, ...), custom_call_target="tpu_custom_call" | custom-call | tf_op jit(solution)/shard_map/pallas_call | solution.py:364
  (51 shorter events, 13.8 us)
Async XLA Ops:
  4.5 6.9 %copy-start.3 = (bf16[128,2048]{1,0:T(8,128)(2,1)S(1)}, bf16[128,2048]{1,0:T(8,128)(2,1)}, u32[]{:S(2)}) copy-start(bf16[128,2048]{1,0:T(8,128)(2,1)} %grads_out.1) | copy-start | bytes 1572868
  4.5 7.9 %copy-start.1 = (f32[2,32,1024]{2,1,0:T(8,128)S(1)}, f32[2,32,1024]{2,1,0:T(8,128)}, u32[]{:S(2)}) copy-start(f32[2,32,1024]{2,1,0:T(8,128)} %warm_q.2) | copy-start | bytes 786436
  4.5 36.1 %all-to-all-start = ((bf16[8,144,1024]{2,1,0:T(8,128)(2,1)}), bf16[8,144,1024]{2,1,0:T(8,128)(2,1)S(1)}, u32[]{:S(2)}, u32[]{:S(2)}) async-start(bf16[8,144,1024]{2,1,0:T(8,128)(2,1)} %shard_map.67), calls=%async_computation | async-start | bytes 4718592 | tf_op jit(solution)/shard_map/all_to_all | solution.py:372
  12.1 5.2 %collective-permute-start = (bf16[128,1024]{1,0:T(8,128)(2,1)}, bf16[128,1024]{1,0:T(8,128)(2,1)S(1)}, u32[]{:S(2)}, u32[]{:S(2)}) collective-permute-start(bf16[128,1024]{1,0:T(8,128)(2,1)} %get-tuple-element.38), channel_id=1, source_target_pairs={{0,1},{1,0},{2,3},{3,2},{4,5},{5,4},{6,7},{7,6},{8,9},{9,8},{10,11... | collective-permute-start | bytes 786440 | tf_op jit(solution)/shard_map/ppermute | solution.py:397
  17.3 0.7 copy-start.4
  40.5 25.9 %copy-start = (bf16[8,144,1024]{2,1,0:T(8,128)(2,1)}, bf16[8,144,1024]{2,1,0:T(8,128)(2,1)S(1)}, u32[]{:S(2)}) copy-start(bf16[8,144,1024]{2,1,0:T(8,128)(2,1)S(1)} %all-to-all-done.got) | copy-start | bytes 7077892
  40.5 39.0 %collective-permute-start.4 = (bf16[8,144,1024]{2,1,0:T(8,128)(2,1)S(1)}, bf16[8,144,1024]{2,1,0:T(8,128)(2,1)}, u32[]{:S(2)}, u32[]{:S(2)}) collective-permute-start(bf16[8,144,1024]{2,1,0:T(8,128)(2,1)S(1)} %all-to-all-done.got), channel_id=1, source_target_pairs={{0,1},{1,0},{2,3},{3,2},{4,5},{5,4},{6,7},{7,6},{8,9},{9,8},{10,11... | collective-permute-start | bytes 7077896 | tf_op jit(solution)/shard_map/ppermute | solution.py:397
  41.4 38.1 %collective-permute-start.5 = (bf16[1024,1024]{1,0:T(8,128)(2,1)}, bf16[1024,1024]{1,0:T(8,128)(2,1)}, u32[]{:S(2)}, u32[]{:S(2)}) collective-permute-start(bf16[1024,1024]{1,0:T(8,128)(2,1)} %get-tuple-element.28), channel_id=1, source_target_pairs={{0,1},{1,0},{2,3},{3,2},{4,5},{5,4},{6,7},{7,6},{8,9},{9,8},{10,11... | collective-permute-start | bytes 6291464 | tf_op jit(solution)/shard_map/ppermute | solution.py:397
  41.4 23.4 %collective-permute-start.3 = (bf16[256,1024]{1,0:T(8,128)(2,1)S(1)}, bf16[256,1024]{1,0:T(8,128)(2,1)}, u32[]{:S(2)}, u32[]{:S(2)}) collective-permute-start(bf16[256,1024]{1,0:T(8,128)(2,1)S(1)} %pad_maximum_fusion.refs_0_), channel_id=1, source_target_pairs={{0,6},{2,0},{4,2},{6,4},{1,7},{3,1},{5,3},{7,5},{8,14},{10,8},{12,... | collective-permute-start | bytes 1572872 | tf_op jit(solution)/shard_map/ppermute | solution.py:450
  42.3 26.3 %collective-permute-start.2 = (bf16[256,1024]{1,0:T(8,128)(2,1)S(1)}, bf16[256,1024]{1,0:T(8,128)(2,1)}, u32[]{:S(2)}, u32[]{:S(2)}) collective-permute-start(bf16[256,1024]{1,0:T(8,128)(2,1)S(1)} %pad_maximum_fusion.refs_0_), channel_id=1, source_target_pairs={{0,2},{2,4},{4,6},{6,0},{1,3},{3,5},{5,7},{7,1},{8,10},{10,12},{12... | collective-permute-start | bytes 1572872 | tf_op jit(solution)/shard_map/ppermute | solution.py:450
  44.0 20.7 %all-to-all-start.1 = ((f32[32,8,256]{2,1,0:T(8,128)}), f32[32,8,256]{2,1,0:T(8,128)S(1)}, u32[]{:S(2)}, u32[]{:S(2)}) async-start(f32[32,8,256]{2,1,0:T(8,128)} %bitcast.2), calls=%async_computation.1 | async-start | bytes 524288 | tf_op jit(solution)/shard_map/all_to_all | solution.py:372
  66.5 13.1 %collective-permute-start.7 = (bf16[128,1024]{1,0:T(8,128)(2,1)}, bf16[128,1024]{1,0:T(8,128)(2,1)S(1)}, u32[]{:S(2)}, u32[]{:S(2)}) collective-permute-start(bf16[128,1024]{1,0:T(8,128)(2,1)} %slice.19), channel_id=1, source_target_pairs={{0,6},{2,0},{4,2},{6,4},{1,7},{3,1},{5,3},{7,5},{8,14},{10,8},{12,... | collective-permute-start | bytes 786440 | tf_op jit(solution)/shard_map/ppermute | solution.py:470
  70.2 9.3 %collective-permute-start.6 = (bf16[128,1024]{1,0:T(8,128)(2,1)}, bf16[128,1024]{1,0:T(8,128)(2,1)}, u32[]{:S(2)}, u32[]{:S(2)}) collective-permute-start(bf16[128,1024]{1,0:T(8,128)(2,1)} %slice.18), channel_id=1, source_target_pairs={{0,2},{2,4},{4,6},{6,0},{1,3},{3,5},{5,7},{7,1},{8,10},{10,12},{12... | collective-permute-start | bytes 786440 | tf_op jit(solution)/shard_map/ppermute | solution.py:469
  70.2 4.5 %collective-permute-start.1 = (f32[8,128]{1,0:T(8,128)S(1)}, f32[8,128]{1,0:T(8,128)S(1)}, u32[]{:S(2)}, u32[]{:S(2)}) collective-permute-start(f32[8,128]{1,0:T(8,128)S(1)} %get-tuple-element.40), channel_id=1, source_target_pairs={{0,1},{1,0},{2,3},{3,2},{4,5},{5,4},{6,7},{7,6},{8,9},{9,8},{10,11... | collective-permute-start | bytes 12296 | tf_op jit(solution)/shard_map/ppermute | solution.py:397
  75.5 16.1 %all-to-all-start.2 = ((f32[32,8,256]{2,1,0:T(8,128)}), f32[32,8,256]{2,1,0:T(8,128)S(1)}, u32[]{:S(2)}, u32[]{:S(2)}) async-start(f32[32,8,256]{2,1,0:T(8,128)} %broadcast_in_dim.12), calls=%async_computation.2 | async-start | bytes 524288 | tf_op jit(solution)/shard_map/all_to_all | solution.py:372
  91.6 13.3 %copy-start.2 = (bf16[1024,1024]{1,0:T(8,128)(2,1)S(1)}, bf16[1024,1024]{1,0:T(8,128)(2,1)}, u32[]{:S(2)}) copy-start(bf16[1024,1024]{1,0:T(8,128)(2,1)} %get-tuple-element.32.refs_3_) | copy-start | bytes 6291460
  97.3 13.6 %all-to-all-start.3 = ((f32[16,8,264]{2,1,0:T(8,128)}), f32[16,8,264]{2,1,0:T(8,128)S(1)}, u32[]{:S(2)}, u32[]{:S(2)}) async-start(f32[16,8,264]{2,1,0:T(8,128)} %bitcast.4), calls=%async_computation.3 | async-start | bytes 393216 | tf_op jit(solution)/shard_map/all_to_all | solution.py:372
  103.8 112.5 %collective-permute-start.9 = (bf16[1024,1024]{1,0:T(8,128)(2,1)}, bf16[1024,1024]{1,0:T(8,128)(2,1)}, u32[]{:S(2)}, u32[]{:S(2)}) collective-permute-start(bf16[1024,1024]{1,0:T(8,128)(2,1)} %get-tuple-element.31.refs_2_), channel_id=1, source_target_pairs={{0,1},{1,0},{2,3},{3,2},{4,5},{5,4},{6,7},{7,6},{8,9},{9,8},{10,11... | collective-permute-start | bytes 6291464 | tf_op jit(solution)/shard_map/ppermute | solution.py:397
  104.9 111.4 %collective-permute-start.10 = (bf16[1024,1024]{1,0:T(8,128)(2,1)S(1)}, bf16[1024,1024]{1,0:T(8,128)(2,1)}, u32[]{:S(2)}, u32[]{:S(2)}) collective-permute-start(bf16[1024,1024]{1,0:T(8,128)(2,1)S(1)} %copy-done.2), channel_id=1, source_target_pairs={{0,1},{1,0},{2,3},{3,2},{4,5},{5,4},{6,7},{7,6},{8,9},{9,8},{10,11... | collective-permute-start | bytes 6291464 | tf_op jit(solution)/shard_map/ppermute | solution.py:397
  204.0 12.3 %collective-permute-start.8 = (f32[128,520]{1,0:T(8,128)S(1)}, f32[128,520]{1,0:T(8,128)S(1)}, u32[]{:S(2)}, u32[]{:S(2)}) collective-permute-start(f32[128,520]{1,0:T(8,128)S(1)} %pad_maximum_fusion.1), channel_id=1, source_target_pairs={{0,1},{1,0},{2,3},{3,2},{4,5},{5,4},{6,7},{7,6},{8,9},{9,8},{10,11... | collective-permute-start | bytes 798728 | tf_op jit(solution)/shard_map/ppermute | solution.py:397

commit v5 on v4

--- a/solution.py
+++ b/solution.py
@@ -18,6 +18,7 @@
 MEGA = 1024 * 1024
 CUTS = 4
 PIECES = 2
+MERGE_CUTS = 1
 LANES = 128
 
 
@@ -159,7 +160,7 @@
     y, core = place[0], place[1]
     rows = e.shape[1]
     tokens = blocks[0].shape[0] // 2
-    cut = rows // CUTS
+    cut = rows // MERGE_CUTS
     d_moves, at = [], 0
     for i, block in enumerate(blocks):
         tall = block.shape[0]
@@ -180,14 +181,14 @@
                         x_sems.at[8 * h + i],
                     )
                 )
-        for i in range(CUTS):
+        for i in range(MERGE_CUTS):
             at = pl.ds(i * cut, cut)
             part = error_other.at[at] if h else error.at[0, core, at]
             e_moves.append(
-                pltpu.make_async_copy(part, e.at[h, at], e_sems.at[CUTS * h + i])
+                pltpu.make_async_copy(part, e.at[h, at], e_sems.at[MERGE_CUTS * h + i])
             )
     for move in (
-        d_moves + x_moves[:8] + e_moves[:CUTS] + x_moves[8:] + e_moves[CUTS:]
+        d_moves + x_moves[:8] + e_moves[:MERGE_CUTS] + x_moves[8:] + e_moves[MERGE_CUTS:]
     ):
         move.start()
     for move in d_moves:
@@ -196,8 +197,8 @@
     for h in range(2):
         for move in x_moves[8 * h : 8 * h + 8]:
             move.wait()
-        for i in range(CUTS):
-            n = CUTS * h + i
+        for i in range(MERGE_CUTS):
+            n = MERGE_CUTS * h + i
             at = slice(i * cut, (i + 1) * cut)
             e_moves[n].wait()
             grad = dot(x[h, :, at], d[...], ((0,), (0,)))
@@ -498,8 +499,8 @@
             pltpu.VMEM((2, rows, width), BF16),
             pltpu.SemaphoreType.DMA((5,)),
             pltpu.SemaphoreType.DMA((16,)),
-            pltpu.SemaphoreType.DMA((2 * CUTS,)),
-            pltpu.SemaphoreType.DMA((4 * CUTS,)),
+            pltpu.SemaphoreType.DMA((2 * MERGE_CUTS,)),
+            pltpu.SemaphoreType.DMA((4 * MERGE_CUTS,)),
         ],
     )
     high, low, high_given, low_given = merged

time: 225 us -> 224 us (level)
  transfers between devices with their start and end apart: 15 -> 15, of which waited for: 5 -> 6; matrix products, arithmetic and copies ran while one was open for 3% -> 3% of each run, Pallas kernels for 13% -> 12%
where the time goes in v5:
time: 224 us; the launch traced here: 223 us
  blocking collectives  82.1 us (37%)
  starting transfers between devices  48.3 us (22%)
  Pallas kernels  45 us (20%)
  waiting for transfers between devices  39.9 us (18%)
  local copies, waits for them, and re-layouts  5.58 us (2%)
    all_to_all x7, blocking collectives, swap(): return lax.all_to_all(x, axis, 0, 0, tiled=True)  82.1 us
    pallas_call x8, Pallas kernels, call(): pl.pallas_call(kernel, out_shape=outs, compiler_params=params, **kw)(*args)  45 us
    all_to_all x4, waiting for transfers between devices, swap(): return lax.all_to_all(x, axis, 0, 0, tiled=True)  37.8 us
    all_to_all x4, starting transfers between devices, swap(): return lax.all_to_all(x, axis, 0, 0, tiled=True)  27.2 us
    ppermute x7, starting transfers between devices, flip(): return lax.ppermute(x, 'core', [(0, 1), (1, 0)])  17.6 us
  transfers between devices with their start and end apart: 15, of which 6 were waited for; matrix products, arithmetic and copies ran while one was open for 3% of the time, Pallas kernels for 12%

profile of v5, /device:TPU:1, one launch (start us, length us, event | category | flops | bytes accessed | tf_op | source)
XLA Modules:
  0.0 223.2 jit_solution(407733368956623949)
XLA Ops:
  0.6 3.8 %shard_map.67 = bf16[8,144,1024]{2,1,0:T(8,128)(2,1)} custom-call(bf16[128,8192]{1,0:T(8,128)(2,1)} %acts.1, bf16[128,2048]{1,0:T(8,128)(2,1)} %grads_out.1, f32[2,32,1024]{2,1,0:T(8,128)} %warm_q.2), custom_call_target="tpu_custom_call" | custom-call | tf_op jit(solution)/shard_map/pallas_call | solution.py:365
  4.5 6.9 %all-to-all-start = ((bf16[8,144,1024]{2,1,0:T(8,128)(2,1)}), bf16[8,144,1024]{2,1,0:T(8,128)(2,1)S(1)}, u32[]{:S(2)}, u32[]{:S(2)}) async-start(bf16[8,144,1024]{2,1,0:T(8,128)(2,1)} %shard_map.67), calls=%async_computation | async-start | bytes 4718592 | tf_op jit(solution)/shard_map/all_to_all | solution.py:373
  12.3 4.9 %shard_map.68 = (f32[64,1024]{1,0:T(8,128)S(1)}, bf16[1024,1024]{1,0:T(8,128)(2,1)}) custom-call(s32[2]{0:T(128)S(1)} %pad_add_fusion.place, bf16[1,2,1024,1024]{3,2,1,0:T(8,128)(2,1)} %error.2, f32[2,32,1024]{2,1,0:T(8,128)S(1)} %copy-done.1), custom_call_target="tpu_custom_call" | custom-call | flops 10000000000 | bytes 100000000 | tf_op jit(solution)/shard_map/pallas_call | solution.py:365
  19.0 21.6 %all-to-all-done.got = bf16[8,144,1024]{2,1,0:T(8,128)(2,1)S(1)} async-done(((bf16[8,144,1024]{2,1,0:T(8,128)(2,1)}), bf16[8,144,1024]{2,1,0:T(8,128)(2,1)S(1)}, u32[]{:S(2)}, u32[]{:S(2)}) %all-to-all-start) | async-done | bytes 2359328 | tf_op jit(solution)/shard_map/all_to_all | solution.py:373
  44.0 10.2 %all-to-all-start.1 = ((f32[32,8,256]{2,1,0:T(8,128)}), f32[32,8,256]{2,1,0:T(8,128)S(1)}, u32[]{:S(2)}, u32[]{:S(2)}) async-start(f32[32,8,256]{2,1,0:T(8,128)} %bitcast.2), calls=%async_computation.1 | async-start | bytes 524288 | tf_op jit(solution)/shard_map/all_to_all | solution.py:373
  54.3 10.4 %all-to-all-done.1 = f32[32,8,256]{2,1,0:T(8,128)S(1)} async-done(((f32[32,8,256]{2,1,0:T(8,128)}), f32[32,8,256]{2,1,0:T(8,128)S(1)}, u32[]{:S(2)}, u32[]{:S(2)}) %all-to-all-start.1) | async-done | bytes 262176 | tf_op jit(solution)/shard_map/all_to_all | solution.py:373
  66.5 2.1 collective-permute-start.7
  70.2 3.7 %collective-permute-start.1 = (f32[8,128]{1,0:T(8,128)S(1)}, f32[8,128]{1,0:T(8,128)S(1)}, u32[]{:S(2)}, u32[]{:S(2)}) collective-permute-start(f32[8,128]{1,0:T(8,128)S(1)} %get-tuple-element.40), channel_id=1, source_target_pairs={{0,1},{1,0},{2,3},{3,2},{4,5},{5,4},{6,7},{7,6},{8,9},{9,8},{10,11... | collective-permute-start | bytes 12296 | tf_op jit(solution)/shard_map/ppermute | solution.py:398
  75.5 4.1 %all-to-all-start.2 = ((f32[32,8,256]{2,1,0:T(8,128)}), f32[32,8,256]{2,1,0:T(8,128)S(1)}, u32[]{:S(2)}, u32[]{:S(2)}) async-start(f32[32,8,256]{2,1,0:T(8,128)} %broadcast_in_dim.12), calls=%async_computation.2 | async-start | bytes 524288 | tf_op jit(solution)/shard_map/all_to_all | solution.py:373
  79.6 11.0 %shard_map.70 = (bf16[1024,1024]{1,0:T(8,128)(2,1)}, bf16[1024,1024]{1,0:T(8,128)(2,1)}, bf16[1024,1024]{1,0:T(8,128)(2,1)}, bf16[1024,1024]{1,0:T(8,128)(2,1)}) custom-call(s32[2]{0:T(128)S(1)} %pad_add_fusion.place, bf16[8,144,1024]{2,1,0:T(8,128)(2,1)} %copy-done, bf16[8,144,1024]{2,1,0:T(8,128)(2,1)} %collective-permute-done.4.got_other, ...), custom_call_target="tpu_custom_call" | custom-call | flops 40000000000 | bytes 20000000 | tf_op jit(solution)/shard_map/pallas_call | solution.py:365
  91.3 5.6 %shard_map.71 = (f32[32,1024]{1,0:T(8,128)}, f32[128,256]{1,0:T(8,128)}, f32[128,264]{1,0:T(8,128)}) custom-call(f32[256,256]{1,0:T(8,128)S(1)} %bitcast.12, bf16[1024,1024]{1,0:T(8,128)(2,1)} %get-tuple-element.29.refs_0_, bf16[1024,1024]{1,0:T(8,128)(2,1)} %get-tuple-element.30.refs_1_, bf16[1024,1024]{1,0:T(8,128)(2,1)} %get-tuple-element.31.refs_2_, ...), custom_call_target="tpu_custom_call" | custom-call | tf_op jit(solution)/shard_map/pallas_call | solution.py:365
  96.9 6.0 %all-to-all-start.3 = ((f32[16,8,264]{2,1,0:T(8,128)}), f32[16,8,264]{2,1,0:T(8,128)S(1)}, u32[]{:S(2)}, u32[]{:S(2)}) async-start(f32[16,8,264]{2,1,0:T(8,128)} %bitcast.4), calls=%async_computation.3 | async-start | bytes 393216 | tf_op jit(solution)/shard_map/all_to_all | solution.py:373
  104.7 5.1 %all-to-all-done.3 = f32[16,8,264]{2,1,0:T(8,128)S(1)} async-done(((f32[16,8,264]{2,1,0:T(8,128)}), f32[16,8,264]{2,1,0:T(8,128)S(1)}, u32[]{:S(2)}, u32[]{:S(2)}) %all-to-all-start.3) | async-done | bytes 135200 | tf_op jit(solution)/shard_map/all_to_all | solution.py:373
  109.9 14.1 %all_to_all.85 = f32[8,8,264]{2,1,0:T(8,128)S(1)} all-to-all(f32[8,8,264]{2,1,0:T(8,128)S(1)} %broadcast_in_dim.13), channel_id=1, replica_groups=mesh['z'=8,'x'=4,'y'=4,'core'=2] {'z'}, dimensions={0} | all-to-all | bytes 135168 | tf_op jit(solution)/shard_map/all_to_all | solution.py:373
  124.0 10.2 %all_to_all.86 = f32[16,8,264]{2,1,0:T(8,128)S(1)} all-to-all(f32[16,8,264]{2,1,0:T(8,128)S(1)} %broadcast_in_dim.14), channel_id=1, replica_groups=mesh['z'=8,'x'=4,'y'=4,'core'=2] {'x','y'}, dimensions={0} | all-to-all | bytes 270336 | tf_op jit(solution)/shard_map/all_to_all | solution.py:373
  134.2 6.0 %shard_map.72 = f32[256,256]{1,0:T(8,128)S(1)} custom-call(f32[128,264]{1,0:T(8,128)S(1)} %bitcast.15, bf16[1024,1024]{1,0:T(8,128)(2,1)} %get-tuple-element.29.refs_0_, bf16[1024,1024]{1,0:T(8,128)(2,1)} %get-tuple-element.30.refs_1_, bf16[1024,1024]{1,0:T(8,128)(2,1)} %get-tuple-element.31.refs_2_, bf16[1024,1024]{1,0:T(8,128)(2,1)} %get-tuple-element.32.refs_3_), custom_call_target="tpu_custom_call" | custom-call | tf_op jit(solution)/shard_map/pallas_call | solution.py:365
  140.2 13.6 %all_to_all.87 = f32[32,8,256]{2,1,0:T(8,128)S(1)} all-to-all(f32[32,8,256]{2,1,0:T(8,128)S(1)} %bitcast.14), channel_id=1, replica_groups=mesh['z'=8,'x'=4,'y'=4,'core'=2] {'z','x'}, dimensions={0} | all-to-all | bytes 524288 | tf_op jit(solution)/shard_map/all_to_all | solution.py:373
  153.8 13.7 %all_to_all.88 = f32[32,8,256]{2,1,0:T(8,128)S(1)} all-to-all(f32[32,8,256]{2,1,0:T(8,128)S(1)} %broadcast_in_dim.15), channel_id=1, replica_groups=mesh['z'=8,'x'=4,'y'=4,'core'=2] {'z','x'}, dimensions={0} | all-to-all | bytes 524288 | tf_op jit(solution)/shard_map/all_to_all | solution.py:373
  167.5 4.8 %shard_map.73 = (f32[32,1024]{1,0:T(8,128)S(1)}, f32[128,256]{1,0:T(8,128)S(1)}, f32[128,264]{1,0:T(8,128)S(1)}) custom-call(f32[256,256]{1,0:T(8,128)S(1)} %bitcast.13, bf16[1024,1024]{1,0:T(8,128)(2,1)} %get-tuple-element.29.refs_0_, bf16[1024,1024]{1,0:T(8,128)(2,1)} %get-tuple-element.30.refs_1_, bf16[1024,1024]{1,0:T(8,128)(2,1)} %get-tuple-element.31.refs_2_, ...), custom_call_target="tpu_custom_call" | custom-call | tf_op jit(solution)/shard_map/pallas_call | solution.py:365
  172.3 10.4 %all_to_all.89 = f32[16,8,264]{2,1,0:T(8,128)S(1)} all-to-all(f32[16,8,264]{2,1,0:T(8,128)S(1)} %bitcast.16), channel_id=1, replica_groups=mesh['z'=8,'x'=4,'y'=4,'core'=2] {'x','y'}, dimensions={0} | all-to-all | bytes 270336 | tf_op jit(solution)/shard_map/all_to_all | solution.py:373
  182.8 10.0 %all_to_all.90 = f32[8,8,264]{2,1,0:T(8,128)S(1)} all-to-all(f32[8,8,264]{2,1,0:T(8,128)S(1)} %broadcast_in_dim.16), channel_id=1, replica_groups=mesh['z'=8,'x'=4,'y'=4,'core'=2] {'z'}, dimensions={0} | all-to-all | bytes 135168 | tf_op jit(solution)/shard_map/all_to_all | solution.py:373
  192.8 10.2 %all_to_all.91 = f32[16,8,264]{2,1,0:T(8,128)S(1)} all-to-all(f32[16,8,264]{2,1,0:T(8,128)S(1)} %broadcast_in_dim.17), channel_id=1, replica_groups=mesh['z'=8,'x'=4,'y'=4,'core'=2] {'x','y'}, dimensions={0} | all-to-all | bytes 270336 | tf_op jit(solution)/shard_map/all_to_all | solution.py:373
  203.0 11.1 %collective-permute-start.8 = (f32[128,520]{1,0:T(8,128)S(1)}, f32[128,520]{1,0:T(8,128)S(1)}, u32[]{:S(2)}, u32[]{:S(2)}) collective-permute-start(f32[128,520]{1,0:T(8,128)S(1)} %pad_maximum_fusion.1), channel_id=1, source_target_pairs={{0,1},{1,0},{2,3},{3,2},{4,5},{5,4},{6,7},{7,6},{8,9},{9,8},{10,11... | collective-permute-start | bytes 798728 | tf_op jit(solution)/shard_map/ppermute | solution.py:398
  215.3 7.7 %shard_map.74 = (bf16[1,2,1024,1024]{3,2,1,0:T(8,128)(2,1)}, f32[2,32,1024]{2,1,0:T(8,128)}, f32[2,32,1024]{2,1,0:T(8,128)}) custom-call(s32[2]{0:T(128)S(1)} %pad_add_fusion.place, f32[128,264]{1,0:T(8,128)S(1)} %bitcast.11, f32[128,520]{1,0:T(8,128)S(1)} %collective-permute-done.8.other, f32[32,1024]{1,0:T(8,128)S(1)} %get-tuple-element.36.p_mine, ...), custom_call_target="tpu_custom_call" | custom-call | tf_op jit(solution)/shard_map/pallas_call | solution.py:365
  (51 shorter events, 15.0 us)
Async XLA Ops:
  4.5 6.9 %copy-start.3 = (bf16[128,2048]{1,0:T(8,128)(2,1)S(1)}, bf16[128,2048]{1,0:T(8,128)(2,1)}, u32[]{:S(2)}) copy-start(bf16[128,2048]{1,0:T(8,128)(2,1)} %grads_out.1) | copy-start | bytes 1572868
  4.5 7.9 %copy-start.1 = (f32[2,32,1024]{2,1,0:T(8,128)S(1)}, f32[2,32,1024]{2,1,0:T(8,128)}, u32[]{:S(2)}) copy-start(f32[2,32,1024]{2,1,0:T(8,128)} %warm_q.2) | copy-start | bytes 786436
  4.5 36.1 %all-to-all-start = ((bf16[8,144,1024]{2,1,0:T(8,128)(2,1)}), bf16[8,144,1024]{2,1,0:T(8,128)(2,1)S(1)}, u32[]{:S(2)}, u32[]{:S(2)}) async-start(bf16[8,144,1024]{2,1,0:T(8,128)(2,1)} %shard_map.67), calls=%async_computation | async-start | bytes 4718592 | tf_op jit(solution)/shard_map/all_to_all | solution.py:373
  12.1 5.2 %collective-permute-start = (bf16[128,1024]{1,0:T(8,128)(2,1)}, bf16[128,1024]{1,0:T(8,128)(2,1)S(1)}, u32[]{:S(2)}, u32[]{:S(2)}) collective-permute-start(bf16[128,1024]{1,0:T(8,128)(2,1)} %get-tuple-element.38), channel_id=1, source_target_pairs={{0,1},{1,0},{2,3},{3,2},{4,5},{5,4},{6,7},{7,6},{8,9},{9,8},{10,11... | collective-permute-start | bytes 786440 | tf_op jit(solution)/shard_map/ppermute | solution.py:398
  17.3 0.7 copy-start.4
  40.5 25.9 %copy-start = (bf16[8,144,1024]{2,1,0:T(8,128)(2,1)}, bf16[8,144,1024]{2,1,0:T(8,128)(2,1)S(1)}, u32[]{:S(2)}) copy-start(bf16[8,144,1024]{2,1,0:T(8,128)(2,1)S(1)} %all-to-all-done.got) | copy-start | bytes 7077892
  40.5 39.0 %collective-permute-start.4 = (bf16[8,144,1024]{2,1,0:T(8,128)(2,1)S(1)}, bf16[8,144,1024]{2,1,0:T(8,128)(2,1)}, u32[]{:S(2)}, u32[]{:S(2)}) collective-permute-start(bf16[8,144,1024]{2,1,0:T(8,128)(2,1)S(1)} %all-to-all-done.got), channel_id=1, source_target_pairs={{0,1},{1,0},{2,3},{3,2},{4,5},{5,4},{6,7},{7,6},{8,9},{9,8},{10,11... | collective-permute-start | bytes 7077896 | tf_op jit(solution)/shard_map/ppermute | solution.py:398
  41.4 38.1 %collective-permute-start.5 = (bf16[1024,1024]{1,0:T(8,128)(2,1)}, bf16[1024,1024]{1,0:T(8,128)(2,1)}, u32[]{:S(2)}, u32[]{:S(2)}) collective-permute-start(bf16[1024,1024]{1,0:T(8,128)(2,1)} %get-tuple-element.28), channel_id=1, source_target_pairs={{0,1},{1,0},{2,3},{3,2},{4,5},{5,4},{6,7},{7,6},{8,9},{9,8},{10,11... | collective-permute-start | bytes 6291464 | tf_op jit(solution)/shard_map/ppermute | solution.py:398
  41.4 23.4 %collective-permute-start.3 = (bf16[256,1024]{1,0:T(8,128)(2,1)S(1)}, bf16[256,1024]{1,0:T(8,128)(2,1)}, u32[]{:S(2)}, u32[]{:S(2)}) collective-permute-start(bf16[256,1024]{1,0:T(8,128)(2,1)S(1)} %pad_maximum_fusion.refs_0_), channel_id=1, source_target_pairs={{0,6},{2,0},{4,2},{6,4},{1,7},{3,1},{5,3},{7,5},{8,14},{10,8},{12,... | collective-permute-start | bytes 1572872 | tf_op jit(solution)/shard_map/ppermute | solution.py:451
  42.3 26.3 %collective-permute-start.2 = (bf16[256,1024]{1,0:T(8,128)(2,1)S(1)}, bf16[256,1024]{1,0:T(8,128)(2,1)}, u32[]{:S(2)}, u32[]{:S(2)}) collective-permute-start(bf16[256,1024]{1,0:T(8,128)(2,1)S(1)} %pad_maximum_fusion.refs_0_), channel_id=1, source_target_pairs={{0,2},{2,4},{4,6},{6,0},{1,3},{3,5},{5,7},{7,1},{8,10},{10,12},{12... | collective-permute-start | bytes 1572872 | tf_op jit(solution)/shard_map/ppermute | solution.py:451
  44.0 20.7 %all-to-all-start.1 = ((f32[32,8,256]{2,1,0:T(8,128)}), f32[32,8,256]{2,1,0:T(8,128)S(1)}, u32[]{:S(2)}, u32[]{:S(2)}) async-start(f32[32,8,256]{2,1,0:T(8,128)} %bitcast.2), calls=%async_computation.1 | async-start | bytes 524288 | tf_op jit(solution)/shard_map/all_to_all | solution.py:373
  66.5 13.1 %collective-permute-start.7 = (bf16[128,1024]{1,0:T(8,128)(2,1)}, bf16[128,1024]{1,0:T(8,128)(2,1)S(1)}, u32[]{:S(2)}, u32[]{:S(2)}) collective-permute-start(bf16[128,1024]{1,0:T(8,128)(2,1)} %slice.19), channel_id=1, source_target_pairs={{0,6},{2,0},{4,2},{6,4},{1,7},{3,1},{5,3},{7,5},{8,14},{10,8},{12,... | collective-permute-start | bytes 786440 | tf_op jit(solution)/shard_map/ppermute | solution.py:471
  70.2 9.3 %collective-permute-start.6 = (bf16[128,1024]{1,0:T(8,128)(2,1)}, bf16[128,1024]{1,0:T(8,128)(2,1)}, u32[]{:S(2)}, u32[]{:S(2)}) collective-permute-start(bf16[128,1024]{1,0:T(8,128)(2,1)} %slice.18), channel_id=1, source_target_pairs={{0,2},{2,4},{4,6},{6,0},{1,3},{3,5},{5,7},{7,1},{8,10},{10,12},{12... | collective-permute-start | bytes 786440 | tf_op jit(solution)/shard_map/ppermute | solution.py:470
  70.2 4.5 %collective-permute-start.1 = (f32[8,128]{1,0:T(8,128)S(1)}, f32[8,128]{1,0:T(8,128)S(1)}, u32[]{:S(2)}, u32[]{:S(2)}) collective-permute-start(f32[8,128]{1,0:T(8,128)S(1)} %get-tuple-element.40), channel_id=1, source_target_pairs={{0,1},{1,0},{2,3},{3,2},{4,5},{5,4},{6,7},{7,6},{8,9},{9,8},{10,11... | collective-permute-start | bytes 12296 | tf_op jit(solution)/shard_map/ppermute | solution.py:398
  75.5 15.8 %all-to-all-start.2 = ((f32[32,8,256]{2,1,0:T(8,128)}), f32[32,8,256]{2,1,0:T(8,128)S(1)}, u32[]{:S(2)}, u32[]{:S(2)}) async-start(f32[32,8,256]{2,1,0:T(8,128)} %broadcast_in_dim.12), calls=%async_computation.2 | async-start | bytes 524288 | tf_op jit(solution)/shard_map/all_to_all | solution.py:373
  91.3 13.3 %copy-start.2 = (bf16[1024,1024]{1,0:T(8,128)(2,1)S(1)}, bf16[1024,1024]{1,0:T(8,128)(2,1)}, u32[]{:S(2)}) copy-start(bf16[1024,1024]{1,0:T(8,128)(2,1)} %get-tuple-element.32.refs_3_) | copy-start | bytes 6291460
  96.9 12.9 %all-to-all-start.3 = ((f32[16,8,264]{2,1,0:T(8,128)}), f32[16,8,264]{2,1,0:T(8,128)S(1)}, u32[]{:S(2)}, u32[]{:S(2)}) async-start(f32[16,8,264]{2,1,0:T(8,128)} %bitcast.4), calls=%async_computation.3 | async-start | bytes 393216 | tf_op jit(solution)/shard_map/all_to_all | solution.py:373
  102.9 112.4 %collective-permute-start.9 = (bf16[1024,1024]{1,0:T(8,128)(2,1)}, bf16[1024,1024]{1,0:T(8,128)(2,1)}, u32[]{:S(2)}, u32[]{:S(2)}) collective-permute-start(bf16[1024,1024]{1,0:T(8,128)(2,1)} %get-tuple-element.31.refs_2_), channel_id=1, source_target_pairs={{0,1},{1,0},{2,3},{3,2},{4,5},{5,4},{6,7},{7,6},{8,9},{9,8},{10,11... | collective-permute-start | bytes 6291464 | tf_op jit(solution)/shard_map/ppermute | solution.py:398
  104.6 110.7 %collective-permute-start.10 = (bf16[1024,1024]{1,0:T(8,128)(2,1)S(1)}, bf16[1024,1024]{1,0:T(8,128)(2,1)}, u32[]{:S(2)}, u32[]{:S(2)}) collective-permute-start(bf16[1024,1024]{1,0:T(8,128)(2,1)S(1)} %copy-done.2), channel_id=1, source_target_pairs={{0,1},{1,0},{2,3},{3,2},{4,5},{5,4},{6,7},{7,6},{8,9},{9,8},{10,11... | collective-permute-start | bytes 6291464 | tf_op jit(solution)/shard_map/ppermute | solution.py:398
  203.0 12.3 %collective-permute-start.8 = (f32[128,520]{1,0:T(8,128)S(1)}, f32[128,520]{1,0:T(8,128)S(1)}, u32[]{:S(2)}, u32[]{:S(2)}) collective-permute-start(f32[128,520]{1,0:T(8,128)S(1)} %pad_maximum_fusion.1), channel_id=1, source_target_pairs={{0,1},{1,0},{2,3},{3,2},{4,5},{5,4},{6,7},{7,6},{8,9},{9,8},{10,11... | collective-permute-start | bytes 798728 | tf_op jit(solution)/shard_map/ppermute | solution.py:398

commit v6 on v5

--- a/solution.py
+++ b/solution.py
@@ -94,15 +94,6 @@
     ]
     for move in moves:
         move.start()
-    sends = []
-    for i in range(parts):
-        moves[i].wait()
-        sends.append(
-            pltpu.make_async_copy(
-                here.at[i], out.at[i, pl.ds(0, tokens)], out_sems.at[i]
-            )
-        )
-        sends[-1].start()
     rank, width = warm_q.shape[1:]
     per = rank // piece
     for k in range(2):
@@ -113,6 +104,15 @@
             for b in range(per):
                 at = (half * 2 * per + k * per + b) * tokens
                 w_rows[:, at : at + tokens] = value[b * piece : (b + 1) * piece]
+    sends = []
+    for i in range(parts):
+        moves[i].wait()
+        sends.append(
+            pltpu.make_async_copy(
+                here.at[i], out.at[i, pl.ds(0, tokens)], out_sems.at[i]
+            )
+        )
+        sends[-1].start()
     for i in range(parts):
         sends.append(
             pltpu.make_async_copy(
@@ -242,22 +242,25 @@
     return narrow(dot(both, high, dims), left.shape[0]) + dot(left_high, low, dims)
 
 
-def right_factor(replicas, p_sum, *refs):
+def right_factor(replicas, place, p_sum, *refs):
     sources, (p_mine, p_given, out, high, low, sems) = refs[:4], refs[4:]
     moves = fetch(sources, high, low, sems)
-    p = [x / replicas for x in unpack(p_sum[...], p_mine.shape[0])]
-    p_mine[...] = p[0]
-    stack(p_given, p[1], 0)
-    gram = q = 0.0
-    for h in range(2):
-        gram += exact(p[h], p[h], ((1,), (1,)))
-    for h in range(2):
+
+    @pl.when(place[1] >= 0)
+    def _():
+        p = [x / replicas for x in unpack(p_sum[...], p_mine.shape[0])]
+        p_mine[...] = p[0]
+        stack(p_given, p[1], 0)
+        gram = exact(p[0], p[0], ((1,), (1,))) + exact(p[1], p[1], ((1,), (1,)))
+        stack(out, gram, high.shape[2] // CUTS)
+
+    q = 0.0
+    for h, p in enumerate((p_mine[...], unstack(p_given[...]))):
         for both in moves[PIECES * h : PIECES * (h + 1)]:
             for move in both:
                 move.wait()
-        q += multiply(p[h], high[h], low[h], ((1,), (0,)))
+        q += multiply(p, high[h], low[h], ((1,), (0,)))
     stack(out, q, 0)
-    stack(out, gram, q.shape[1] // CUTS)
 
 
 def inverse_factors(grams):
@@ -513,9 +516,10 @@
                 array((CUTS * rank, rows // CUTS), F32),
                 array((CUTS * rank, (width + rank) // CUTS), F32),
             ],
+            place,
             p_sum,
             *merged,
-            in_specs=[VMEM] + [HBM] * 4,
+            in_specs=[smem, VMEM] + [HBM] * 4,
             scratch_shapes=local,
         )
         return p_raw, total_everywhere(sent)

time: 224 us -> 224 us (level)
  transfers between devices with their start and end apart: 15 -> 15, of which waited for: 6 -> 6; matrix products, arithmetic and copies ran while one was open for 3% -> 3% of each run, Pallas kernels for 12% -> 13%
where the time goes in v6:
time: 224 us; the launch traced here: 223 us
  blocking collectives  82.1 us (37%)
  starting transfers between devices  48.3 us (22%)
  Pallas kernels  44.9 us (20%)
  waiting for transfers between devices  39.9 us (18%)
  local copies, waits for them, and re-layouts  5.58 us (2%)
    all_to_all x7, blocking collectives, swap(): return lax.all_to_all(x, axis, 0, 0, tiled=True)  82.1 us
    pallas_call x8, Pallas kernels, call(): pl.pallas_call(kernel, out_shape=outs, compiler_params=params, **kw)(*args)  44.9 us
    all_to_all x4, waiting for transfers between devices, swap(): return lax.all_to_all(x, axis, 0, 0, tiled=True)  37.8 us
    all_to_all x4, starting transfers between devices, swap(): return lax.all_to_all(x, axis, 0, 0, tiled=True)  27.2 us
    ppermute x7, starting transfers between devices, flip(): return lax.ppermute(x, 'core', [(0, 1), (1, 0)])  17.6 us
  transfers between devices with their start and end apart: 15, of which 6 were waited for; matrix products, arithmetic and copies ran while one was open for 3% of the time, Pallas kernels for 13%

profile of v6, /device:TPU:1, one launch (start us, length us, event | category | flops | bytes accessed | tf_op | source)
XLA Modules:
  0.0 223.0 jit_solution(7901020037171958907)
XLA Ops:
  0.6 3.6 %shard_map.67 = bf16[8,144,1024]{2,1,0:T(8,128)(2,1)} custom-call(bf16[128,8192]{1,0:T(8,128)(2,1)} %acts.1, bf16[128,2048]{1,0:T(8,128)(2,1)} %grads_out.1, f32[2,32,1024]{2,1,0:T(8,128)} %warm_q.2), custom_call_target="tpu_custom_call" | custom-call | tf_op jit(solution)/shard_map/pallas_call | solution.py:368
  4.3 6.9 %all-to-all-start = ((bf16[8,144,1024]{2,1,0:T(8,128)(2,1)}), bf16[8,144,1024]{2,1,0:T(8,128)(2,1)S(1)}, u32[]{:S(2)}, u32[]{:S(2)}) async-start(bf16[8,144,1024]{2,1,0:T(8,128)(2,1)} %shard_map.67), calls=%async_computation | async-start | bytes 4718592 | tf_op jit(solution)/shard_map/all_to_all | solution.py:376
  12.2 4.9 %shard_map.68 = (f32[64,1024]{1,0:T(8,128)S(1)}, bf16[1024,1024]{1,0:T(8,128)(2,1)}) custom-call(s32[2]{0:T(128)S(1)} %pad_add_fusion.place, bf16[1,2,1024,1024]{3,2,1,0:T(8,128)(2,1)} %error.2, f32[2,32,1024]{2,1,0:T(8,128)S(1)} %copy-done.1), custom_call_target="tpu_custom_call" | custom-call | flops 10000000000 | bytes 100000000 | tf_op jit(solution)/shard_map/pallas_call | solution.py:368
  18.8 21.6 %all-to-all-done.got = bf16[8,144,1024]{2,1,0:T(8,128)(2,1)S(1)} async-done(((bf16[8,144,1024]{2,1,0:T(8,128)(2,1)}), bf16[8,144,1024]{2,1,0:T(8,128)(2,1)S(1)}, u32[]{:S(2)}, u32[]{:S(2)}) %all-to-all-start) | async-done | bytes 2359328 | tf_op jit(solution)/shard_map/all_to_all | solution.py:376
  43.9 10.2 %all-to-all-start.1 = ((f32[32,8,256]{2,1,0:T(8,128)}), f32[32,8,256]{2,1,0:T(8,128)S(1)}, u32[]{:S(2)}, u32[]{:S(2)}) async-start(f32[32,8,256]{2,1,0:T(8,128)} %bitcast.2), calls=%async_computation.1 | async-start | bytes 524288 | tf_op jit(solution)/shard_map/all_to_all | solution.py:376
  54.1 10.4 %all-to-all-done.1 = f32[32,8,256]{2,1,0:T(8,128)S(1)} async-done(((f32[32,8,256]{2,1,0:T(8,128)}), f32[32,8,256]{2,1,0:T(8,128)S(1)}, u32[]{:S(2)}, u32[]{:S(2)}) %all-to-all-start.1) | async-done | bytes 262176 | tf_op jit(solution)/shard_map/all_to_all | solution.py:376
  66.3 2.1 collective-permute-start.7
  70.1 3.7 %collective-permute-start.1 = (f32[8,128]{1,0:T(8,128)S(1)}, f32[8,128]{1,0:T(8,128)S(1)}, u32[]{:S(2)}, u32[]{:S(2)}) collective-permute-start(f32[8,128]{1,0:T(8,128)S(1)} %get-tuple-element.40), channel_id=1, source_target_pairs={{0,1},{1,0},{2,3},{3,2},{4,5},{5,4},{6,7},{7,6},{8,9},{9,8},{10,11... | collective-permute-start | bytes 12296 | tf_op jit(solution)/shard_map/ppermute | solution.py:401
  75.3 4.1 %all-to-all-start.2 = ((f32[32,8,256]{2,1,0:T(8,128)}), f32[32,8,256]{2,1,0:T(8,128)S(1)}, u32[]{:S(2)}, u32[]{:S(2)}) async-start(f32[32,8,256]{2,1,0:T(8,128)} %broadcast_in_dim.12), calls=%async_computation.2 | async-start | bytes 524288 | tf_op jit(solution)/shard_map/all_to_all | solution.py:376
  79.4 11.0 %shard_map.70 = (bf16[1024,1024]{1,0:T(8,128)(2,1)}, bf16[1024,1024]{1,0:T(8,128)(2,1)}, bf16[1024,1024]{1,0:T(8,128)(2,1)}, bf16[1024,1024]{1,0:T(8,128)(2,1)}) custom-call(s32[2]{0:T(128)S(1)} %pad_add_fusion.place, bf16[8,144,1024]{2,1,0:T(8,128)(2,1)} %copy-done, bf16[8,144,1024]{2,1,0:T(8,128)(2,1)} %collective-permute-done.4.got_other, ...), custom_call_target="tpu_custom_call" | custom-call | flops 40000000000 | bytes 20000000 | tf_op jit(solution)/shard_map/pallas_call | solution.py:368
  91.1 5.6 %shard_map.71 = (f32[32,1024]{1,0:T(8,128)}, f32[128,256]{1,0:T(8,128)}, f32[128,264]{1,0:T(8,128)}) custom-call(s32[2]{0:T(128)S(1)} %pad_add_fusion.place, f32[256,256]{1,0:T(8,128)S(1)} %bitcast.12, bf16[1024,1024]{1,0:T(8,128)(2,1)} %get-tuple-element.29.refs_0_, bf16[1024,1024]{1,0:T(8,128)(2,1)} %get-tuple-element.30.refs_1_, ...), custom_call_target="tpu_custom_call" | custom-call | tf_op jit(solution)/shard_map/pallas_call | solution.py:368
  96.7 6.0 %all-to-all-start.3 = ((f32[16,8,264]{2,1,0:T(8,128)}), f32[16,8,264]{2,1,0:T(8,128)S(1)}, u32[]{:S(2)}, u32[]{:S(2)}) async-start(f32[16,8,264]{2,1,0:T(8,128)} %bitcast.4), calls=%async_computation.3 | async-start | bytes 393216 | tf_op jit(solution)/shard_map/all_to_all | solution.py:376
  104.5 5.1 %all-to-all-done.3 = f32[16,8,264]{2,1,0:T(8,128)S(1)} async-done(((f32[16,8,264]{2,1,0:T(8,128)}), f32[16,8,264]{2,1,0:T(8,128)S(1)}, u32[]{:S(2)}, u32[]{:S(2)}) %all-to-all-start.3) | async-done | bytes 135200 | tf_op jit(solution)/shard_map/all_to_all | solution.py:376
  109.7 14.1 %all_to_all.85 = f32[8,8,264]{2,1,0:T(8,128)S(1)} all-to-all(f32[8,8,264]{2,1,0:T(8,128)S(1)} %broadcast_in_dim.13), channel_id=1, replica_groups=mesh['z'=8,'x'=4,'y'=4,'core'=2] {'z'}, dimensions={0} | all-to-all | bytes 135168 | tf_op jit(solution)/shard_map/all_to_all | solution.py:376
  123.8 10.2 %all_to_all.86 = f32[16,8,264]{2,1,0:T(8,128)S(1)} all-to-all(f32[16,8,264]{2,1,0:T(8,128)S(1)} %broadcast_in_dim.14), channel_id=1, replica_groups=mesh['z'=8,'x'=4,'y'=4,'core'=2] {'x','y'}, dimensions={0} | all-to-all | bytes 270336 | tf_op jit(solution)/shard_map/all_to_all | solution.py:376
  134.0 6.0 %shard_map.72 = f32[256,256]{1,0:T(8,128)S(1)} custom-call(f32[128,264]{1,0:T(8,128)S(1)} %bitcast.15, bf16[1024,1024]{1,0:T(8,128)(2,1)} %get-tuple-element.29.refs_0_, bf16[1024,1024]{1,0:T(8,128)(2,1)} %get-tuple-element.30.refs_1_, bf16[1024,1024]{1,0:T(8,128)(2,1)} %get-tuple-element.31.refs_2_, bf16[1024,1024]{1,0:T(8,128)(2,1)} %get-tuple-element.32.refs_3_), custom_call_target="tpu_custom_call" | custom-call | tf_op jit(solution)/shard_map/pallas_call | solution.py:368
  140.0 13.6 %all_to_all.87 = f32[32,8,256]{2,1,0:T(8,128)S(1)} all-to-all(f32[32,8,256]{2,1,0:T(8,128)S(1)} %bitcast.14), channel_id=1, replica_groups=mesh['z'=8,'x'=4,'y'=4,'core'=2] {'z','x'}, dimensions={0} | all-to-all | bytes 524288 | tf_op jit(solution)/shard_map/all_to_all | solution.py:376
  153.6 13.7 %all_to_all.88 = f32[32,8,256]{2,1,0:T(8,128)S(1)} all-to-all(f32[32,8,256]{2,1,0:T(8,128)S(1)} %broadcast_in_dim.15), channel_id=1, replica_groups=mesh['z'=8,'x'=4,'y'=4,'core'=2] {'z','x'}, dimensions={0} | all-to-all | bytes 524288 | tf_op jit(solution)/shard_map/all_to_all | solution.py:376
  167.3 4.8 %shard_map.73 = (f32[32,1024]{1,0:T(8,128)S(1)}, f32[128,256]{1,0:T(8,128)S(1)}, f32[128,264]{1,0:T(8,128)S(1)}) custom-call(s32[2]{0:T(128)S(1)} %pad_add_fusion.place, f32[256,256]{1,0:T(8,128)S(1)} %bitcast.13, bf16[1024,1024]{1,0:T(8,128)(2,1)} %get-tuple-element.29.refs_0_, bf16[1024,1024]{1,0:T(8,128)(2,1)} %get-tuple-element.30.refs_1_, ...), custom_call_target="tpu_custom_call" | custom-call | tf_op jit(solution)/shard_map/pallas_call | solution.py:368
  172.1 10.4 %all_to_all.89 = f32[16,8,264]{2,1,0:T(8,128)S(1)} all-to-all(f32[16,8,264]{2,1,0:T(8,128)S(1)} %bitcast.16), channel_id=1, replica_groups=mesh['z'=8,'x'=4,'y'=4,'core'=2] {'x','y'}, dimensions={0} | all-to-all | bytes 270336 | tf_op jit(solution)/shard_map/all_to_all | solution.py:376
  182.6 10.0 %all_to_all.90 = f32[8,8,264]{2,1,0:T(8,128)S(1)} all-to-all(f32[8,8,264]{2,1,0:T(8,128)S(1)} %broadcast_in_dim.16), channel_id=1, replica_groups=mesh['z'=8,'x'=4,'y'=4,'core'=2] {'z'}, dimensions={0} | all-to-all | bytes 135168 | tf_op jit(solution)/shard_map/all_to_all | solution.py:376
  192.6 10.2 %all_to_all.91 = f32[16,8,264]{2,1,0:T(8,128)S(1)} all-to-all(f32[16,8,264]{2,1,0:T(8,128)S(1)} %broadcast_in_dim.17), channel_id=1, replica_groups=mesh['z'=8,'x'=4,'y'=4,'core'=2] {'x','y'}, dimensions={0} | all-to-all | bytes 270336 | tf_op jit(solution)/shard_map/all_to_all | solution.py:376
  202.8 11.1 %collective-permute-start.8 = (f32[128,520]{1,0:T(8,128)S(1)}, f32[128,520]{1,0:T(8,128)S(1)}, u32[]{:S(2)}, u32[]{:S(2)}) collective-permute-start(f32[128,520]{1,0:T(8,128)S(1)} %pad_maximum_fusion.1), channel_id=1, source_target_pairs={{0,1},{1,0},{2,3},{3,2},{4,5},{5,4},{6,7},{7,6},{8,9},{9,8},{10,11... | collective-permute-start | bytes 798728 | tf_op jit(solution)/shard_map/ppermute | solution.py:401
  215.1 7.7 %shard_map.74 = (bf16[1,2,1024,1024]{3,2,1,0:T(8,128)(2,1)}, f32[2,32,1024]{2,1,0:T(8,128)}, f32[2,32,1024]{2,1,0:T(8,128)}) custom-call(s32[2]{0:T(128)S(1)} %pad_add_fusion.place, f32[128,264]{1,0:T(8,128)S(1)} %bitcast.11, f32[128,520]{1,0:T(8,128)S(1)} %collective-permute-done.8.other, f32[32,1024]{1,0:T(8,128)S(1)} %get-tuple-element.36.p_mine, ...), custom_call_target="tpu_custom_call" | custom-call | tf_op jit(solution)/shard_map/pallas_call | solution.py:368
  (51 shorter events, 15.0 us)
Async XLA Ops:
  4.3 6.9 %copy-start.3 = (bf16[128,2048]{1,0:T(8,128)(2,1)S(1)}, bf16[128,2048]{1,0:T(8,128)(2,1)}, u32[]{:S(2)}) copy-start(bf16[128,2048]{1,0:T(8,128)(2,1)} %grads_out.1) | copy-start | bytes 1572868
  4.3 7.9 %copy-start.1 = (f32[2,32,1024]{2,1,0:T(8,128)S(1)}, f32[2,32,1024]{2,1,0:T(8,128)}, u32[]{:S(2)}) copy-start(f32[2,32,1024]{2,1,0:T(8,128)} %warm_q.2) | copy-start | bytes 786436
  4.3 36.1 %all-to-all-start = ((bf16[8,144,1024]{2,1,0:T(8,128)(2,1)}), bf16[8,144,1024]{2,1,0:T(8,128)(2,1)S(1)}, u32[]{:S(2)}, u32[]{:S(2)}) async-start(bf16[8,144,1024]{2,1,0:T(8,128)(2,1)} %shard_map.67), calls=%async_computation | async-start | bytes 4718592 | tf_op jit(solution)/shard_map/all_to_all | solution.py:376
  12.0 5.2 %collective-permute-start = (bf16[128,1024]{1,0:T(8,128)(2,1)}, bf16[128,1024]{1,0:T(8,128)(2,1)S(1)}, u32[]{:S(2)}, u32[]{:S(2)}) collective-permute-start(bf16[128,1024]{1,0:T(8,128)(2,1)} %get-tuple-element.38), channel_id=1, source_target_pairs={{0,1},{1,0},{2,3},{3,2},{4,5},{5,4},{6,7},{7,6},{8,9},{9,8},{10,11... | collective-permute-start | bytes 786440 | tf_op jit(solution)/shard_map/ppermute | solution.py:401
  17.1 0.7 copy-start.4
  40.4 25.9 %copy-start = (bf16[8,144,1024]{2,1,0:T(8,128)(2,1)}, bf16[8,144,1024]{2,1,0:T(8,128)(2,1)S(1)}, u32[]{:S(2)}) copy-start(bf16[8,144,1024]{2,1,0:T(8,128)(2,1)S(1)} %all-to-all-done.got) | copy-start | bytes 7077892
  40.4 39.0 %collective-permute-start.4 = (bf16[8,144,1024]{2,1,0:T(8,128)(2,1)S(1)}, bf16[8,144,1024]{2,1,0:T(8,128)(2,1)}, u32[]{:S(2)}, u32[]{:S(2)}) collective-permute-start(bf16[8,144,1024]{2,1,0:T(8,128)(2,1)S(1)} %all-to-all-done.got), channel_id=1, source_target_pairs={{0,1},{1,0},{2,3},{3,2},{4,5},{5,4},{6,7},{7,6},{8,9},{9,8},{10,11... | collective-permute-start | bytes 7077896 | tf_op jit(solution)/shard_map/ppermute | solution.py:401
  41.2 38.1 %collective-permute-start.5 = (bf16[1024,1024]{1,0:T(8,128)(2,1)}, bf16[1024,1024]{1,0:T(8,128)(2,1)}, u32[]{:S(2)}, u32[]{:S(2)}) collective-permute-start(bf16[1024,1024]{1,0:T(8,128)(2,1)} %get-tuple-element.28), channel_id=1, source_target_pairs={{0,1},{1,0},{2,3},{3,2},{4,5},{5,4},{6,7},{7,6},{8,9},{9,8},{10,11... | collective-permute-start | bytes 6291464 | tf_op jit(solution)/shard_map/ppermute | solution.py:401
  41.3 23.3 %collective-permute-start.3 = (bf16[256,1024]{1,0:T(8,128)(2,1)S(1)}, bf16[256,1024]{1,0:T(8,128)(2,1)}, u32[]{:S(2)}, u32[]{:S(2)}) collective-permute-start(bf16[256,1024]{1,0:T(8,128)(2,1)S(1)} %pad_maximum_fusion.refs_0_), channel_id=1, source_target_pairs={{0,6},{2,0},{4,2},{6,4},{1,7},{3,1},{5,3},{7,5},{8,14},{10,8},{12,... | collective-permute-start | bytes 1572872 | tf_op jit(solution)/shard_map/ppermute | solution.py:454
  42.1 26.2 %collective-permute-start.2 = (bf16[256,1024]{1,0:T(8,128)(2,1)S(1)}, bf16[256,1024]{1,0:T(8,128)(2,1)}, u32[]{:S(2)}, u32[]{:S(2)}) collective-permute-start(bf16[256,1024]{1,0:T(8,128)(2,1)S(1)} %pad_maximum_fusion.refs_0_), channel_id=1, source_target_pairs={{0,2},{2,4},{4,6},{6,0},{1,3},{3,5},{5,7},{7,1},{8,10},{10,12},{12... | collective-permute-start | bytes 1572872 | tf_op jit(solution)/shard_map/ppermute | solution.py:454
  43.9 20.7 %all-to-all-start.1 = ((f32[32,8,256]{2,1,0:T(8,128)}), f32[32,8,256]{2,1,0:T(8,128)S(1)}, u32[]{:S(2)}, u32[]{:S(2)}) async-start(f32[32,8,256]{2,1,0:T(8,128)} %bitcast.2), calls=%async_computation.1 | async-start | bytes 524288 | tf_op jit(solution)/shard_map/all_to_all | solution.py:376
  66.3 13.1 %collective-permute-start.7 = (bf16[128,1024]{1,0:T(8,128)(2,1)}, bf16[128,1024]{1,0:T(8,128)(2,1)S(1)}, u32[]{:S(2)}, u32[]{:S(2)}) collective-permute-start(bf16[128,1024]{1,0:T(8,128)(2,1)} %slice.19), channel_id=1, source_target_pairs={{0,6},{2,0},{4,2},{6,4},{1,7},{3,1},{5,3},{7,5},{8,14},{10,8},{12,... | collective-permute-start | bytes 786440 | tf_op jit(solution)/shard_map/ppermute | solution.py:474
  70.0 9.3 %collective-permute-start.6 = (bf16[128,1024]{1,0:T(8,128)(2,1)}, bf16[128,1024]{1,0:T(8,128)(2,1)}, u32[]{:S(2)}, u32[]{:S(2)}) collective-permute-start(bf16[128,1024]{1,0:T(8,128)(2,1)} %slice.18), channel_id=1, source_target_pairs={{0,2},{2,4},{4,6},{6,0},{1,3},{3,5},{5,7},{7,1},{8,10},{10,12},{12... | collective-permute-start | bytes 786440 | tf_op jit(solution)/shard_map/ppermute | solution.py:473
  70.1 4.5 %collective-permute-start.1 = (f32[8,128]{1,0:T(8,128)S(1)}, f32[8,128]{1,0:T(8,128)S(1)}, u32[]{:S(2)}, u32[]{:S(2)}) collective-permute-start(f32[8,128]{1,0:T(8,128)S(1)} %get-tuple-element.40), channel_id=1, source_target_pairs={{0,1},{1,0},{2,3},{3,2},{4,5},{5,4},{6,7},{7,6},{8,9},{9,8},{10,11... | collective-permute-start | bytes 12296 | tf_op jit(solution)/shard_map/ppermute | solution.py:401
  75.3 15.8 %all-to-all-start.2 = ((f32[32,8,256]{2,1,0:T(8,128)}), f32[32,8,256]{2,1,0:T(8,128)S(1)}, u32[]{:S(2)}, u32[]{:S(2)}) async-start(f32[32,8,256]{2,1,0:T(8,128)} %broadcast_in_dim.12), calls=%async_computation.2 | async-start | bytes 524288 | tf_op jit(solution)/shard_map/all_to_all | solution.py:376
  91.1 13.3 %copy-start.2 = (bf16[1024,1024]{1,0:T(8,128)(2,1)S(1)}, bf16[1024,1024]{1,0:T(8,128)(2,1)}, u32[]{:S(2)}) copy-start(bf16[1024,1024]{1,0:T(8,128)(2,1)} %get-tuple-element.32.refs_3_) | copy-start | bytes 6291460
  96.7 12.9 %all-to-all-start.3 = ((f32[16,8,264]{2,1,0:T(8,128)}), f32[16,8,264]{2,1,0:T(8,128)S(1)}, u32[]{:S(2)}, u32[]{:S(2)}) async-start(f32[16,8,264]{2,1,0:T(8,128)} %bitcast.4), calls=%async_computation.3 | async-start | bytes 393216 | tf_op jit(solution)/shard_map/all_to_all | solution.py:376
  102.7 112.4 %collective-permute-start.9 = (bf16[1024,1024]{1,0:T(8,128)(2,1)}, bf16[1024,1024]{1,0:T(8,128)(2,1)}, u32[]{:S(2)}, u32[]{:S(2)}) collective-permute-start(bf16[1024,1024]{1,0:T(8,128)(2,1)} %get-tuple-element.31.refs_2_), channel_id=1, source_target_pairs={{0,1},{1,0},{2,3},{3,2},{4,5},{5,4},{6,7},{7,6},{8,9},{9,8},{10,11... | collective-permute-start | bytes 6291464 | tf_op jit(solution)/shard_map/ppermute | solution.py:401
  104.4 110.7 %collective-permute-start.10 = (bf16[1024,1024]{1,0:T(8,128)(2,1)S(1)}, bf16[1024,1024]{1,0:T(8,128)(2,1)}, u32[]{:S(2)}, u32[]{:S(2)}) collective-permute-start(bf16[1024,1024]{1,0:T(8,128)(2,1)S(1)} %copy-done.2), channel_id=1, source_target_pairs={{0,1},{1,0},{2,3},{3,2},{4,5},{5,4},{6,7},{7,6},{8,9},{9,8},{10,11... | collective-permute-start | bytes 6291464 | tf_op jit(solution)/shard_map/ppermute | solution.py:401
  202.8 12.3 %collective-permute-start.8 = (f32[128,520]{1,0:T(8,128)S(1)}, f32[128,520]{1,0:T(8,128)S(1)}, u32[]{:S(2)}, u32[]{:S(2)}) collective-permute-start(f32[128,520]{1,0:T(8,128)S(1)} %pad_maximum_fusion.1), channel_id=1, source_target_pairs={{0,1},{1,0},{2,3},{3,2},{4,5},{5,4},{6,7},{7,6},{8,9},{9,8},{10,11... | collective-permute-start | bytes 798728 | tf_op jit(solution)/shard_map/ppermute | solution.py:401

commit v7 on v6

--- a/solution.py
+++ b/solution.py
@@ -17,7 +17,7 @@
 HBM = pl.BlockSpec(memory_space=pltpu.HBM)
 MEGA = 1024 * 1024
 CUTS = 4
-PIECES = 2
+PIECES = 4
 MERGE_CUTS = 1
 LANES = 128
 

time: 224 us -> 227 us (1.013)
  Pallas kernels: 44.9 us -> 48.2 us
    pallas_call x8, Pallas kernels: 44.9 us -> 48.2 us  [call(): pl.pallas_call(kernel, out_shape=outs, compiler_params=params, **kw)(*args)]
where the time goes in v7:
time: 227 us; the launch traced here: 226 us
  blocking collectives  82.1 us (36%)
  starting transfers between devices  48.3 us (21%)
  Pallas kernels  48.2 us (21%)
  waiting for transfers between devices  39.9 us (18%)
  local copies, waits for them, and re-layouts  5.58 us (2%)
    all_to_all x7, blocking collectives, swap(): return lax.all_to_all(x, axis, 0, 0, tiled=True)  82.1 us
    pallas_call x8, Pallas kernels, call(): pl.pallas_call(kernel, out_shape=outs, compiler_params=params, **kw)(*args)  48.2 us
    all_to_all x4, waiting for transfers between devices, swap(): return lax.all_to_all(x, axis, 0, 0, tiled=True)  37.8 us
    all_to_all x4, starting transfers between devices, swap(): return lax.all_to_all(x, axis, 0, 0, tiled=True)  27.2 us
    ppermute x7, starting transfers between devices, flip(): return lax.ppermute(x, 'core', [(0, 1), (1, 0)])  17.6 us
  transfers between devices with their start and end apart: 15, of which 6 were waited for; matrix products, arithmetic and copies ran while one was open for 3% of the time, Pallas kernels for 13%

profile of v7, /device:TPU:1, one launch (start us, length us, event | category | flops | bytes accessed | tf_op | source)
XLA Modules:
  0.0 226.3 jit_solution(7974234187963308935)
XLA Ops:
  0.6 3.6 %shard_map.67 = bf16[8,144,1024]{2,1,0:T(8,128)(2,1)} custom-call(bf16[128,8192]{1,0:T(8,128)(2,1)} %acts.1, bf16[128,2048]{1,0:T(8,128)(2,1)} %grads_out.1, f32[2,32,1024]{2,1,0:T(8,128)} %warm_q.2), custom_call_target="tpu_custom_call" | custom-call | tf_op jit(solution)/shard_map/pallas_call | solution.py:368
  4.3 6.9 %all-to-all-start = ((bf16[8,144,1024]{2,1,0:T(8,128)(2,1)}), bf16[8,144,1024]{2,1,0:T(8,128)(2,1)S(1)}, u32[]{:S(2)}, u32[]{:S(2)}) async-start(bf16[8,144,1024]{2,1,0:T(8,128)(2,1)} %shard_map.67), calls=%async_computation | async-start | bytes 4718592 | tf_op jit(solution)/shard_map/all_to_all | solution.py:376
  12.2 4.9 %shard_map.68 = (f32[64,1024]{1,0:T(8,128)S(1)}, bf16[1024,1024]{1,0:T(8,128)(2,1)}) custom-call(s32[2]{0:T(128)S(1)} %pad_add_fusion.place, bf16[1,2,1024,1024]{3,2,1,0:T(8,128)(2,1)} %error.2, f32[2,32,1024]{2,1,0:T(8,128)S(1)} %copy-done.1), custom_call_target="tpu_custom_call" | custom-call | flops 10000000000 | bytes 100000000 | tf_op jit(solution)/shard_map/pallas_call | solution.py:368
  18.8 21.6 %all-to-all-done.got = bf16[8,144,1024]{2,1,0:T(8,128)(2,1)S(1)} async-done(((bf16[8,144,1024]{2,1,0:T(8,128)(2,1)}), bf16[8,144,1024]{2,1,0:T(8,128)(2,1)S(1)}, u32[]{:S(2)}, u32[]{:S(2)}) %all-to-all-start) | async-done | bytes 2359328 | tf_op jit(solution)/shard_map/all_to_all | solution.py:376
  43.9 10.2 %all-to-all-start.1 = ((f32[32,8,256]{2,1,0:T(8,128)}), f32[32,8,256]{2,1,0:T(8,128)S(1)}, u32[]{:S(2)}, u32[]{:S(2)}) async-start(f32[32,8,256]{2,1,0:T(8,128)} %bitcast.2), calls=%async_computation.1 | async-start | bytes 524288 | tf_op jit(solution)/shard_map/all_to_all | solution.py:376
  54.1 10.4 %all-to-all-done.1 = f32[32,8,256]{2,1,0:T(8,128)S(1)} async-done(((f32[32,8,256]{2,1,0:T(8,128)}), f32[32,8,256]{2,1,0:T(8,128)S(1)}, u32[]{:S(2)}, u32[]{:S(2)}) %all-to-all-start.1) | async-done | bytes 262176 | tf_op jit(solution)/shard_map/all_to_all | solution.py:376
  66.3 2.1 collective-permute-start.7
  70.1 3.7 %collective-permute-start.1 = (f32[8,128]{1,0:T(8,128)S(1)}, f32[8,128]{1,0:T(8,128)S(1)}, u32[]{:S(2)}, u32[]{:S(2)}) collective-permute-start(f32[8,128]{1,0:T(8,128)S(1)} %get-tuple-element.40), channel_id=1, source_target_pairs={{0,1},{1,0},{2,3},{3,2},{4,5},{5,4},{6,7},{7,6},{8,9},{9,8},{10,11... | collective-permute-start | bytes 12296 | tf_op jit(solution)/shard_map/ppermute | solution.py:401
  75.3 4.1 %all-to-all-start.2 = ((f32[32,8,256]{2,1,0:T(8,128)}), f32[32,8,256]{2,1,0:T(8,128)S(1)}, u32[]{:S(2)}, u32[]{:S(2)}) async-start(f32[32,8,256]{2,1,0:T(8,128)} %broadcast_in_dim.12), calls=%async_computation.2 | async-start | bytes 524288 | tf_op jit(solution)/shard_map/all_to_all | solution.py:376
  79.4 11.0 %shard_map.70 = (bf16[1024,1024]{1,0:T(8,128)(2,1)}, bf16[1024,1024]{1,0:T(8,128)(2,1)}, bf16[1024,1024]{1,0:T(8,128)(2,1)}, bf16[1024,1024]{1,0:T(8,128)(2,1)}) custom-call(s32[2]{0:T(128)S(1)} %pad_add_fusion.place, bf16[8,144,1024]{2,1,0:T(8,128)(2,1)} %copy-done, bf16[8,144,1024]{2,1,0:T(8,128)(2,1)} %collective-permute-done.4.got_other, ...), custom_call_target="tpu_custom_call" | custom-call | flops 40000000000 | bytes 20000000 | tf_op jit(solution)/shard_map/pallas_call | solution.py:368
  91.1 5.6 %shard_map.71 = (f32[32,1024]{1,0:T(8,128)}, f32[128,256]{1,0:T(8,128)}, f32[128,264]{1,0:T(8,128)}) custom-call(s32[2]{0:T(128)S(1)} %pad_add_fusion.place, f32[256,256]{1,0:T(8,128)S(1)} %bitcast.12, bf16[1024,1024]{1,0:T(8,128)(2,1)} %get-tuple-element.29.refs_0_, bf16[1024,1024]{1,0:T(8,128)(2,1)} %get-tuple-element.30.refs_1_, ...), custom_call_target="tpu_custom_call" | custom-call | tf_op jit(solution)/shard_map/pallas_call | solution.py:368
  96.7 6.0 %all-to-all-start.3 = ((f32[16,8,264]{2,1,0:T(8,128)}), f32[16,8,264]{2,1,0:T(8,128)S(1)}, u32[]{:S(2)}, u32[]{:S(2)}) async-start(f32[16,8,264]{2,1,0:T(8,128)} %bitcast.4), calls=%async_computation.3 | async-start | bytes 393216 | tf_op jit(solution)/shard_map/all_to_all | solution.py:376
  104.5 5.1 %all-to-all-done.3 = f32[16,8,264]{2,1,0:T(8,128)S(1)} async-done(((f32[16,8,264]{2,1,0:T(8,128)}), f32[16,8,264]{2,1,0:T(8,128)S(1)}, u32[]{:S(2)}, u32[]{:S(2)}) %all-to-all-start.3) | async-done | bytes 135200 | tf_op jit(solution)/shard_map/all_to_all | solution.py:376
  109.7 14.1 %all_to_all.85 = f32[8,8,264]{2,1,0:T(8,128)S(1)} all-to-all(f32[8,8,264]{2,1,0:T(8,128)S(1)} %broadcast_in_dim.13), channel_id=1, replica_groups=mesh['z'=8,'x'=4,'y'=4,'core'=2] {'z'}, dimensions={0} | all-to-all | bytes 135168 | tf_op jit(solution)/shard_map/all_to_all | solution.py:376
  123.9 10.2 %all_to_all.86 = f32[16,8,264]{2,1,0:T(8,128)S(1)} all-to-all(f32[16,8,264]{2,1,0:T(8,128)S(1)} %broadcast_in_dim.14), channel_id=1, replica_groups=mesh['z'=8,'x'=4,'y'=4,'core'=2] {'x','y'}, dimensions={0} | all-to-all | bytes 270336 | tf_op jit(solution)/shard_map/all_to_all | solution.py:376
  134.1 8.4 %shard_map.72 = f32[256,256]{1,0:T(8,128)S(1)} custom-call(f32[128,264]{1,0:T(8,128)S(1)} %bitcast.15, bf16[1024,1024]{1,0:T(8,128)(2,1)} %get-tuple-element.29.refs_0_, bf16[1024,1024]{1,0:T(8,128)(2,1)} %get-tuple-element.30.refs_1_, bf16[1024,1024]{1,0:T(8,128)(2,1)} %get-tuple-element.31.refs_2_, bf16[1024,1024]{1,0:T(8,128)(2,1)} %get-tuple-element.32.refs_3_), custom_call_target="tpu_custom_call" | custom-call | tf_op jit(solution)/shard_map/pallas_call | solution.py:368
  142.5 13.6 %all_to_all.87 = f32[32,8,256]{2,1,0:T(8,128)S(1)} all-to-all(f32[32,8,256]{2,1,0:T(8,128)S(1)} %bitcast.14), channel_id=1, replica_groups=mesh['z'=8,'x'=4,'y'=4,'core'=2] {'z','x'}, dimensions={0} | all-to-all | bytes 524288 | tf_op jit(solution)/shard_map/all_to_all | solution.py:376
  156.1 13.7 %all_to_all.88 = f32[32,8,256]{2,1,0:T(8,128)S(1)} all-to-all(f32[32,8,256]{2,1,0:T(8,128)S(1)} %broadcast_in_dim.15), channel_id=1, replica_groups=mesh['z'=8,'x'=4,'y'=4,'core'=2] {'z','x'}, dimensions={0} | all-to-all | bytes 524288 | tf_op jit(solution)/shard_map/all_to_all | solution.py:376
  169.8 4.9 %shard_map.73 = (f32[32,1024]{1,0:T(8,128)S(1)}, f32[128,256]{1,0:T(8,128)S(1)}, f32[128,264]{1,0:T(8,128)S(1)}) custom-call(s32[2]{0:T(128)S(1)} %pad_add_fusion.place, f32[256,256]{1,0:T(8,128)S(1)} %bitcast.13, bf16[1024,1024]{1,0:T(8,128)(2,1)} %get-tuple-element.29.refs_0_, bf16[1024,1024]{1,0:T(8,128)(2,1)} %get-tuple-element.30.refs_1_, ...), custom_call_target="tpu_custom_call" | custom-call | tf_op jit(solution)/shard_map/pallas_call | solution.py:368
  174.7 10.4 %all_to_all.89 = f32[16,8,264]{2,1,0:T(8,128)S(1)} all-to-all(f32[16,8,264]{2,1,0:T(8,128)S(1)} %bitcast.16), channel_id=1, replica_groups=mesh['z'=8,'x'=4,'y'=4,'core'=2] {'x','y'}, dimensions={0} | all-to-all | bytes 270336 | tf_op jit(solution)/shard_map/all_to_all | solution.py:376
  185.2 10.0 %all_to_all.90 = f32[8,8,264]{2,1,0:T(8,128)S(1)} all-to-all(f32[8,8,264]{2,1,0:T(8,128)S(1)} %broadcast_in_dim.16), channel_id=1, replica_groups=mesh['z'=8,'x'=4,'y'=4,'core'=2] {'z'}, dimensions={0} | all-to-all | bytes 135168 | tf_op jit(solution)/shard_map/all_to_all | solution.py:376
  195.1 10.2 %all_to_all.91 = f32[16,8,264]{2,1,0:T(8,128)S(1)} all-to-all(f32[16,8,264]{2,1,0:T(8,128)S(1)} %broadcast_in_dim.17), channel_id=1, replica_groups=mesh['z'=8,'x'=4,'y'=4,'core'=2] {'x','y'}, dimensions={0} | all-to-all | bytes 270336 | tf_op jit(solution)/shard_map/all_to_all | solution.py:376
  205.3 11.1 %collective-permute-start.8 = (f32[128,520]{1,0:T(8,128)S(1)}, f32[128,520]{1,0:T(8,128)S(1)}, u32[]{:S(2)}, u32[]{:S(2)}) collective-permute-start(f32[128,520]{1,0:T(8,128)S(1)} %pad_maximum_fusion.1), channel_id=1, source_target_pairs={{0,1},{1,0},{2,3},{3,2},{4,5},{5,4},{6,7},{7,6},{8,9},{9,8},{10,11... | collective-permute-start | bytes 798728 | tf_op jit(solution)/shard_map/ppermute | solution.py:401
  217.7 8.5 %shard_map.74 = (bf16[1,2,1024,1024]{3,2,1,0:T(8,128)(2,1)}, f32[2,32,1024]{2,1,0:T(8,128)}, f32[2,32,1024]{2,1,0:T(8,128)}) custom-call(s32[2]{0:T(128)S(1)} %pad_add_fusion.place, f32[128,264]{1,0:T(8,128)S(1)} %bitcast.11, f32[128,520]{1,0:T(8,128)S(1)} %collective-permute-done.8.other, f32[32,1024]{1,0:T(8,128)S(1)} %get-tuple-element.36.p_mine, ...), custom_call_target="tpu_custom_call" | custom-call | tf_op jit(solution)/shard_map/pallas_call | solution.py:368
  (51 shorter events, 15.0 us)
Async XLA Ops:
  4.3 6.9 %copy-start.3 = (bf16[128,2048]{1,0:T(8,128)(2,1)S(1)}, bf16[128,2048]{1,0:T(8,128)(2,1)}, u32[]{:S(2)}) copy-start(bf16[128,2048]{1,0:T(8,128)(2,1)} %grads_out.1) | copy-start | bytes 1572868
  4.3 7.9 %copy-start.1 = (f32[2,32,1024]{2,1,0:T(8,128)S(1)}, f32[2,32,1024]{2,1,0:T(8,128)}, u32[]{:S(2)}) copy-start(f32[2,32,1024]{2,1,0:T(8,128)} %warm_q.2) | copy-start | bytes 786436
  4.3 36.1 %all-to-all-start = ((bf16[8,144,1024]{2,1,0:T(8,128)(2,1)}), bf16[8,144,1024]{2,1,0:T(8,128)(2,1)S(1)}, u32[]{:S(2)}, u32[]{:S(2)}) async-start(bf16[8,144,1024]{2,1,0:T(8,128)(2,1)} %shard_map.67), calls=%async_computation | async-start | bytes 4718592 | tf_op jit(solution)/shard_map/all_to_all | solution.py:376
  12.0 5.2 %collective-permute-start = (bf16[128,1024]{1,0:T(8,128)(2,1)}, bf16[128,1024]{1,0:T(8,128)(2,1)S(1)}, u32[]{:S(2)}, u32[]{:S(2)}) collective-permute-start(bf16[128,1024]{1,0:T(8,128)(2,1)} %get-tuple-element.38), channel_id=1, source_target_pairs={{0,1},{1,0},{2,3},{3,2},{4,5},{5,4},{6,7},{7,6},{8,9},{9,8},{10,11... | collective-permute-start | bytes 786440 | tf_op jit(solution)/shard_map/ppermute | solution.py:401
  17.1 0.7 copy-start.4
  40.4 25.9 %copy-start = (bf16[8,144,1024]{2,1,0:T(8,128)(2,1)}, bf16[8,144,1024]{2,1,0:T(8,128)(2,1)S(1)}, u32[]{:S(2)}) copy-start(bf16[8,144,1024]{2,1,0:T(8,128)(2,1)S(1)} %all-to-all-done.got) | copy-start | bytes 7077892
  40.4 39.0 %collective-permute-start.4 = (bf16[8,144,1024]{2,1,0:T(8,128)(2,1)S(1)}, bf16[8,144,1024]{2,1,0:T(8,128)(2,1)}, u32[]{:S(2)}, u32[]{:S(2)}) collective-permute-start(bf16[8,144,1024]{2,1,0:T(8,128)(2,1)S(1)} %all-to-all-done.got), channel_id=1, source_target_pairs={{0,1},{1,0},{2,3},{3,2},{4,5},{5,4},{6,7},{7,6},{8,9},{9,8},{10,11... | collective-permute-start | bytes 7077896 | tf_op jit(solution)/shard_map/ppermute | solution.py:401
  41.2 38.1 %collective-permute-start.5 = (bf16[1024,1024]{1,0:T(8,128)(2,1)}, bf16[1024,1024]{1,0:T(8,128)(2,1)}, u32[]{:S(2)}, u32[]{:S(2)}) collective-permute-start(bf16[1024,1024]{1,0:T(8,128)(2,1)} %get-tuple-element.28), channel_id=1, source_target_pairs={{0,1},{1,0},{2,3},{3,2},{4,5},{5,4},{6,7},{7,6},{8,9},{9,8},{10,11... | collective-permute-start | bytes 6291464 | tf_op jit(solution)/shard_map/ppermute | solution.py:401
  41.3 23.3 %collective-permute-start.3 = (bf16[256,1024]{1,0:T(8,128)(2,1)S(1)}, bf16[256,1024]{1,0:T(8,128)(2,1)}, u32[]{:S(2)}, u32[]{:S(2)}) collective-permute-start(bf16[256,1024]{1,0:T(8,128)(2,1)S(1)} %pad_maximum_fusion.refs_0_), channel_id=1, source_target_pairs={{0,6},{2,0},{4,2},{6,4},{1,7},{3,1},{5,3},{7,5},{8,14},{10,8},{12,... | collective-permute-start | bytes 1572872 | tf_op jit(solution)/shard_map/ppermute | solution.py:454
  42.1 26.2 %collective-permute-start.2 = (bf16[256,1024]{1,0:T(8,128)(2,1)S(1)}, bf16[256,1024]{1,0:T(8,128)(2,1)}, u32[]{:S(2)}, u32[]{:S(2)}) collective-permute-start(bf16[256,1024]{1,0:T(8,128)(2,1)S(1)} %pad_maximum_fusion.refs_0_), channel_id=1, source_target_pairs={{0,2},{2,4},{4,6},{6,0},{1,3},{3,5},{5,7},{7,1},{8,10},{10,12},{12... | collective-permute-start | bytes 1572872 | tf_op jit(solution)/shard_map/ppermute | solution.py:454
  43.9 20.7 %all-to-all-start.1 = ((f32[32,8,256]{2,1,0:T(8,128)}), f32[32,8,256]{2,1,0:T(8,128)S(1)}, u32[]{:S(2)}, u32[]{:S(2)}) async-start(f32[32,8,256]{2,1,0:T(8,128)} %bitcast.2), calls=%async_computation.1 | async-start | bytes 524288 | tf_op jit(solution)/shard_map/all_to_all | solution.py:376
  66.3 13.1 %collective-permute-start.7 = (bf16[128,1024]{1,0:T(8,128)(2,1)}, bf16[128,1024]{1,0:T(8,128)(2,1)S(1)}, u32[]{:S(2)}, u32[]{:S(2)}) collective-permute-start(bf16[128,1024]{1,0:T(8,128)(2,1)} %slice.19), channel_id=1, source_target_pairs={{0,6},{2,0},{4,2},{6,4},{1,7},{3,1},{5,3},{7,5},{8,14},{10,8},{12,... | collective-permute-start | bytes 786440 | tf_op jit(solution)/shard_map/ppermute | solution.py:474
  70.0 9.3 %collective-permute-start.6 = (bf16[128,1024]{1,0:T(8,128)(2,1)}, bf16[128,1024]{1,0:T(8,128)(2,1)}, u32[]{:S(2)}, u32[]{:S(2)}) collective-permute-start(bf16[128,1024]{1,0:T(8,128)(2,1)} %slice.18), channel_id=1, source_target_pairs={{0,2},{2,4},{4,6},{6,0},{1,3},{3,5},{5,7},{7,1},{8,10},{10,12},{12... | collective-permute-start | bytes 786440 | tf_op jit(solution)/shard_map/ppermute | solution.py:473
  70.1 4.5 %collective-permute-start.1 = (f32[8,128]{1,0:T(8,128)S(1)}, f32[8,128]{1,0:T(8,128)S(1)}, u32[]{:S(2)}, u32[]{:S(2)}) collective-permute-start(f32[8,128]{1,0:T(8,128)S(1)} %get-tuple-element.40), channel_id=1, source_target_pairs={{0,1},{1,0},{2,3},{3,2},{4,5},{5,4},{6,7},{7,6},{8,9},{9,8},{10,11... | collective-permute-start | bytes 12296 | tf_op jit(solution)/shard_map/ppermute | solution.py:401
  75.3 15.8 %all-to-all-start.2 = ((f32[32,8,256]{2,1,0:T(8,128)}), f32[32,8,256]{2,1,0:T(8,128)S(1)}, u32[]{:S(2)}, u32[]{:S(2)}) async-start(f32[32,8,256]{2,1,0:T(8,128)} %broadcast_in_dim.12), calls=%async_computation.2 | async-start | bytes 524288 | tf_op jit(solution)/shard_map/all_to_all | solution.py:376
  91.1 13.4 %copy-start.2 = (bf16[1024,1024]{1,0:T(8,128)(2,1)S(1)}, bf16[1024,1024]{1,0:T(8,128)(2,1)}, u32[]{:S(2)}) copy-start(bf16[1024,1024]{1,0:T(8,128)(2,1)} %get-tuple-element.32.refs_3_) | copy-start | bytes 6291460
  96.7 12.9 %all-to-all-start.3 = ((f32[16,8,264]{2,1,0:T(8,128)}), f32[16,8,264]{2,1,0:T(8,128)S(1)}, u32[]{:S(2)}, u32[]{:S(2)}) async-start(f32[16,8,264]{2,1,0:T(8,128)} %bitcast.4), calls=%async_computation.3 | async-start | bytes 393216 | tf_op jit(solution)/shard_map/all_to_all | solution.py:376
  102.7 114.9 %collective-permute-start.9 = (bf16[1024,1024]{1,0:T(8,128)(2,1)}, bf16[1024,1024]{1,0:T(8,128)(2,1)}, u32[]{:S(2)}, u32[]{:S(2)}) collective-permute-start(bf16[1024,1024]{1,0:T(8,128)(2,1)} %get-tuple-element.31.refs_2_), channel_id=1, source_target_pairs={{0,1},{1,0},{2,3},{3,2},{4,5},{5,4},{6,7},{7,6},{8,9},{9,8},{10,11... | collective-permute-start | bytes 6291464 | tf_op jit(solution)/shard_map/ppermute | solution.py:401
  104.4 113.2 %collective-permute-start.10 = (bf16[1024,1024]{1,0:T(8,128)(2,1)S(1)}, bf16[1024,1024]{1,0:T(8,128)(2,1)}, u32[]{:S(2)}, u32[]{:S(2)}) collective-permute-start(bf16[1024,1024]{1,0:T(8,128)(2,1)S(1)} %copy-done.2), channel_id=1, source_target_pairs={{0,1},{1,0},{2,3},{3,2},{4,5},{5,4},{6,7},{7,6},{8,9},{9,8},{10,11... | collective-permute-start | bytes 6291464 | tf_op jit(solution)/shard_map/ppermute | solution.py:401
  205.3 12.3 %collective-permute-start.8 = (f32[128,520]{1,0:T(8,128)S(1)}, f32[128,520]{1,0:T(8,128)S(1)}, u32[]{:S(2)}, u32[]{:S(2)}) collective-permute-start(f32[128,520]{1,0:T(8,128)S(1)} %pad_maximum_fusion.1), channel_id=1, source_target_pairs={{0,1},{1,0},{2,3},{3,2},{4,5},{5,4},{6,7},{7,6},{8,9},{9,8},{10,11... | collective-permute-start | bytes 798728 | tf_op jit(solution)/shard_map/ppermute | solution.py:401
